TPU v7x, 32 devices: a whole 2x2x4 slice. The times are simulated.
32 devices in a mesh: dp: 16 (over z, y, core), head: 2 (over x).
Axes of the slice: x: 2, y: 2, z: 4, core: 2. Of those that a mesh axis runs over, the one named last changes fastest.
Arguments:
- tokens: bfloat16 [32768, 768], P('dp'), may hold values from -6 to 6
- segments: int32 [64, 512], P('dp'), may hold values from 0 to 7, never falling along the last dimension, each value on 1 to 128 neighbouring positions
- qkv_weight: bfloat16 [2, 3, 192, 768], P(None, None, None, 'head'), may hold values from -0.4375 to 0.4375
- out_weight: bfloat16 [2, 768, 768], P(None, 'head'), may hold values from -0.625 to 0.625
- inner_weight: bfloat16 [2, 192, 3072], P(None, None, 'head'), may hold values from -0.4375 to 0.4375
- outer_weight: bfloat16 [2, 768, 768], P(None, None, 'head'), may hold values from -0.21875 to 0.21875
- norm_gains: float32 [2, 2, 768], replicated, may hold values from 0.5 to 1.5
- cotangent: bfloat16 [32768, 768], P('dp'), may hold values from -6 to 6
Outputs:
- activations: bfloat16 [32768, 768], P('dp')
- input_grad: bfloat16 [32768, 768], P('dp')
- qkv_grad: float32 [2, 3, 192, 768], P(None, None, None, 'head')
- out_grad: float32 [2, 768, 768], P(None, 'head')
- inner_grad: float32 [2, 192, 3072], P(None, None, 'head')
- outer_grad: float32 [2, 768, 768], P(None, None, 'head')
- gain_grad: float32 [2, 2, 768], replicated
Inputs may be any that keep to these rules, and one draw needn't show every extreme that they name: `segments`: along each packed row the ids never fall; a document holds at most 128 positions and some document holds exactly that many.
All inputs are finite; a program needn't handle non-finite values.
Results may differ from a plain program's by a relative error of at most 0.035.
Values may be sent and summed in bfloat16 or wider, within the bound.
No kernel may reach another device: no remote copies, remote signals or barrier semaphores. Data moves between devices by JAX's collectives and lax.ppermute only.
A program may use at most 256 MiB of HBM per device.

v0:
```python
import jax
import jax.numpy as jnp
from jax import lax
from jax.sharding import PartitionSpec as P

HEAD_DIM = 64


epsilon = 1e-12
masked_score = -1e30


def normalize(before, gains):
    average = jnp.mean(before, axis=-1, keepdims=True)
    centered = before - average
    spread = jnp.mean(centered * centered, axis=-1, keepdims=True)
    return centered * lax.rsqrt(spread + epsilon) * gains


def gelu_exact(values):
    return jax.nn.gelu(values, approximate=False)


def grouped(inputs, weight):
    in_width = weight.shape[0]
    groups = inputs.shape[1] // in_width
    in_parts = inputs.reshape(inputs.shape[0], groups, in_width)
    kernel = weight.reshape(in_width, groups, weight.shape[1] // groups)
    result = jnp.einsum("tgi,igo->tgo", in_parts, kernel, preferred_element_type=jnp.float32)
    return result.reshape(inputs.shape[0], -1)


def grouped_back(gradient, weight, inputs):
    token_count = inputs.shape[0]
    in_width = weight.shape[0]
    groups = inputs.shape[1] // in_width
    in_parts = inputs.reshape(token_count, groups, in_width)
    kernel = weight.reshape(in_width, groups, weight.shape[1] // groups)
    grad_parts = gradient.reshape(token_count, groups, -1)
    grad_inputs = jnp.einsum("tgo,igo->tgi", grad_parts, kernel, preferred_element_type=jnp.float32)
    grad_weight = jnp.einsum(
        "tgi,tgo->igo", in_parts, grad_parts, preferred_element_type=jnp.float32
    )
    return (grad_inputs.reshape(token_count, -1), grad_weight.reshape(in_width, -1))


def row_scores(queries, key_rows, segment_ids):
    length = queries.shape[0]
    head_total = queries.shape[1] // HEAD_DIM
    split_shape = (length, head_total, HEAD_DIM)
    scores = jnp.einsum(
        "qhe,khe->hqk",
        queries.reshape(split_shape),
        key_rows.reshape(split_shape),
        preferred_element_type=jnp.float32,
    ) * HEAD_DIM ** (-0.5)
    same_doc = segment_ids[:, None] == segment_ids[None, :]
    return (jnp.where(same_doc[None], scores, masked_score), split_shape)


def attend_row(bundle):
    queries, key_rows, value_rows, segment_ids = bundle
    scores, split_shape = row_scores(queries, key_rows, segment_ids)
    maximum = jnp.max(scores, axis=-1, keepdims=True)
    weights = jnp.exp(scores - maximum)
    summed = jnp.sum(weights, axis=-1, keepdims=True)
    probabilities = (weights / summed).astype(jnp.bfloat16)
    context = jnp.einsum(
        "hqk,khe->qhe",
        probabilities,
        value_rows.reshape(split_shape),
        preferred_element_type=jnp.float32,
    )
    return (context.reshape(queries.shape[0], -1), maximum + jnp.log(summed))


def attend_back(bundle):
    queries, key_rows, value_rows, grad_context, segment_ids, log_total = bundle
    scores, split_shape = row_scores(queries, key_rows, segment_ids)
    probabilities = jnp.exp(scores - log_total)
    grad_split = grad_context.reshape(split_shape)
    grad_value = jnp.einsum(
        "hqk,qhe->khe",
        probabilities.astype(jnp.bfloat16),
        grad_split,
        preferred_element_type=jnp.float32,
    )
    grad_probs = jnp.einsum(
        "qhe,khe->hqk",
        grad_split,
        value_rows.reshape(split_shape),
        preferred_element_type=jnp.float32,
    )
    intersection = jnp.sum(probabilities * grad_probs, axis=-1, keepdims=True)
    grad_scores = (probabilities * (grad_probs - intersection)).astype(jnp.bfloat16)
    grad_query = jnp.einsum(
        "hqk,khe->qhe",
        grad_scores,
        key_rows.reshape(split_shape),
        preferred_element_type=jnp.float32,
    ) * HEAD_DIM ** (-0.5)
    grad_key = jnp.einsum(
        "hqk,qhe->khe",
        grad_scores,
        queries.reshape(split_shape),
        preferred_element_type=jnp.float32,
    ) * HEAD_DIM ** (-0.5)
    length = queries.shape[0]
    return (
        grad_query.reshape(length, -1).astype(jnp.bfloat16),
        grad_key.reshape(length, -1).astype(jnp.bfloat16),
        grad_value.reshape(length, -1).astype(jnp.bfloat16),
    )


def project(context, out_rows):
    partial_sum = jnp.dot(context, out_rows, preferred_element_type=jnp.float32)
    return lax.psum(partial_sum.astype(jnp.bfloat16), "head").astype(jnp.float32)


def layer_forward(current, weights, segment_rows, offset):
    qkv_w, out_rows, inner_w, outer_w, gains = weights
    token_count = current.shape[0]
    channels = qkv_w.shape[-1]
    rows_in = qkv_w.shape[1]
    groups = channels // rows_in
    state_in = lax.dynamic_slice_in_dim(current.astype(jnp.bfloat16), offset, channels, 1)
    kernel = qkv_w.reshape(3, rows_in, groups, channels // groups)
    qkv = jnp.einsum(
        "tgi,sigo->stgo",
        state_in.reshape(token_count, groups, rows_in),
        kernel,
        preferred_element_type=jnp.float32,
    )
    qkv = qkv.reshape(3, token_count, channels).astype(jnp.bfloat16)
    row_count, seq_len = segment_rows.shape
    stacked = qkv.reshape(3, row_count, seq_len, channels)
    context, log_total = lax.map(attend_row, (stacked[0], stacked[1], stacked[2], segment_rows))
    context = context.reshape(token_count, channels).astype(jnp.bfloat16)
    attention = project(context, out_rows)
    before_first = current + attention
    first = normalize(before_first, gains[0])
    first_in = lax.dynamic_slice_in_dim(first.astype(jnp.bfloat16), offset, channels, 1)
    pre_act = grouped(first_in, inner_w)
    activated = gelu_exact(pre_act).astype(jnp.bfloat16)
    branch = grouped(activated, outer_w).astype(jnp.bfloat16)
    branch = lax.all_gather(branch, "head", axis=1, tiled=True)
    before_second = first + branch.astype(jnp.float32)
    output = normalize(before_second, gains[1])
    saved_parts = (
        state_in,
        qkv,
        log_total,
        context,
        before_first,
        first_in,
        pre_act,
        activated,
        before_second,
    )
    return (output, saved_parts)


def layer_backward(gradient, saved_parts, weights, segment_rows, offset):
    qkv_w, out_rows, inner_w, outer_w, gains = weights
    state_in, qkv, log_total, context, before_first, first_in, pre_act, activated, before_second = (
        saved_parts
    )
    token_count = state_in.shape[0]
    channels = qkv.shape[-1]
    unused_second, second_back = jax.vjp(normalize, before_second, gains[1])
    grad_second, gain_second = second_back(gradient)
    grad_branch = lax.dynamic_slice_in_dim(grad_second, offset, channels, 1).astype(jnp.bfloat16)
    grad_act, outer_part = grouped_back(grad_branch, outer_w, activated)
    unused_act, gelu_back = jax.vjp(gelu_exact, pre_act)
    (grad_pre,) = gelu_back(grad_act.astype(jnp.bfloat16).astype(jnp.float32))
    grad_pre = grad_pre.astype(jnp.bfloat16)
    grad_first_in, inner_part = grouped_back(grad_pre, inner_w, first_in)
    grad_first_in = lax.all_gather(
        grad_first_in.astype(jnp.bfloat16), "head", axis=1, tiled=True
    ).astype(grad_first_in.dtype)
    grad_first = grad_second + grad_first_in
    unused_first, first_back = jax.vjp(normalize, before_first, gains[0])
    grad_before, gain_first = first_back(grad_first)
    grad_attention = grad_before.astype(jnp.bfloat16)
    grad_context = lax.dot_general(
        grad_attention, out_rows, (((1,), (1,)), ((), ())), preferred_element_type=jnp.float32
    ).astype(jnp.bfloat16)
    out_part = lax.dot_general(
        context, grad_attention, (((0,), (0,)), ((), ())), preferred_element_type=jnp.float32
    )
    row_count, seq_len = segment_rows.shape
    stacked = qkv.reshape(3, row_count, seq_len, channels)
    grad_rows = lax.map(
        attend_back,
        (
            stacked[0],
            stacked[1],
            stacked[2],
            grad_context.reshape(row_count, seq_len, channels),
            segment_rows,
            log_total,
        ),
    )
    grad_qkv = jnp.stack(grad_rows).reshape(3, token_count, channels)
    rows_in = qkv_w.shape[1]
    groups = channels // rows_in
    kernel = qkv_w.reshape(3, rows_in, groups, channels // groups)
    grad_parts = grad_qkv.reshape(3, token_count, groups, channels // groups)
    in_parts = state_in.reshape(token_count, groups, rows_in)
    grad_state_in = jnp.einsum(
        "stgo,sigo->tgi", grad_parts, kernel, preferred_element_type=jnp.float32
    ).reshape(token_count, channels)
    qkv_part = jnp.einsum(
        "tgi,stgo->sigo", in_parts, grad_parts, preferred_element_type=jnp.float32
    ).reshape(3, rows_in, channels)
    grad_state_in = lax.all_gather(
        grad_state_in.astype(jnp.bfloat16), "head", axis=1, tiled=True
    ).astype(grad_state_in.dtype)
    grad_current = grad_before + grad_state_in
    grads = (qkv_part, out_part, inner_part, outer_part, jnp.stack([gain_first, gain_second]))
    return (grad_current, grads)


def reduce_grads(grads):
    return lax.psum(grads, "dp")


def shards(
    tokens, segments, qkv_weight, out_weight, inner_weight, outer_weight, norm_gains, cotangent
):
    head_place = lax.axis_index("head")
    current = tokens.astype(jnp.float32)
    gradient = cotangent.astype(jnp.float32)
    offset = head_place * qkv_weight.shape[-1]
    layer_total = qkv_weight.shape[0]
    saved_layers = []
    for layer_index in range(layer_total):
        weights = (
            qkv_weight[layer_index],
            out_weight[layer_index],
            inner_weight[layer_index],
            outer_weight[layer_index],
            norm_gains[layer_index],
        )
        current, saved_parts = layer_forward(current, weights, segments, offset)
        saved_layers.append(saved_parts)
    activations = current.astype(jnp.bfloat16)
    layer_grads = []
    for layer_index in reversed(range(layer_total)):
        weights = (
            qkv_weight[layer_index],
            out_weight[layer_index],
            inner_weight[layer_index],
            outer_weight[layer_index],
            norm_gains[layer_index],
        )
        gradient, grads = layer_backward(
            gradient, saved_layers[layer_index], weights, segments, offset
        )
        lifted = tuple((member[None] for member in grads))
        layer_grads.insert(0, lifted)
    joined = tuple(
        (
            jnp.concatenate([layer_entry[position] for layer_entry in layer_grads], 0)
            for position in range(5)
        )
    )
    joined = reduce_grads(joined)
    input_grad = gradient.astype(jnp.bfloat16)
    return (activations, input_grad, joined[0], joined[1], joined[2], joined[3], joined[4])


def solution(mesh):
    return jax.shard_map(
        shards,
        mesh=mesh,
        in_specs=(
            P("dp", None),
            P("dp", None),
            P(None, None, None, "head"),
            P(None, "head", None),
            P(None, None, "head"),
            P(None, None, "head"),
            P(),
            P("dp", None),
        ),
        out_specs=(
            P("dp", None),
            P("dp", None),
            P(None, None, None, "head"),
            P(None, "head", None),
            P(None, None, "head"),
            P(None, None, "head"),
            P(),
        ),
        check_vma=False,
    )
```

profile of v0, /device:TPU:0, one launch (start us, length us, event | category | flops | bytes accessed | tf_op | source)
XLA Modules:
  0.0 1245.6 jit_solution(6845169037934230303)
XLA Ops:
  33.9 39.6 %while.52 = (s32[]{:T(128)}, bf16[4,512,384]{2,1,0:T(8,128)(2,1)}, f32[4,6,512,1]{2,1,3,0:T(8,128)}, bf16[4,512,384]{1,2,0:T(8,128)(2,1)S(1)}, s32[4,512]{1,0:T(...) while((s32[]{:T(128)}, bf16[4,512,384]{2,1,0:T(8,128)(2,1)}, ...), condition=%wide.region_3.4_spmd, body=%wide.region_0.3_spmd.sunk | while | flops 421786624 | bytes 25537632 | solution.py:138
  90.7 78.1 %all-reduce.5.cloned.1.call-done = bf16[2048,768]{1,0:T(8,128)(2,1)} async-done(((bf16[2048,768]{1,0:T(8,128)(2,1)}), bf16[2048,768]{1,0:T(8,128)(2,1)}) %all-reduce.5.cloned.1.call-update) | async-done | bytes 3145744 | tf_op jit(solution)/shard_map/psum | solution.py:118
  178.4 31.9 %fusion.51 = (bf16[2048,2,768]{2,0,1:T(8,128)(2,1)S(1)}, f32[2048,2,768]{2,0,1:T(8,128)}, f32[2,2048,768]{2,1,0:T(8,128)}) fusion(bf16[2048,2,192]{0,2,1:T(8,128)(2,1)S(1)} %bitcast.534, bf16[192,2,768]{2,1,0:T(2,128)(2,1)} %reshape_squeeze.25), kind=kOutput, calls=%fused_computation.111 | convolution fusion | flops 1412431872 | bytes 33619968 | tf_op jit(solution)/shard_map/tgi,igo->tgo/dot_general | solution.py:29
  217.1 11.6 copy.79
  228.7 33.1 %all-gather.7.cloned.1.call-done = bf16[2048,768]{1,0:T(8,128)(2,1)} async-done(((bf16[2048,384]{1,0:T(8,128)(2,1)}), bf16[2048,768]{1,0:T(8,128)(2,1)}) %all-gather.7.cloned.1.call-update) | async-done | bytes 3145744 | tf_op jit(solution)/shard_map/all_gather | solution.py:147
  291.8 39.4 %while.53 = (s32[]{:T(128)}, bf16[4,512,384]{2,1,0:T(8,128)(2,1)}, f32[4,6,512,1]{2,1,3,0:T(8,128)}, bf16[4,512,384]{1,2,0:T(8,128)(2,1)S(1)}, s32[4,512]{1,0:T(...) while((s32[]{:T(128)}, bf16[4,512,384]{2,1,0:T(8,128)(2,1)}, ...), condition=%wide.region_12.13_spmd, body=%wide.region_9.12_spmd.sunk | while | flops 421786624 | bytes 25537632 | solution.py:138
  331.2 6.1 convolution_convert_fusion
  342.6 80.7 %all-reduce.7.cloned.1.call-done = bf16[2048,768]{1,0:T(8,128)(2,1)} async-done(((bf16[2048,768]{1,0:T(8,128)(2,1)}), bf16[2048,768]{1,0:T(8,128)(2,1)}) %all-reduce.7.cloned.1.call-update) | async-done | bytes 3145744 | tf_op jit(solution)/shard_map/psum | solution.py:118
  431.6 32.0 %fusion.49 = (bf16[2048,2,768]{2,0,1:T(8,128)(2,1)S(1)}, f32[2048,2,768]{2,0,1:T(8,128)}, f32[2,2048,768]{2,1,0:T(8,128)}) fusion(bf16[2048,2,192]{0,2,1:T(8,128)(2,1)S(1)} %bitcast.536, bf16[192,2,768]{2,1,0:T(2,128)(2,1)} %reshape_squeeze.28), kind=kOutput, calls=%fused_computation.104 | convolution fusion | flops 1412431872 | bytes 33619968 | tf_op jit(solution)/shard_map/tgi,igo->tgo/dot_general | solution.py:29
  470.0 45.0 %all-gather.9.cloned.1.call-done = bf16[2048,768]{1,0:T(8,128)(2,1)} async-done(((bf16[2048,384]{1,0:T(8,128)(2,1)}), bf16[2048,768]{1,0:T(8,128)(2,1)}) %all-gather.9.cloned.1.call-update) | async-done | bytes 3145744 | tf_op jit(solution)/shard_map/all_gather | solution.py:147
  533.4 11.8 fusion.46
  551.7 45.0 %all-gather.11.cloned.1.call-done = bf16[2048,768]{1,0:T(8,128)(2,1)} async-done(((bf16[2048,384]{1,0:T(8,128)(2,1)}), bf16[2048,768]{1,0:T(8,128)(2,1)}) %all-gather.11.cloned.1.call-update) | async-done | bytes 3145744 | tf_op jit(solution)/shard_map/all_gather | solution.py:179
  596.8 8.2 multiply_reduce_fusion.2
  605.0 6.1 fusion.103
  618.2 89.3 %while.54 = (s32[]{:T(128)}, bf16[4,512,384]{1,2,0:T(8,128)(2,1)}, bf16[4,512,384]{1,2,0:T(8,128)(2,1)}, bf16[4,512,384]{1,2,0:T(8,128)(2,1)}, bf16[4,512,384]{1...) while((s32[]{:T(128)}, bf16[4,512,384]{1,2,0:T(8,128)(2,1)}, ...), condition=%wide.region_24.25_spmd, body=%wide.region_22.24_spmd.sunk | while | flops 1031468032 | bytes 77425840 | solution.py:194
  650.6 5.2 multiply_reduce_fusion.14
  672.8 5.2 multiply_reduce_fusion.14
  695.0 5.2 multiply_reduce_fusion.14
  736.5 45.0 %all-gather.13.cloned.1.call-done = bf16[2048,768]{1,0:T(8,128)(2,1)} async-done(((bf16[2048,384]{1,0:T(8,128)(2,1)}), bf16[2048,768]{1,0:T(8,128)(2,1)}) %all-gather.13.cloned.1.call-update) | async-done | bytes 3145744 | tf_op jit(solution)/shard_map/all_gather | solution.py:217
  781.6 7.7 multiply_reduce_fusion.3
  789.3 6.2 fusion.102
  799.1 11.8 fusion.39
  837.8 5.8 convolution_bitcast_fusion
  843.6 20.9 %all-gather.15.cloned.1.call-done = bf16[2048,768]{1,0:T(8,128)(2,1)} async-done(((bf16[2048,384]{1,0:T(8,128)(2,1)}), bf16[2048,768]{1,0:T(8,128)(2,1)}) %all-gather.15.cloned.1.call-update) | async-done | bytes 3145744 | tf_op jit(solution)/shard_map/all_gather | solution.py:179
  864.5 6.4 multiply_reduce_fusion.4
  871.0 6.0 fusion.101
  884.0 89.3 %while.55 = (s32[]{:T(128)}, bf16[4,512,384]{1,2,0:T(8,128)(2,1)}, bf16[4,512,384]{1,2,0:T(8,128)(2,1)}, bf16[4,512,384]{1,2,0:T(8,128)(2,1)}, bf16[4,512,384]{1...) while((s32[]{:T(128)}, bf16[4,512,384]{1,2,0:T(8,128)(2,1)}, ...), condition=%wide.region_31.32_spmd, body=%wide.region_29.31_spmd.sunk | while | flops 1031468032 | bytes 77425840 | solution.py:194
  1002.3 5.4 convolution_bitcast_fusion.4
  1011.8 5.7 fusion.116
  1048.5 64.6 %psum.55 = f32[2,2,768]{2,1,0:T(2,128)} all-reduce(f32[2,2,768]{2,1,0:T(2,128)S(1)} %pad_maximum_fusion.4), channel_id=1, replica_groups=mesh['dp'=16,'head'=2] {'dp'}, use_global_device_ids=true, to_apply=%region_40.41 | all-reduce | flops 3072 | bytes 24576 | tf_op jit(solution)/shard_map/psum | solution.py:226
  1113.1 6.3 add_convert_fusion
  1119.3 110.4 %all-reduce.9.cloned.1.call-done = (f32[2,3,192,384]{3,2,1,0:T(8,128)}, f32[2,384,768]{2,1,0:T(8,128)}, f32[2,192,1536]{2,1,0:T(8,128)}, f32[2,768,384]{2,1,0:T(8,128)}) async-done(((f32[2,3,192,384]{3,2,1,0:T(8,128)}, f32[2,384,768]{2,1,0:T(8,128)}, f32[2,192,1536]{2,1,0:T(8,128)}, f32[2,768,384]{2,1,0:T(8,128)}), (f32[2,3,192,384]{3,2,1,0:T(8,128)}, f32[2,384,768]{2,1,0:T(8,128)}, ...) | async-done | bytes 8847376 | tf_op jit(solution)/shard_map/psum | solution.py:226
  (567 shorter events, 521.0 us)
Async XLA Ops:
  7.2 161.6 %all-reduce.5.cloned.1.call-start = ((), (), s32[]{:S(2)}) async-start(), calls=%async_computation | async-start | bytes 6291456 | tf_op jit(solution)/shard_map/psum | solution.py:118
  80.1 88.6 %copy-start.4 = (bf16[2048,768]{1,0:T(8,128)(2,1)S(1)}, bf16[2048,768]{1,0:T(8,128)(2,1)}, u32[]{:S(2)}) copy-start(bf16[2048,768]{1,0:T(8,128)(2,1)} %param.16) | copy-start | bytes 9437188
  80.2 181.7 %all-gather.7.cloned.1.call-start = ((), (), s32[]{:S(2)}) async-start(), calls=%async_computation.1 | async-start | bytes 4718592 | tf_op jit(solution)/shard_map/all_gather | solution.py:147
  90.7 82.7 %copy-start.70 = (f32[768]{0:T(1024)}, f32[768]{0:T(1024)S(1)}, u32[]{:S(2)}) copy-start(f32[768]{0:T(1024)S(1)} %get-tuple-element.281) | copy-start | bytes 9220
  178.4 31.9 %copy-start.16 = (bf16[2048,384]{0,1:T(8,128)(2,1)}, bf16[2048,384]{0,1:T(8,128)(2,1)S(1)}, u32[]{:S(2)}) copy-start(bf16[2048,384]{0,1:T(8,128)(2,1)S(1)} %copy.74) | copy-start | bytes 4718596
  178.4 34.6 %copy-start.45 = (bf16[1,768,384]{1,2,0:T(8,128)(2,1)S(1)}, bf16[1,768,384]{1,2,0:T(8,128)(2,1)}, u32[]{:S(2)}) copy-start(bf16[1,768,384]{1,2,0:T(8,128)(2,1)} %copy.76) | copy-start | bytes 1769476
  216.7 206.5 %all-reduce.7.cloned.1.call-start = ((), (), s32[]{:S(2)}) async-start(), calls=%async_computation.2 | async-start | bytes 6291456 | tf_op jit(solution)/shard_map/psum | solution.py:118
  266.2 157.0 %copy-start.51 = (f32[2048]{0:T(1024)}, f32[2048]{0:T(1024)S(1)}, u32[]{:S(2)}) copy-start(f32[2048]{0:T(1024)S(1)} %broadcast_multiply_fusion.2) | copy-start | bytes 24580
  267.1 156.1 %copy-start.55 = (f32[2048]{0:T(1024)}, f32[2048]{0:T(1024)S(1)}, u32[]{:S(2)}) copy-start(f32[2048]{0:T(1024)S(1)} %fusion.97) | copy-start | bytes 24580
  331.2 92.1 %copy-start.60 = (f32[768]{0:T(1024)S(1)}, f32[768]{0:T(1024)}, u32[]{:S(2)}) copy-start(f32[768]{0:T(1024)} %get-tuple-element.280) | copy-start | bytes 9220
  337.3 177.7 %all-gather.9.cloned.1.call-start = ((), (), s32[]{:S(2)}) async-start(), calls=%async_computation.3 | async-start | bytes 4718592 | tf_op jit(solution)/shard_map/all_gather | solution.py:147
  431.6 32.0 %copy-start.18 = (bf16[2048,384]{0,1:T(8,128)(2,1)}, bf16[2048,384]{0,1:T(8,128)(2,1)S(1)}, u32[]{:S(2)}) copy-start(bf16[2048,384]{0,1:T(8,128)(2,1)S(1)} %copy.84) | copy-start | bytes 4718596
  431.6 34.6 %copy-start.47 = (bf16[1,768,384]{1,2,0:T(8,128)(2,1)S(1)}, bf16[1,768,384]{1,2,0:T(8,128)(2,1)}, u32[]{:S(2)}) copy-start(bf16[1,768,384]{1,2,0:T(8,128)(2,1)} %copy.86) | copy-start | bytes 1769476
  470.0 50.0 %copy-start.15 = (bf16[2048,768]{1,0:T(8,128)(2,1)S(1)}, bf16[2048,768]{1,0:T(8,128)(2,1)}, u32[]{:S(2)}) copy-start(bf16[2048,768]{1,0:T(8,128)(2,1)} %param.23) | copy-start | bytes 9437188
  470.0 50.0 %copy-start.69 = (f32[768]{0:T(1024)S(1)}, f32[768]{0:T(1024)}, u32[]{:S(2)}) copy-start(f32[768]{0:T(1024)} %get-tuple-element.279) | copy-start | bytes 9220
  470.0 126.8 %all-gather.11.cloned.1.call-start = ((), (), s32[]{:S(2)}) async-start(), calls=%async_computation.4 | async-start | bytes 4718592 | tf_op jit(solution)/shard_map/all_gather | solution.py:179
  533.4 14.5 %copy-start.46 = (bf16[192,2,768]{2,1,0:T(2,128)(2,1)S(1)}, bf16[192,2,768]{2,1,0:T(2,128)(2,1)}, u32[]{:S(2)}) copy-start(bf16[192,2,768]{2,1,0:T(2,128)(2,1)} %reshape_squeeze.28) | copy-start | bytes 1769476
  551.7 229.9 %all-gather.13.cloned.1.call-start = ((), (), s32[]{:S(2)}) async-start(), calls=%async_computation.5 | async-start | bytes 4718592 | tf_op jit(solution)/shard_map/all_gather | solution.py:217
  551.7 53.2 %copy-start.68 = (f32[2048]{0:T(1024)S(1)}, f32[2048]{0:T(1024)}, u32[]{:S(2)}) copy-start(f32[2048]{0:T(1024)} %copy-done.67) | copy-start | bytes 24580
  731.1 50.5 %copy-start.52 = (f32[2048]{0:T(1024)S(1)}, f32[2048]{0:T(1024)}, u32[]{:S(2)}) copy-start(f32[2048]{0:T(1024)} %copy-done.51) | copy-start | bytes 24580
  731.1 50.5 %copy-start.56 = (f32[2048]{0:T(1024)S(1)}, f32[2048]{0:T(1024)}, u32[]{:S(2)}) copy-start(f32[2048]{0:T(1024)} %copy-done.55) | copy-start | bytes 24580
  731.1 50.5 %copy-start.61 = (f32[768]{0:T(1024)S(1)}, f32[768]{0:T(1024)}, u32[]{:S(2)}) copy-start(f32[768]{0:T(1024)} %get-tuple-element.280) | copy-start | bytes 9220
  736.5 52.8 %copy-start.66 = (f32[2048]{0:T(1024)S(1)}, f32[2048]{0:T(1024)}, u32[]{:S(2)}) copy-start(f32[2048]{0:T(1024)} %copy-done.65) | copy-start | bytes 24580
  736.5 128.0 %all-gather.15.cloned.1.call-start = ((), (), s32[]{:S(2)}) async-start(), calls=%async_computation.6 | async-start | bytes 4718592 | tf_op jit(solution)/shard_map/all_gather | solution.py:179
  799.0 14.4 %copy-start.44 = (bf16[192,2,768]{2,1,0:T(2,128)(2,1)S(1)}, bf16[192,2,768]{2,1,0:T(2,128)(2,1)}, u32[]{:S(2)}) copy-start(bf16[192,2,768]{2,1,0:T(2,128)(2,1)} %reshape_squeeze.25) | copy-start | bytes 1769476
  819.4 293.7 %all-gather.17.cloned.1.call-start = ((), (), s32[]{:S(2)}) async-start(), calls=%async_computation.7 | async-start | bytes 4718592 | tf_op jit(solution)/shard_map/all_gather | solution.py:217
  834.4 30.1 %copy-start.5 = (bf16[2048,768]{1,0:T(8,128)(2,1)S(1)}, bf16[2048,768]{1,0:T(8,128)(2,1)}, u32[]{:S(2)}) copy-start(bf16[2048,768]{1,0:T(8,128)(2,1)} %param.16) | copy-start | bytes 9437188
  834.4 30.1 %copy-start.54 = (f32[2048]{0:T(1024)S(1)}, f32[2048]{0:T(1024)}, u32[]{:S(2)}) copy-start(f32[2048]{0:T(1024)} %copy-done.53) | copy-start | bytes 24580
  834.4 30.1 %copy-start.58 = (f32[2048]{0:T(1024)S(1)}, f32[2048]{0:T(1024)}, u32[]{:S(2)}) copy-start(f32[2048]{0:T(1024)} %copy-done.57) | copy-start | bytes 24580
  834.4 30.1 %copy-start.71 = (f32[768]{0:T(1024)S(1)}, f32[768]{0:T(1024)}, u32[]{:S(2)}) copy-start(f32[768]{0:T(1024)} %copy-done.70) | copy-start | bytes 9220
  843.6 27.4 %copy-start.64 = (f32[2048]{0:T(1024)S(1)}, f32[2048]{0:T(1024)}, u32[]{:S(2)}) copy-start(f32[2048]{0:T(1024)} %copy-done.63) | copy-start | bytes 24580
  1002.2 227.5 %all-reduce.9.cloned.1.call-start = ((), (), s32[]{:S(2)}) async-start(), calls=%async_computation.8 | async-start | bytes 17694720 | tf_op jit(solution)/shard_map/psum | solution.py:226
  (73 other events, 398.1 us)
Sparse Core Ops, SparseCore 0:
  80.3 88.4 all-reduce.4
  216.9 44.9 all-gather.6
  337.5 85.7 all-reduce.6
  470.1 44.9 all-gather.8
  551.8 44.9 all-gather.10
  736.6 44.9 all-gather.12
  819.5 44.9 all-gather.14
  1002.4 44.9 all-gather.16
  1052.0 177.6 all-reduce.8
where the time goes:
time: 1260 us; the launch traced here: 1250 us
  waiting for transfers between devices  458 us (36%)
  matrix products  295 us (23%)
  local copies, waits for them, and re-layouts  283 us (22%)
  other arithmetic  127 us (10%)
  blocking collectives  64.6 us (5%)
  between operations  15.5 us (1%)
    psum x2, waiting for transfers between devices, project(): lax.psum(partial_sum.astype(jnp.bfloat16), 'head').astype(jnp.float32)  159 us
    psum x1, waiting for transfers between devices, reduce_grads(): return lax.psum(grads, 'dp')  110 us
    all_gather x2, waiting for transfers between devices, layer_forward(): branch = lax.all_gather(branch, 'head', axis=1, tiled=True)  78.1 us
    dot_general x4, matrix products, grouped(): jnp.einsum('tgi,igo->tgo', in_parts, kernel, preferred_element_type=jnp.f...  68.2 us
    all_gather x2, waiting for transfers between devices, layer_backward(): lax.all_gather(grad_first_in.astype(jnp.bfloat16), 'head', axis=1, tiled=...  66 us
    psum x1, blocking collectives, reduce_grads(): return lax.psum(grads, 'dp')  64.6 us
    dynamic_slice x72, local copies, waits for them, and re-layouts, layer_forward(): lax.map(attend_row, (stacked[0], stacked[1], stacked[2], segment_rows))  55.5 us
    all_gather x2, waiting for transfers between devices, layer_backward(): lax.all_gather(grad_state_in.astype(jnp.bfloat16), 'head', axis=1, tiled=...  45 us
  transfers between devices with their start and end apart: 9, of which 8 were waited for; matrix products, arithmetic and copies ran while one was open for 8% of the time, Pallas kernels for 0%

commit v1 on v0

v1 whole, which is shorter than its diff:
```python
import functools
import jax
import jax.numpy as jnp
from jax import lax
from jax.experimental import pallas as pl
from jax.experimental.pallas import tpu as pltpu
from jax.sharding import PartitionSpec as P

HEAD_DIM = 64
QUERY_TILE = 256
REACH = 128

epsilon = 1e-12
masked_score = -1e30
f32 = jnp.float32
bf16 = jnp.bfloat16

NN = (((1,), (0,)), ((), ()))
NT = (((1,), (1,)), ((), ()))
TN = (((0,), (0,)), ((), ()))


def mm(left, right, dims):
    return lax.dot_general(left, right, dims, preferred_element_type=f32)


def key_start(tile, seq_len):
    return min(max(tile * QUERY_TILE - REACH, 0), seq_len - QUERY_TILE - REACH)


def live_keys(tile, piece, seq_len):
    window = QUERY_TILE + REACH
    first_query = tile * QUERY_TILE + piece * REACH
    start = key_start(tile, seq_len)
    low = max(first_query - REACH - start, 0)
    high = min(first_query + 2 * REACH - start, window)
    return low, high


def block_diagonal(parts):
    rows = []
    for index, part in enumerate(parts):
        empty = jnp.zeros_like(part)
        rows.append(
            jnp.concatenate([part if at == index else empty for at in range(len(parts))], axis=1)
        )
    return jnp.concatenate(rows, axis=0)


def fill_rows(middle, low, high, total):
    pieces = []
    if low > 0:
        pieces.append(jnp.zeros((low, middle.shape[1]), middle.dtype))
    pieces.append(middle)
    if high < total:
        pieces.append(jnp.zeros((total - high, middle.shape[1]), middle.dtype))
    return jnp.concatenate(pieces, axis=0) if len(pieces) > 1 else middle


def attend_kernel(
    place, x_ref, w_ref, segq_ref, segk_ref, xt_ref, qt_ref, kt_ref, v_ref, p_ref, ct_ref
):
    seq_len, channels = x_ref.shape
    width = w_ref.shape[1]
    window = QUERY_TILE + REACH
    heads = width // HEAD_DIM
    tiles = seq_len // QUERY_TILE
    x = x_ref[...]
    xt = x.T
    xt_ref[0] = xt
    segq = segq_ref[0]
    segk = segk_ref[0]
    masks = {}
    for tile in range(tiles):
        start = key_start(tile, seq_len)
        for piece in range(QUERY_TILE // REACH):
            low, high = live_keys(tile, piece, seq_len)
            at = tile * QUERY_TILE + piece * REACH
            same = segk[start + low : start + high] == segq[:, at : at + REACH]
            masks[tile, piece] = jnp.where(same, 0.0, masked_score)
    for group in range(channels // width):
        span = slice(group * width, (group + 1) * width)
        xg = x[:, span]
        xtg = xt[span]
        wq, wk, wv = (w_ref[s][:, span] for s in range(3))
        qt = mm(wq, xtg, TN).astype(bf16) * jnp.asarray(HEAD_DIM**-0.5, bf16)
        kt = mm(wk, xtg, TN).astype(bf16)
        vt = mm(wv, xtg, TN).astype(bf16)
        keys = mm(xg, wk, NN).astype(bf16)
        values = mm(xg, wv, NN).astype(bf16)
        qt_ref[0, span] = qt
        kt_ref[0, span] = kt * jnp.asarray(HEAD_DIM**-0.5, bf16)
        v_ref[0, group] = values
        for tile in range(tiles):
            start = key_start(tile, seq_len)
            asked = slice(tile * QUERY_TILE, (tile + 1) * QUERY_TILE)
            spread = block_diagonal(
                [qt[i * HEAD_DIM : (i + 1) * HEAD_DIM, asked] for i in range(heads)]
            )
            scores = mm(keys[start : start + window], spread, NN)
            for i in range(heads):
                probs = []
                for piece in range(QUERY_TILE // REACH):
                    low, high = live_keys(tile, piece, seq_len)
                    at = i * QUERY_TILE + piece * REACH
                    s = scores[low:high, at : at + REACH] + masks[tile, piece]
                    top = jnp.max(s, axis=0, keepdims=True)
                    e = jnp.exp(s - top)
                    total = jnp.sum(e, axis=0, keepdims=True)
                    p = (e * (1.0 / total)).astype(bf16)
                    probs.append(fill_rows(p, low, high, window))
                probs = jnp.concatenate(probs, axis=1)
                p_ref[0, group, tile, :, i * QUERY_TILE : (i + 1) * QUERY_TILE] = probs
                context = mm(
                    vt[i * HEAD_DIM : (i + 1) * HEAD_DIM, start : start + window], probs, NN
                )
                at = group * width + i * HEAD_DIM
                ct_ref[0, at : at + HEAD_DIM, asked] = context.astype(bf16)


def attend_back_kernel(
    last,
    place,
    dc_ref,
    ct_ref,
    p_ref,
    qt_ref,
    kt_ref,
    v_ref,
    xt_ref,
    w_ref,
    dz_ref,
    dx_ref,
    grad_ref,
    ds_ref,
):
    channels, seq_len = xt_ref.shape[1:]
    width = w_ref.shape[1]
    window = QUERY_TILE + REACH
    heads = width // HEAD_DIM
    tiles = seq_len // QUERY_TILE
    step = pl.program_id(0)
    grads = [[], [], []]
    d_inputs = []
    for group in range(channels // width):
        span = slice(group * width, (group + 1) * width)
        dq_tiles = []
        dk_tiles = []
        dv_tiles = []
        for tile in range(tiles):
            start = key_start(tile, seq_len)
            asked = slice(tile * QUERY_TILE, (tile + 1) * QUERY_TILE)
            d_context = dc_ref[0, span, asked]
            context = ct_ref[0, span, asked]
            both = d_context.astype(f32) * context.astype(f32)
            spread_dc = block_diagonal(
                [d_context[i * HEAD_DIM : (i + 1) * HEAD_DIM] for i in range(heads)]
            )
            qt = qt_ref[0, span, asked]
            spread_q = block_diagonal(
                [qt[i * HEAD_DIM : (i + 1) * HEAD_DIM] for i in range(heads)]
            )
            d_probs = mm(v_ref[0, group, start : start + window], spread_dc, NN)
            dq_heads = []
            for i in range(heads):
                shared = jnp.sum(both[i * HEAD_DIM : (i + 1) * HEAD_DIM], axis=0, keepdims=True)
                for piece in range(QUERY_TILE // REACH):
                    low, high = live_keys(tile, piece, seq_len)
                    at = i * QUERY_TILE + piece * REACH
                    p = p_ref[0, group, tile, low:high, at : at + REACH].astype(f32)
                    dp = d_probs[low:high, at : at + REACH]
                    ds = (p * (dp - shared[:, piece * REACH : (piece + 1) * REACH])).astype(bf16)
                    ds_ref[:, at : at + REACH] = fill_rows(ds, low, high, window)
                rows = slice(group * width + i * HEAD_DIM, group * width + (i + 1) * HEAD_DIM)
                dq_heads.append(
                    mm(
                        kt_ref[0, rows, start : start + window],
                        ds_ref[:, i * QUERY_TILE : (i + 1) * QUERY_TILE],
                        NN,
                    )
                )
            dq_tiles.append(jnp.concatenate(dq_heads, axis=0))
            dk_tiles.append(mm(ds_ref[...], spread_q, NT))
            dv_tiles.append(mm(p_ref[0, group, tile], spread_dc, NT))
        dq = jnp.concatenate(dq_tiles, axis=1).astype(bf16)
        dk = join_windows(dk_tiles, seq_len).astype(bf16)
        dv = join_windows(dv_tiles, seq_len).astype(bf16)
        xtg = xt_ref[0, span]
        grads[0].append(mm(xtg, dq, NT))
        grads[1].append(mm(xtg, dk, NN))
        grads[2].append(mm(xtg, dv, NN))
        wq, wk, wv = (w_ref[s][:, span] for s in range(3))
        d_inputs.append(
            dz_ref[0, 0, span] + mm(wq, dq, NN) + mm(wk, dk, NT) + mm(wv, dv, NT)
        )
    joined = [jnp.concatenate(parts, axis=1) for parts in grads]

    @pl.when(step == 0)
    def _():
        for s in range(3):
            grad_ref[s] = joined[s]

    @pl.when(step > 0)
    def _():
        for s in range(3):
            grad_ref[s] += joined[s]

    d_input = jnp.concatenate(d_inputs, axis=0)
    if last:
        dx_ref[...] = d_input.astype(bf16).T
    else:
        dx_ref[0] = d_input


def join_windows(pieces, seq_len):
    window = QUERY_TILE + REACH
    rows = []
    for at in range(0, seq_len, REACH):
        held = []
        for tile, piece in enumerate(pieces):
            start = key_start(tile, seq_len)
            if start <= at < start + window:
                held.append(piece[at - start : at - start + REACH])
        rows.append(functools.reduce(jnp.add, held))
    return jnp.concatenate(rows, axis=0)


def feature_mean(values):
    return jnp.sum(values, axis=0, keepdims=True) * (1.0 / values.shape[0])


def normalize(before):
    centered = before - feature_mean(before)
    inverse = lax.rsqrt(feature_mean(centered * centered) + epsilon)
    return centered * inverse, inverse


def normalize_back(gradient, gains, normal, inverse):
    scaled = gradient * gains
    return inverse * (scaled - feature_mean(scaled) - normal * feature_mean(scaled * normal))


def ffn_kernel(first_layer, place, *refs):
    if first_layer:
        xt0, xt1, *refs = refs
    else:
        x_ref, *refs = refs
    (ct0, ct1, ow0, ow1, iw0, iw1, uw0, uw1, gains, *refs) = refs
    (n1_ref, r1_ref, act_ref, slope_ref, n2_ref, r2_ref, tok_ref, *refs) = refs
    if first_layer:
        next_ref, *refs = refs
    z_scr, fb_scr = refs
    half, seq_len = z_scr.shape[1:]
    wide = 2 * half
    width = iw0.shape[0]
    own = place[0]
    sides = (own, 1 - own)
    attention = mm(ow0[...], ct0[0], TN) + mm(ow1[...], ct1[0], TN)
    z_scr[...] = attention.reshape(2, half, seq_len)
    if first_layer:
        z_scr[sides[0]] += xt0[0].astype(f32)
        z_scr[sides[1]] += xt1[0].astype(f32)
        before = z_scr[...].reshape(wide, seq_len)
    else:
        before = (z_scr[...] + x_ref[0]).reshape(wide, seq_len)
    normal, inverse = normalize(before)
    first = normal * gains[0]
    n1_ref[0] = normal.reshape(2, half, seq_len)
    r1_ref[0] = inverse
    z_scr[...] = first.reshape(2, half, seq_len)
    fb_scr[...] = first.astype(bf16).reshape(2, half, seq_len)
    for j, (iw, uw) in enumerate(((iw0, uw0), (iw1, uw1))):
        hidden = iw.shape[1] // (half // width)
        for group in range(half // width):
            span = slice(group * width, (group + 1) * width)
            pre = mm(iw[:, group * hidden : (group + 1) * hidden], fb_scr[sides[j], span], TN)
            below = 0.5 + 0.5 * lax.erf(pre * 0.7071067811865476)
            act = (pre * below).astype(bf16)
            slope = below + pre * (jnp.exp(-0.5 * pre * pre) * 0.3989422804014327)
            act_ref[0, j, group] = act
            slope_ref[0, j, group] = slope.astype(bf16)
            z_scr[sides[j], span] += mm(uw[:, span], act, TN)
    normal, inverse = normalize(z_scr[...].reshape(wide, seq_len))
    n2_ref[0] = normal.reshape(2, half, seq_len)
    r2_ref[0] = inverse
    output = normal * gains[1]
    if first_layer:
        next_ref[0] = output.reshape(2, half, seq_len)
    tok_ref[...] = output.astype(bf16).T


def ffn_back_kernel(last_layer, place, *refs):
    if last_layer:
        cot_ref, *refs = refs
    else:
        g0, g1, *refs = refs
    (n2_ref, r2_ref, act_ref, slope_ref, n1_ref, r1_ref, ct0, ct1, *refs) = refs
    (ow0, ow1, iw0, iw1, uw0, uw1, gains, *refs) = refs
    (dz1_ref, dc0, dc1, outer_ref, inner_ref, out_ref, gain_ref, d_scr, b_scr, f_scr) = refs
    half, seq_len = d_scr.shape[1:]
    wide = 2 * half
    width = iw0.shape[0]
    own = place[0]
    sides = (own, 1 - own)
    step = pl.program_id(0)

    @pl.when(step == 0)
    def _():
        outer_ref[...] = jnp.zeros_like(outer_ref)
        inner_ref[...] = jnp.zeros_like(inner_ref)
        out_ref[...] = jnp.zeros_like(out_ref)
        gain_ref[...] = jnp.zeros_like(gain_ref)

    if last_layer:
        g = cot_ref[...].T.astype(f32)
    else:
        d_scr[sides[0]] = g0[0]
        d_scr[sides[1]] = g1[0]
        g = d_scr[...].reshape(wide, seq_len)
    normal = n2_ref[0].reshape(wide, seq_len)
    gain_ref[1] += jnp.sum(g * normal, axis=1, keepdims=True)
    d_second = normalize_back(g, gains[1], normal, r2_ref[0])
    d_scr[...] = d_second.reshape(2, half, seq_len)
    b_scr[...] = d_second.astype(bf16).reshape(2, half, seq_len)
    normal = n1_ref[0].reshape(wide, seq_len)
    f_scr[...] = (normal * gains[0]).astype(bf16).reshape(2, half, seq_len)
    for j, (iw, uw) in enumerate(((iw0, uw0), (iw1, uw1))):
        hidden = iw.shape[1] // (half // width)
        outers = []
        for group in range(half // width):
            span = slice(group * width, (group + 1) * width)
            units = slice(group * hidden, (group + 1) * hidden)
            d_branch = b_scr[sides[j], span]
            first = f_scr[sides[j], span]
            outers.append(mm(act_ref[0, j, group], d_branch, NT))
            d_act = mm(uw[:, span], d_branch, NN)
            d_pre = (d_act * slope_ref[0, j, group].astype(f32)).astype(bf16)
            inner_ref[j, :, units] += mm(first, d_pre, NT)
            d_scr[sides[j], span] += mm(iw[:, units], d_pre, NN)
        outer_ref[j] += jnp.concatenate(outers, axis=1)
    d_first = d_scr[...].reshape(wide, seq_len)
    gain_ref[0] += jnp.sum(d_first * normal, axis=1, keepdims=True)
    d_before = normalize_back(d_first, gains[0], normal, r1_ref[0])
    dz1_ref[0] = d_before.reshape(2, half, seq_len)
    d_attention = d_before.astype(bf16)
    for j, (ow, ct, dc) in enumerate(((ow0, ct0, dc0), (ow1, ct1, dc1))):
        out_ref[j] += mm(ct[0], d_attention, NT)
        dc[0] = mm(ow[...], d_attention, NN).astype(bf16)


def whole(shape):
    return pl.BlockSpec(shape, lambda r, place: (0,) * len(shape))


def per_row(shape):
    rest = (0,) * (len(shape) - 1)
    return pl.BlockSpec((1,) + tuple(shape[1:]), lambda r, place: (r,) + rest)


def struct(shape, dtype):
    return jax.ShapeDtypeStruct(shape, dtype)


def call(kernel, rows, place, operands, in_specs, outs, out_specs, scratch, name):
    return pl.pallas_call(
        kernel,
        out_shape=outs,
        grid_spec=pltpu.PrefetchScalarGridSpec(
            num_scalar_prefetch=1,
            grid=(rows,),
            in_specs=in_specs,
            out_specs=out_specs,
            scratch_shapes=scratch,
        ),
        compiler_params=pltpu.CompilerParams(vmem_limit_bytes=60 * 2**20),
        name=name,
    )(place, *operands)


def attend(x_tok, w, segq, segk, place, rows):
    seq_len = segq.shape[-1]
    channels = w.shape[-1]
    width = w.shape[1]
    heads = width // HEAD_DIM
    groups = channels // width
    tiles = seq_len // QUERY_TILE
    window = QUERY_TILE + REACH
    outs = [
        struct((rows, channels, seq_len), bf16),
        struct((rows, channels, seq_len), bf16),
        struct((rows, channels, seq_len), bf16),
        struct((rows, groups, seq_len, width), bf16),
        struct((rows, groups, tiles, window, heads * QUERY_TILE), bf16),
        struct((rows, channels, seq_len), bf16),
    ]
    return call(
        attend_kernel,
        rows,
        place,
        (x_tok, w, segq, segk),
        [
            pl.BlockSpec((seq_len, channels), lambda r, place: (place[0] + r, place[1])),
            whole(w.shape),
            pl.BlockSpec((1, 1, seq_len), lambda r, place: (place[2] + r, 0, 0)),
            pl.BlockSpec((1, seq_len, 1), lambda r, place: (place[2] + r, 0, 0)),
        ],
        outs,
        [per_row(o.shape) for o in outs],
        [],
        "attend",
    )


def attend_back(d_context, saved, w, d_before, place, rows, last):
    xt, qt, kt, values, probs, ct = saved
    channels, seq_len = xt.shape[1:]
    window = QUERY_TILE + REACH
    heads = w.shape[1] // HEAD_DIM
    if last:
        dx = struct((rows * seq_len, channels), bf16)
        dx_spec = pl.BlockSpec((seq_len, channels), lambda r, place: (r, 0))
    else:
        dx = struct((rows, channels, seq_len), f32)
        dx_spec = per_row(dx.shape)
    operands = (d_context, ct, probs, qt, kt, values, xt)
    return call(
        functools.partial(attend_back_kernel, last),
        rows,
        place,
        operands + (w, d_before),
        [per_row(o.shape) for o in operands]
        + [
            whole(w.shape),
            pl.BlockSpec((1, 1, channels, seq_len), lambda r, place: (r, place[1], 0, 0)),
        ],
        [dx, struct(w.shape, f32)],
        [dx_spec, whole(w.shape)],
        [pltpu.VMEM((window, heads * QUERY_TILE), bf16)],
        "attend_back",
    )


def ffn(x_parts, contexts, weights, gains, place, rows, first_layer):
    half, seq_len = contexts[0].shape[1:]
    hidden = weights[2].shape[1] * 2 // (2 * (half // weights[2].shape[0]))
    groups = half // weights[2].shape[0]
    stream = (rows, 2, half, seq_len)
    acts = (rows, 2, groups, hidden, seq_len)
    outs = [
        struct(stream, f32),
        struct((rows, 1, seq_len), f32),
        struct(acts, bf16),
        struct(acts, bf16),
        struct(stream, f32),
        struct((rows, 1, seq_len), f32),
        struct((rows * seq_len, 2 * half), bf16),
    ]
    out_specs = [per_row(o.shape) for o in outs]
    out_specs[-1] = pl.BlockSpec((seq_len, 2 * half), lambda r, place: (r, 0))
    if first_layer:
        outs.append(struct(stream, f32))
        out_specs.append(per_row(stream))
    return call(
        functools.partial(ffn_kernel, first_layer),
        rows,
        place,
        tuple(x_parts) + tuple(contexts) + tuple(weights) + (gains,),
        [per_row(o.shape) for o in x_parts]
        + [per_row(o.shape) for o in contexts]
        + [whole(o.shape) for o in weights]
        + [whole(gains.shape)],
        outs,
        out_specs,
        [pltpu.VMEM((2, half, seq_len), f32), pltpu.VMEM((2, half, seq_len), bf16)],
        "ffn",
    )


def ffn_back(g_parts, saved, contexts, weights, gains, place, rows, last_layer):
    half, seq_len = contexts[0].shape[1:]
    if last_layer:
        g_specs = [pl.BlockSpec((seq_len, 2 * half), lambda r, place: (place[1] + r, 0))]
    else:
        g_specs = [per_row(o.shape) for o in g_parts]
    stream = (rows, 2, half, seq_len)
    ow, iw, uw = weights[0], weights[2], weights[4]
    grad_shapes = [(2,) + uw.shape, (2,) + iw.shape, (2,) + ow.shape, gains.shape]
    outs = [
        struct(stream, f32),
        struct(contexts[0].shape, bf16),
        struct(contexts[0].shape, bf16),
    ]
    out_specs = [per_row(o.shape) for o in outs] + [whole(s) for s in grad_shapes]
    outs += [struct(s, f32) for s in grad_shapes]
    operands = tuple(saved) + tuple(contexts)
    return call(
        functools.partial(ffn_back_kernel, last_layer),
        rows,
        place,
        tuple(g_parts) + operands + tuple(weights) + (gains,),
        g_specs
        + [per_row(o.shape) for o in operands]
        + [whole(o.shape) for o in weights]
        + [whole(gains.shape)],
        outs,
        out_specs,
        [
            pltpu.VMEM((2, half, seq_len), f32),
            pltpu.VMEM((2, half, seq_len), bf16),
            pltpu.VMEM((2, half, seq_len), bf16),
        ],
        "ffn_back",
    )


def swap(values):
    return lax.ppermute(values, "head", [(0, 1), (1, 0)])


def shards(
    tokens, segments, qkv_weight, out_weight, inner_weight, outer_weight, norm_gains, cotangent
):
    head_place = lax.axis_index("head").astype(jnp.int32)
    layers = qkv_weight.shape[0]
    row_total, seq_len = segments.shape
    rows = row_total // 2
    offset = head_place * rows
    segq = segments.reshape(row_total, 1, seq_len)
    segk = segments.reshape(row_total, seq_len, 1)
    gains = norm_gains[..., None]
    zero = jnp.zeros((), jnp.int32)
    far_qkv = [swap(qkv_weight[i]) for i in range(layers)]
    far_rest = [
        [swap(w[i]) for w in (out_weight, inner_weight, outer_weight)] for i in range(layers)
    ]
    ffn_weights = []
    for i in range(layers):
        both = []
        for near, far in zip((out_weight, inner_weight, outer_weight), far_rest[i]):
            both += [near[i], far]
        ffn_weights.append(both)
    sides = (head_place, 1 - head_place)
    x_tok = tokens
    x_stream = None
    saved_attend = []
    saved_ffn = []
    contexts = []
    for i in range(layers):
        held = []
        for j, w in enumerate((qkv_weight[i], far_qkv[i])):
            place = jnp.stack([offset if i == 0 else zero, sides[j], offset])
            held.append(attend(x_tok, w, segq, segk, place, rows))
        saved_attend.append(held)
        contexts.append([h[5] for h in held])
        first_layer = i == 0
        x_parts = [h[0] for h in held] if first_layer else [x_stream]
        place = jnp.stack([head_place, offset])
        results = ffn(x_parts, contexts[i], ffn_weights[i], gains[i], place, rows, i < layers - 1)
        n1, r1, act, slope, n2, r2, x_tok = results[:7]
        if i < layers - 1:
            x_stream = results[7]
        saved_ffn.append((n2, r2, act, slope, n1, r1))
    far_tok = swap(x_tok)
    activations = in_order(x_tok, far_tok, head_place)
    g_parts = [cotangent]
    grads = [None] * layers
    for i in reversed(range(layers)):
        place = jnp.stack([head_place, offset])
        d_before, dc0, dc1, outer, inner, out, gain = ffn_back(
            g_parts, saved_ffn[i], contexts[i], ffn_weights[i], gains[i], place, rows, i == layers - 1
        )
        g_parts = []
        qkv = []
        for j, (w, dc) in enumerate(((qkv_weight[i], dc0), (far_qkv[i], dc1))):
            place = jnp.stack([zero, sides[j], zero])
            dx, grad = attend_back(dc, saved_attend[i][j], w, d_before, place, rows, i == 0)
            g_parts.append(dx)
            qkv.append(grad)
        grads[i] = (qkv, out, inner, outer, gain[..., 0])
    mine = jnp.where(head_place == 0, jnp.concatenate(g_parts, 1), jnp.concatenate(g_parts[::-1], 1))
    input_grad = in_order(mine, swap(mine), head_place)
    totals = []
    for at in range(4):
        near = jnp.stack([g[at][0] for g in grads])
        far = jnp.stack([g[at][1] for g in grads])
        totals.append(near + swap(far.astype(bf16)).astype(f32))
    totals = lax.psum(tuple(totals), "dp")
    gain_total = lax.psum(jnp.stack([g[4] for g in grads]), ("dp", "head"))
    return (activations, input_grad, *totals, gain_total)


def in_order(near, far, head_place):
    return jnp.where(
        head_place == 0, jnp.concatenate([near, far]), jnp.concatenate([far, near])
    )


def solution(mesh):
    return jax.shard_map(
        shards,
        mesh=mesh,
        in_specs=(
            P("dp", None),
            P("dp", None),
            P(None, None, None, "head"),
            P(None, "head", None),
            P(None, None, "head"),
            P(None, None, "head"),
            P(),
            P("dp", None),
        ),
        out_specs=(
            P("dp", None),
            P("dp", None),
            P(None, None, None, "head"),
            P(None, "head", None),
            P(None, None, "head"),
            P(None, None, "head"),
            P(),
        ),
        check_vma=False,
    )
```

time: 1260 us -> 519 us (0.41)
  waiting for transfers between devices: 458 us -> 142 us
  matrix products: 295 us -> 0 us
  local copies, waits for them, and re-layouts: 283 us -> 25.7 us
  Pallas kernels: 0 us -> 179 us
  other arithmetic: 127 us -> 34.3 us
  blocking collectives: 64.6 us -> 98.4 us
  starting transfers between devices: 0.78 us -> 18 us
    dot_general x78 -> x0, matrix products: 290 us -> none  [the longest x4 68.2 us: grouped(): jnp.einsum('tgi,igo->tgo', in_parts, kernel, preferred_element_type=jnp.f...]
    psum x3 -> x1, waiting for transfers between devices: 269 us -> 66.6 us  [shards(): totals = lax.psum(tuple(totals), 'dp')]
    all_gather x6 -> x0, waiting for transfers between devices: 189 us -> none  [the longest x2 78.1 us: layer_forward(): branch = lax.all_gather(branch, 'head', axis=1, tiled=True)]
    pallas_call x0 -> x12, Pallas kernels: none -> 179 us  [call(): pl.pallas_call(kernel, out_shape=outs, grid_spec=pltpu.PrefetchScalarGrid...]
    reduce_sum x23 -> x0, other arithmetic: 77 us -> none  [the longest x5 28.2 us: normalize(): return centered * lax.rsqrt(spread + epsilon) * gains]
    ppermute x0 -> x14, waiting for transfers between devices: none -> 75.6 us  [swap(): return lax.ppermute(values, 'head', [(0, 1), (1, 0)])]
    another operation x30 -> x0, local copies, waits for them, and re-layouts: 66.8 us -> none  [the longest x8 21.9 us: layer_backward(): grad_qkv = jnp.stack(grad_rows).reshape(3, token_count, channels)]
    dynamic_slice x77 -> x0, local copies, waits for them, and re-layouts: 60.1 us -> none  [the longest x72 55.5 us: layer_forward(): lax.map(attend_row, (stacked[0], stacked[1], stacked[2], segment_rows))]
  transfers between devices with their start and end apart: 9 -> 15, of which waited for: 8 -> 7; matrix products, arithmetic and copies ran while one was open for 8% -> 8% of each run, Pallas kernels for 0% -> 16%
where the time goes in v1:
time: 519 us; the launch traced here: 513 us
  Pallas kernels  179 us (34%)
  waiting for transfers between devices  142 us (27%)
  blocking collectives  98.4 us (19%)
  other arithmetic  34.3 us (7%)
  local copies, waits for them, and re-layouts  25.7 us (5%)
  starting transfers between devices  18 us (3%)
  between operations  14.8 us (3%)
    pallas_call x12, Pallas kernels, call(): pl.pallas_call(kernel, out_shape=outs, grid_spec=pltpu.PrefetchScalarGrid...  179 us
    psum x1, blocking collectives, shards(): gain_total = lax.psum(jnp.stack([g[4] for g in grads]), ('dp', 'head'))  98.4 us
    ppermute x14, waiting for transfers between devices, swap(): return lax.ppermute(values, 'head', [(0, 1), (1, 0)])  75.6 us
    psum x1, waiting for transfers between devices, shards(): totals = lax.psum(tuple(totals), 'dp')  66.6 us
    ppermute x14, starting transfers between devices, swap(): return lax.ppermute(values, 'head', [(0, 1), (1, 0)])  18 us
    add x4, other arithmetic, shards(): totals.append(near + swap(far.astype(bf16)).astype(f32))  12 us
    unnamed x58, local copies, waits for them, and re-layouts  11.7 us
  transfers between devices with their start and end apart: 15, of which 7 were waited for; matrix products, arithmetic and copies ran while one was open for 8% of the time, Pallas kernels for 16%

profile of v1, /device:TPU:0, one launch (start us, length us, event | category | flops | bytes accessed | tf_op | source)
XLA Modules:
  0.0 512.7 jit_solution(1563650701144752887)
XLA Ops:
  7.2 2.3 slice_bitcast_fusion.6
  9.5 2.9 collective-permute-start
  12.8 2.1 collective-permute-start.2
  19.0 4.8 collective-permute-done.w_ref
  23.8 2.1 collective-permute-start.6
  25.8 10.6 %collective-permute-done.1.refs_5_.refs_11_ = bf16[384,768]{1,0:T(8,128)(2,1)} collective-permute-done((bf16[384,768]{1,0:T(8,128)(2,1)S(1)}, bf16[384,768]{1,0:T(8,128)(2,1)}, u32[]{:S(2)}, u32[]{:S(2)}) %collective-permute-start.1) | collective-permute-done | bytes 589856 | tf_op jit(solution)/shard_map/ppermute | solution.py:517
  44.1 9.4 %attend.4 = (bf16[2,384,512]{2,1,0:T(8,128)(2,1)}, bf16[2,384,512]{2,1,0:T(8,128)(2,1)}, bf16[2,384,512]{2,1,0:T(8,128)(2,1)}, bf16[2,2,512,192]{3,2,1,0:T(8,128...) custom-call(s32[3]{0:T(128)} %add_add_fusion.place, bf16[2048,768]{1,0:T(8,128)(2,1)} %x_ref.3, ...), custom_call_target="tpu_custom_call" | custom-call | tf_op jit(solution)/shard_map/attend/pallas_call | solution.py:365
  56.6 9.2 %attend.5 = (bf16[2,384,512]{2,1,0:T(8,128)(2,1)}, bf16[2,384,512]{2,1,0:T(8,128)(2,1)}, bf16[2,384,512]{2,1,0:T(8,128)(2,1)}, bf16[2,2,512,192]{3,2,1,0:T(8,128...) custom-call(s32[3]{0:T(128)} %add_add_fusion.1.place, bf16[2048,768]{1,0:T(8,128)(2,1)} %x_ref.3, ...), custom_call_target="tpu_custom_call" | custom-call | tf_op jit(solution)/shard_map/attend/pallas_call | solution.py:365
  65.8 21.1 %ffn.2 = (f32[2,2,384,512]{3,2,1,0:T(8,128)}, f32[2,1,512]{2,1,0:T(1,128)}, bf16[2,2,2,768,512]{4,3,2,1,0:T(8,128)(2,1)}, bf16[2,2,2,768,512]{4,3,2,1,0:T(8,128)...) custom-call(s32[2]{0:T(128)} %pad_add_fusion.4.place, ...), custom_call_target="tpu_custom_call" | custom-call | tf_op jit(solution)/shard_map/ffn/pallas_call | solution.py:365
  86.9 9.2 %attend.6 = (bf16[2,384,512]{2,1,0:T(8,128)(2,1)}, bf16[2,384,512]{2,1,0:T(8,128)(2,1)}, bf16[2,384,512]{2,1,0:T(8,128)(2,1)}, bf16[2,2,512,192]{3,2,1,0:T(8,128...) custom-call(s32[3]{0:T(128)} %fusion.place, bf16[1024,768]{1,0:T(8,128)(2,1)} %get-tuple-element.73.x_ref, ...), custom_call_target="tpu_custom_call" | custom-call | tf_op jit(solution)/shard_map/attend/pallas_call | solution.py:365
  96.1 12.1 %collective-permute-done.4.w_ref = bf16[3,192,384]{2,1,0:T(8,128)(2,1)S(1)} collective-permute-done((bf16[3,192,384]{2,1,0:T(8,128)(2,1)S(1)}, bf16[3,192,384]{2,1,0:T(8,128)(2,1)S(1)}, u32[]{:S(2)}, u32[]{:S(2)}) %collective-permute-start.4) | collective-permute-done | bytes 442400 | tf_op jit(solution)/shard_map/ppermute | solution.py:517
  109.0 9.6 %attend.7 = (bf16[2,384,512]{2,1,0:T(8,128)(2,1)}, bf16[2,384,512]{2,1,0:T(8,128)(2,1)}, bf16[2,384,512]{2,1,0:T(8,128)(2,1)}, bf16[2,2,512,192]{3,2,1,0:T(8,128...) custom-call(s32[3]{0:T(128)} %fusion.1.place, bf16[1024,768]{1,0:T(8,128)(2,1)} %get-tuple-element.73.x_ref, ...), custom_call_target="tpu_custom_call" | custom-call | tf_op jit(solution)/shard_map/attend/pallas_call | solution.py:365
  119.4 20.3 %ffn.3 = (f32[2,2,384,512]{3,2,1,0:T(8,128)}, f32[2,1,512]{2,1,0:T(1,128)}, bf16[2,2,2,768,512]{4,3,2,1,0:T(8,128)(2,1)}, bf16[2,2,2,768,512]{4,3,2,1,0:T(8,128)...) custom-call(s32[2]{0:T(128)} %pad_add_fusion.4.place, ...), custom_call_target="tpu_custom_call" | custom-call | tf_op jit(solution)/shard_map/ffn/pallas_call | solution.py:365
  139.7 25.5 %ffn_back.2 = (f32[2,2,384,512]{3,2,1,0:T(8,128)}, bf16[2,384,512]{2,1,0:T(8,128)(2,1)}, bf16[2,384,512]{2,1,0:T(8,128)(2,1)}, f32[2,768,384]{2,1,0:T(8,128)}, f...) custom-call(s32[2]{0:T(128)} %pad_add_fusion.4.place, bf16[2048,768]{1,0:T(8,128)(2,1)} %refs_0_.1, ...), custom_call_target="tpu_custom_call" | custom-call | tf_op jit(solution)/shard_map/ffn_back/pallas_call | solution.py:365
  165.2 12.9 %attend_back.4 = (f32[2,384,512]{2,1,0:T(8,128)}, f32[3,192,384]{2,1,0:T(8,128)}) custom-call(s32[3]{0:T(128)} %pad_add_fusion.3.place, bf16[2,384,512]{2,1,0:T(8,128)(2,1)} %get-tuple-element.83.dc_ref, bf16[2,384,512]{2,1,0:T(8,128)(2,1)} %get-tuple-element.74.refs_1_.refs_7_.ct_ref, bf16[2,2,2,384,768]{4,3,2,1,0:T(8,128)(2,1)} %get-tuple-element.84.p_ref, ...), custom_call_target="tpu_custom_call" | custom-call | tf_op jit(solution)/shard_map/attend_back/pallas_call | solution.py:365
  178.1 13.1 %attend_back.5 = (f32[2,384,512]{2,1,0:T(8,128)}, f32[3,192,384]{2,1,0:T(8,128)}) custom-call(s32[3]{0:T(128)} %pad_add_fusion.2.place, bf16[2,384,512]{2,1,0:T(8,128)(2,1)} %get-tuple-element.91.dc_ref, bf16[2,384,512]{2,1,0:T(8,128)(2,1)} %get-tuple-element.75.refs_2_.refs_8_.ct_ref, bf16[2,2,2,384,768]{4,3,2,1,0:T(8,128)(2,1)} %get-tuple-element.92.p_ref, ...), custom_call_target="tpu_custom_call" | custom-call | tf_op jit(solution)/shard_map/attend_back/pallas_call | solution.py:365
  191.2 22.8 %ffn_back.3 = (f32[2,2,384,512]{3,2,1,0:T(8,128)}, bf16[2,384,512]{2,1,0:T(8,128)(2,1)}, bf16[2,384,512]{2,1,0:T(8,128)(2,1)}, f32[2,768,384]{2,1,0:T(8,128)}, f...) custom-call(s32[2]{0:T(128)} %pad_add_fusion.4.place, ...), custom_call_target="tpu_custom_call" | custom-call | tf_op jit(solution)/shard_map/ffn_back/pallas_call | solution.py:365
  218.3 13.2 %attend_back.7 = (bf16[1024,384]{1,0:T(8,128)(2,1)}, f32[3,192,384]{2,1,0:T(8,128)}) custom-call(s32[3]{0:T(128)} %pad_add_fusion.2.place, bf16[2,384,512]{2,1,0:T(8,128)(2,1)} %get-tuple-element.111.dc_ref, bf16[2,384,512]{2,1,0:T(8,128)(2,1)} %get-tuple-element.71.refs_3_.refs_9_.ct_ref, bf16[2,2,2,384,768]{4,3,2,1,0:T(8,128)(2,1)} %get-tuple-element.112.p_ref, ...), custom_call_target="tpu_custom_call" | custom-call | tf_op jit(solution)/shard_map/attend_back/pallas_call | solution.py:365
  243.5 12.8 %attend_back.6 = (bf16[1024,384]{1,0:T(8,128)(2,1)}, f32[3,192,384]{2,1,0:T(8,128)}) custom-call(s32[3]{0:T(128)} %pad_add_fusion.3.place, bf16[2,384,512]{2,1,0:T(8,128)(2,1)} %get-tuple-element.104.dc_ref, bf16[2,384,512]{2,1,0:T(8,128)(2,1)} %get-tuple-element.70.refs_2_.refs_8_.ct_ref, bf16[2,2,2,384,768]{4,3,2,1,0:T(8,128)(2,1)} %get-tuple-element.105.p_ref, ...), custom_call_target="tpu_custom_call" | custom-call | tf_op jit(solution)/shard_map/attend_back/pallas_call | solution.py:365
  256.3 8.5 %collective-permute-done.10 = bf16[2,3,192,384]{3,2,1,0:T(8,128)(2,1)} collective-permute-done((bf16[2,3,192,384]{3,2,1,0:T(8,128)(2,1)}, bf16[2,3,192,384]{3,2,1,0:T(8,128)(2,1)}, u32[]{:S(2)}, u32[]{:S(2)}) %collective-permute-start.10) | collective-permute-done | bytes 884768 | tf_op jit(solution)/shard_map/ppermute | solution.py:517
  264.8 3.1 maximum_add_fusion.3
  267.9 3.0 maximum_add_fusion.2
  270.9 19.2 %collective-permute-done.12 = bf16[2,192,1536]{2,1,0:T(8,128)(2,1)} collective-permute-done((bf16[2,192,1536]{2,1,0:T(8,128)(2,1)}, bf16[2,192,1536]{2,1,0:T(8,128)(2,1)}, u32[]{:S(2)}, u32[]{:S(2)}) %collective-permute-start.12) | collective-permute-done | bytes 1179680 | tf_op jit(solution)/shard_map/ppermute | solution.py:517
  290.1 3.0 maximum_add_fusion.1
  293.1 20.5 %collective-permute-done.11 = bf16[2,384,768]{2,1,0:T(8,128)(2,1)} collective-permute-done((bf16[2,384,768]{2,1,0:T(8,128)(2,1)}, bf16[2,384,768]{2,1,0:T(8,128)(2,1)}, u32[]{:S(2)}, u32[]{:S(2)}) %collective-permute-start.11) | collective-permute-done | bytes 1179680 | tf_op jit(solution)/shard_map/ppermute | solution.py:517
  313.6 2.9 maximum_add_fusion
  316.5 2.3 maximum_select_fusion.2
  324.0 98.4 %psum.39 = f32[2,2,768]{2,1,0:T(2,128)} all-reduce(f32[2,2,768]{2,1,0:T(2,128)S(1)} %pad_maximum_fusion.4), channel_id=1, replica_groups=mesh['dp'=16,'head'=2] {'dp','head'}, use_global_device_ids=true, to_apply=%region_4.5 | all-reduce | flops 3072 | bytes 24576 | tf_op jit(solution)/shard_map/psum | solution.py:588
  422.4 3.5 maximum_select_fusion.1
  425.9 3.5 maximum_select_fusion
  429.4 66.6 %all-reduce.3.cloned.1.call-done = (f32[2,3,192,384]{3,2,1,0:T(8,128)}, f32[2,384,768]{2,1,0:T(8,128)}, f32[2,192,1536]{2,1,0:T(8,128)}, f32[2,768,384]{2,1,0:T(8,128)}) async-done(((f32[2,3,192,384]{3,2,1,0:T(8,128)}, f32[2,384,768]{2,1,0:T(8,128)}, f32[2,192,1536]{2,1,0:T(8,128)}, f32[2,768,384]{2,1,0:T(8,128)}), (f32[2,3,192,384]{3,2,1,0:T(8,128)}, f32[2,384,768]{2,1,0:T(8,128)}, ...) | async-done | bytes 8847376 | tf_op jit(solution)/shard_map/psum | solution.py:587
  496.0 2.9 copy.27
  (114 shorter events, 44.5 us)
Async XLA Ops:
  7.2 5.3 %copy-start.22 = (bf16[2,384,768]{2,1,0:T(8,128)(2,1)S(1)}, bf16[2,384,768]{2,1,0:T(8,128)(2,1)}, u32[]{:S(2)}) copy-start(bf16[2,384,768]{2,1,0:T(8,128)(2,1)} %param.11) | copy-start | bytes 3538948
  7.2 488.8 %all-reduce.3.cloned.1.call-start = ((), (), s32[]{:S(2)}) async-start(), calls=%async_computation | async-start | bytes 17694720 | tf_op jit(solution)/shard_map/psum | solution.py:587
  7.2 5.5 %copy-start.23 = (bf16[2,192,1536]{2,1,0:T(8,128)(2,1)S(1)}, bf16[2,192,1536]{2,1,0:T(8,128)(2,1)}, u32[]{:S(2)}) copy-start(bf16[2,192,1536]{2,1,0:T(8,128)(2,1)} %param.12) | copy-start | bytes 3538948
  9.5 5.3 %copy-start.24 = (bf16[2,768,384]{2,1,0:T(8,128)(2,1)S(1)}, bf16[2,768,384]{2,1,0:T(8,128)(2,1)}, u32[]{:S(2)}) copy-start(bf16[2,768,384]{2,1,0:T(8,128)(2,1)} %param.13) | copy-start | bytes 3538948
  9.5 14.2 %collective-permute-start = (bf16[3,192,384]{2,1,0:T(8,128)(2,1)}, bf16[3,192,384]{2,1,0:T(8,128)(2,1)}, u32[]{:S(2)}, u32[]{:S(2)}) collective-permute-start(bf16[3,192,384]{2,1,0:T(8,128)(2,1)} %get-tuple-element.140.w_ref), channel_id=1, source_target_pairs={{0,1},{1,0},{2,3},{3,2},{4,5},{5,4},{6,7},{7,6},{8,9},{9,8},{10,11... | collective-permute-start | bytes 1327112 | tf_op jit(solution)/shard_map/ppermute | solution.py:517
  12.6 26.5 %copy-start.26 = (s32[4,512]{1,0:T(4,128)S(1)}, s32[4,512]{1,0:T(4,128)}, u32[]{:S(2)}) copy-start(s32[4,512]{1,0:T(4,128)} %param.9) | copy-start | bytes 24580
  12.6 23.8 %collective-permute-start.1 = (bf16[384,768]{1,0:T(8,128)(2,1)S(1)}, bf16[384,768]{1,0:T(8,128)(2,1)}, u32[]{:S(2)}, u32[]{:S(2)}) collective-permute-start(bf16[384,768]{1,0:T(8,128)(2,1)S(1)} %get-tuple-element.138.refs_4_.refs_10_), channel_id=1, source_target_pairs={{0,1},{1,0},{2,3},{3,2},{4,5},{5,4},{6,7},{7,6},{8,9},{9,8},{10,11... | collective-permute-start | bytes 1769480 | tf_op jit(solution)/shard_map/ppermute | solution.py:517
  12.8 31.3 %copy-start.1 = (bf16[192,1536]{1,0:T(8,128)(2,1)}, bf16[192,1536]{1,0:T(8,128)(2,1)S(1)}, u32[]{:S(2)}) copy-start(bf16[192,1536]{1,0:T(8,128)(2,1)S(1)} %get-tuple-element.135.refs_5_.refs_11_) | copy-start | bytes 1769476
  12.8 31.3 %copy-start.4 = (bf16[192,1536]{1,0:T(8,128)(2,1)}, bf16[192,1536]{1,0:T(8,128)(2,1)S(1)}, u32[]{:S(2)}) copy-start(bf16[192,1536]{1,0:T(8,128)(2,1)S(1)} %get-tuple-element.136.refs_6_.refs_12_) | copy-start | bytes 1769476
  12.8 41.4 %collective-permute-start.2 = (bf16[192,1536]{1,0:T(8,128)(2,1)S(1)}, bf16[192,1536]{1,0:T(8,128)(2,1)}, u32[]{:S(2)}, u32[]{:S(2)}) collective-permute-start(bf16[192,1536]{1,0:T(8,128)(2,1)S(1)} %get-tuple-element.136.refs_6_.refs_12_), channel_id=1, source_target_pairs={{0,1},{1,0},{2,3},{3,2},{4,5},{5,4},{6,7},{7,6},{8,9},{9,8},{10,11... | collective-permute-start | bytes 1769480 | tf_op jit(solution)/shard_map/ppermute | solution.py:517
  15.0 38.6 %copy-start.2 = (bf16[768,384]{1,0:T(8,128)(2,1)}, bf16[768,384]{1,0:T(8,128)(2,1)S(1)}, u32[]{:S(2)}) copy-start(bf16[768,384]{1,0:T(8,128)(2,1)S(1)} %get-tuple-element.133.refs_7_.refs_13_) | copy-start | bytes 1769476
  15.0 38.6 %copy-start.5 = (bf16[768,384]{1,0:T(8,128)(2,1)}, bf16[768,384]{1,0:T(8,128)(2,1)S(1)}, u32[]{:S(2)}) copy-start(bf16[768,384]{1,0:T(8,128)(2,1)S(1)} %get-tuple-element.134.refs_8_.refs_14_) | copy-start | bytes 1769476
  15.0 50.8 %collective-permute-start.3 = (bf16[768,384]{1,0:T(8,128)(2,1)S(1)}, bf16[768,384]{1,0:T(8,128)(2,1)}, u32[]{:S(2)}, u32[]{:S(2)}) collective-permute-start(bf16[768,384]{1,0:T(8,128)(2,1)S(1)} %get-tuple-element.134.refs_8_.refs_14_), channel_id=1, source_target_pairs={{0,1},{1,0},{2,3},{3,2},{4,5},{5,4},{6,7},{7,6},{8,9},{9,8},{10,11... | collective-permute-start | bytes 1769480 | tf_op jit(solution)/shard_map/ppermute | solution.py:517
  15.1 103.5 %collective-permute-start.5 = (bf16[384,768]{1,0:T(8,128)(2,1)S(1)}, bf16[384,768]{1,0:T(8,128)(2,1)}, u32[]{:S(2)}, u32[]{:S(2)}) collective-permute-start(bf16[384,768]{1,0:T(8,128)(2,1)S(1)} %get-tuple-element.137.refs_3_.refs_9_), channel_id=1, source_target_pairs={{0,1},{1,0},{2,3},{3,2},{4,5},{5,4},{6,7},{7,6},{8,9},{9,8},{10,11... | collective-permute-start | bytes 1769480 | tf_op jit(solution)/shard_map/ppermute | solution.py:517
  23.8 94.8 %collective-permute-start.6 = (bf16[192,1536]{1,0:T(8,128)(2,1)S(1)}, bf16[192,1536]{1,0:T(8,128)(2,1)}, u32[]{:S(2)}, u32[]{:S(2)}) collective-permute-start(bf16[192,1536]{1,0:T(8,128)(2,1)S(1)} %get-tuple-element.135.refs_5_.refs_11_), channel_id=1, source_target_pairs={{0,1},{1,0},{2,3},{3,2},{4,5},{5,4},{6,7},{7,6},{8,9},{9,8},{10,11... | collective-permute-start | bytes 1769480 | tf_op jit(solution)/shard_map/ppermute | solution.py:517
  36.4 82.2 %collective-permute-start.7 = (bf16[768,384]{1,0:T(8,128)(2,1)S(1)}, bf16[768,384]{1,0:T(8,128)(2,1)S(1)}, u32[]{:S(2)}, u32[]{:S(2)}) collective-permute-start(bf16[768,384]{1,0:T(8,128)(2,1)S(1)} %get-tuple-element.133.refs_7_.refs_13_), channel_id=1, source_target_pairs={{0,1},{1,0},{2,3},{3,2},{4,5},{5,4},{6,7},{7,6},{8,9},{9,8},{10,11... | collective-permute-start | bytes 1769480 | tf_op jit(solution)/shard_map/ppermute | solution.py:517
  44.1 10.1 %copy-start.9 = (bf16[3,192,384]{2,1,0:T(8,128)(2,1)S(1)}, bf16[3,192,384]{2,1,0:T(8,128)(2,1)}, u32[]{:S(2)}) copy-start(bf16[3,192,384]{2,1,0:T(8,128)(2,1)} %get-tuple-element.139.w_ref) | copy-start | bytes 1327108
  54.2 54.0 %collective-permute-start.4 = (bf16[3,192,384]{2,1,0:T(8,128)(2,1)S(1)}, bf16[3,192,384]{2,1,0:T(8,128)(2,1)S(1)}, u32[]{:S(2)}, u32[]{:S(2)}) collective-permute-start(bf16[3,192,384]{2,1,0:T(8,128)(2,1)S(1)} %copy-done.9), channel_id=1, source_target_pairs={{0,1},{1,0},{2,3},{3,2},{4,5},{5,4},{6,7},{7,6},{8,9},{9,8},{10,11... | collective-permute-start | bytes 1327112 | tf_op jit(solution)/shard_map/ppermute | solution.py:517
  191.2 24.2 %copy-start.18 = (f32[2,768,384]{2,1,0:T(8,128)S(1)}, f32[2,768,384]{2,1,0:T(8,128)}, u32[]{:S(2)}) copy-start(f32[2,768,384]{2,1,0:T(8,128)} %get-tuple-element.126) | copy-start | bytes 7077892
  216.6 51.2 %collective-permute-start.13 = (bf16[2,768,384]{2,1,0:T(8,128)(2,1)}, bf16[2,768,384]{2,1,0:T(8,128)(2,1)}, u32[]{:S(2)}, u32[]{:S(2)}) collective-permute-start(bf16[2,768,384]{2,1,0:T(8,128)(2,1)} %pad_maximum_fusion.2), channel_id=1, source_target_pairs={{0,1},{1,0},{2,3},{3,2},{4,5},{5,4},{6,7},{7,6},{8,9},{9,8},{10,11... | collective-permute-start | bytes 3538952 | tf_op jit(solution)/shard_map/ppermute | solution.py:517
  218.3 14.6 %copy-start.25 = (f32[3,192,384]{2,1,0:T(8,128)S(1)}, f32[3,192,384]{2,1,0:T(8,128)}, u32[]{:S(2)}) copy-start(f32[3,192,384]{2,1,0:T(8,128)} %get-tuple-element.120) | copy-start | bytes 2654212
  233.9 30.9 %collective-permute-start.10 = (bf16[2,3,192,384]{3,2,1,0:T(8,128)(2,1)}, bf16[2,3,192,384]{3,2,1,0:T(8,128)(2,1)}, u32[]{:S(2)}, u32[]{:S(2)}) collective-permute-start(bf16[2,3,192,384]{3,2,1,0:T(8,128)(2,1)} %pad_maximum_fusion.3), channel_id=1, source_target_pairs={{0,1},{1,0},{2,3},{3,2},{4,5},{5,4},{6,7},{7,6},{8,9},{9,8},{10,11... | collective-permute-start | bytes 2654216 | tf_op jit(solution)/shard_map/ppermute | solution.py:517
  234.3 3.0 copy-start.19
  236.2 53.9 %collective-permute-start.12 = (bf16[2,192,1536]{2,1,0:T(8,128)(2,1)}, bf16[2,192,1536]{2,1,0:T(8,128)(2,1)}, u32[]{:S(2)}, u32[]{:S(2)}) collective-permute-start(bf16[2,192,1536]{2,1,0:T(8,128)(2,1)} %pad_maximum_fusion.1), channel_id=1, source_target_pairs={{0,1},{1,0},{2,3},{3,2},{4,5},{5,4},{6,7},{7,6},{8,9},{9,8},{10,11... | collective-permute-start | bytes 3538952 | tf_op jit(solution)/shard_map/ppermute | solution.py:517
  238.5 75.1 %collective-permute-start.11 = (bf16[2,384,768]{2,1,0:T(8,128)(2,1)}, bf16[2,384,768]{2,1,0:T(8,128)(2,1)}, u32[]{:S(2)}, u32[]{:S(2)}) collective-permute-start(bf16[2,384,768]{2,1,0:T(8,128)(2,1)} %pad_maximum_fusion), channel_id=1, source_target_pairs={{0,1},{1,0},{2,3},{3,2},{4,5},{5,4},{6,7},{7,6},{8,9},{9,8},{10,11... | collective-permute-start | bytes 3538952 | tf_op jit(solution)/shard_map/ppermute | solution.py:517
  256.3 11.6 %copy-start.7 = (f32[1,768,384]{2,1,0:T(8,128)S(1)}, f32[1,768,384]{2,1,0:T(8,128)}, u32[]{:S(2)}) copy-start(f32[1,768,384]{2,1,0:T(8,128)} %slice.104) | copy-start | bytes 3538948
  256.3 11.6 %copy-start.8 = (f32[1,768,384]{2,1,0:T(8,128)S(1)}, f32[1,768,384]{2,1,0:T(8,128)}, u32[]{:S(2)}) copy-start(f32[1,768,384]{2,1,0:T(8,128)} %slice.105) | copy-start | bytes 3538948
  267.9 22.2 %copy-start.6 = (f32[1,192,1536]{2,1,0:T(8,128)S(1)}, f32[1,192,1536]{2,1,0:T(8,128)}, u32[]{:S(2)}) copy-start(f32[1,192,1536]{2,1,0:T(8,128)} %slice.101) | copy-start | bytes 3538948
  316.5 3.8 copy-start.15
  318.9 103.5 %collective-permute-start.9 = (bf16[1024,768]{1,0:T(8,128)(2,1)S(1)}, bf16[1024,768]{1,0:T(8,128)(2,1)}, u32[]{:S(2)}, u32[]{:S(2)}) collective-permute-start(bf16[1024,768]{1,0:T(8,128)(2,1)S(1)} %maximum_select_fusion.2), channel_id=1, source_target_pairs={{0,1},{1,0},{2,3},{3,2},{4,5},{5,4},{6,7},{7,6},{8,9},{9,8},{10,11... | collective-permute-start | bytes 4718600 | tf_op jit(solution)/shard_map/ppermute | solution.py:517
  320.3 105.6 %collective-permute-start.8 = (bf16[1024,768]{1,0:T(8,128)(2,1)S(1)}, bf16[1024,768]{1,0:T(8,128)(2,1)}, u32[]{:S(2)}, u32[]{:S(2)}) collective-permute-start(bf16[1024,768]{1,0:T(8,128)(2,1)S(1)} %copy-done.15), channel_id=1, source_target_pairs={{0,1},{1,0},{2,3},{3,2},{4,5},{5,4},{6,7},{7,6},{8,9},{9,8},{10,11... | collective-permute-start | bytes 4718600 | tf_op jit(solution)/shard_map/ppermute | solution.py:517
  496.0 3.0 copy-start.13
  (10 other events, 21.6 us)
Sparse Core Ops, SparseCore 0:
  316.7 179.2 all-reduce.2

commit v2 on v1

--- a/solution.py
+++ b/solution.py
@@ -9,6 +9,8 @@
 HEAD_DIM = 64
 QUERY_TILE = 256
 REACH = 128
+
+SELF, OTHER, OFFSET, CORE, ROW = range(5)
 
 epsilon = 1e-12
 masked_score = -1e30
@@ -57,9 +59,11 @@
     return jnp.concatenate(pieces, axis=0) if len(pieces) > 1 else middle
 
 
-def attend_kernel(
-    place, x_ref, w_ref, segq_ref, segk_ref, xt_ref, qt_ref, kt_ref, v_ref, p_ref, ct_ref
-):
+def across(row):
+    return jnp.broadcast_to(row, (128, row.shape[1])).T
+
+
+def attend_kernel(place, x_ref, w_ref, seg_ref, xt_ref, qt_ref, kt_ref, v_ref, p_ref, ct_ref):
     seq_len, channels = x_ref.shape
     width = w_ref.shape[1]
     window = QUERY_TILE + REACH
@@ -68,8 +72,8 @@
     x = x_ref[...]
     xt = x.T
     xt_ref[0] = xt
-    segq = segq_ref[0]
-    segk = segk_ref[0]
+    segq = seg_ref[pl.ds(place[OFFSET] + pl.program_id(0), 1), :].astype(f32)
+    segk = across(segq)
     masks = {}
     for tile in range(tiles):
         start = key_start(tile, seq_len)
@@ -120,6 +124,7 @@
 
 def attend_back_kernel(
     last,
+    aliased,
     place,
     dc_ref,
     ct_ref,
@@ -130,10 +135,15 @@
     xt_ref,
     w_ref,
     dz_ref,
-    dx_ref,
-    grad_ref,
-    ds_ref,
+    *refs,
 ):
+    if last:
+        later_ref, gain0_ref, gain1_ref, *refs = refs
+        if aliased:
+            _, *refs = refs
+        dx_ref, full_ref, keep_ref, send_ref, grad_ref, ds_ref = refs
+    else:
+        dx_ref, grad_ref, ds_ref = refs
     channels, seq_len = xt_ref.shape[1:]
     width = w_ref.shape[1]
     window = QUERY_TILE + REACH
@@ -206,10 +216,28 @@
             grad_ref[s] += joined[s]
 
     d_input = jnp.concatenate(d_inputs, axis=0)
-    if last:
-        dx_ref[...] = d_input.astype(bf16).T
-    else:
+    if not last:
         dx_ref[0] = d_input
+        return
+    tok = d_input.astype(bf16).T
+    dx_ref[...] = tok
+    full_ref[...] = tok
+
+    @pl.when(step == pl.num_programs(0) - 1)
+    def _():
+        piece = width // 4
+        gain_rows = jnp.concatenate([gain0_ref[...], gain1_ref[...]], axis=0).astype(bf16)
+        gain_rows = jnp.concatenate([gain_rows[:, :channels], gain_rows[:, channels:]], axis=0)
+        for c, out_ref in enumerate((keep_ref, send_ref)):
+            for y in range(2):
+                at = ((place[CORE] ^ c) * 2 + (place[ROW] ^ y)) * piece
+                rows = pl.ds(pl.multiple_of(at, piece), piece)
+                for layer, source in enumerate((grad_ref, later_ref)):
+                    for s in range(3):
+                        out_ref[y, pl.ds((layer * 3 + s) * piece, piece)] = source[
+                            s, rows
+                        ].astype(bf16)
+                out_ref[y, pl.ds(6 * piece, 16)] = gain_rows
 
 
 def join_windows(pieces, seq_len):
@@ -240,112 +268,216 @@
     return inverse * (scaled - feature_mean(scaled) - normal * feature_mean(scaled * normal))
 
 
-def ffn_kernel(first_layer, place, *refs):
-    if first_layer:
+def gather_far(place, x_ref, c_ref, scr):
+    scr[place[CORE]] = x_ref[...]
+    scr[1 - place[CORE]] = c_ref[...]
+
+
+def out_rows(pack):
+    rows = pack[:, 0]
+    return rows.reshape(2 * rows.shape[1], rows.shape[2])
+
+
+def inner_rows(pack, group):
+    return pack[group, 1]
+
+
+def outer_rows(pack, group, width):
+    rows = pack[:, 2]
+    rows = rows.reshape(2 * rows.shape[1], rows.shape[2])
+    half = rows.shape[1] // 2
+    at = group * width
+    return jnp.concatenate([rows[:, at : at + width], rows[:, half + at : half + at + width]], axis=0)
+
+
+def spread_gains(gains_ref, layer, g_scr):
+    for i in range(2):
+        g_scr[i] = across(gains_ref[layer, i : i + 1, :])
+
+
+def wide_gain(g_scr, i, seq_len):
+    return jnp.concatenate([g_scr[i]] * (seq_len // 128), axis=1)
+
+
+def ffn_kernel(layer, more, place, *refs):
+    if layer == 0:
         xt0, xt1, *refs = refs
     else:
         x_ref, *refs = refs
-    (ct0, ct1, ow0, ow1, iw0, iw1, uw0, uw1, gains, *refs) = refs
-    (n1_ref, r1_ref, act_ref, slope_ref, n2_ref, r2_ref, tok_ref, *refs) = refs
-    if first_layer:
-        next_ref, *refs = refs
-    z_scr, fb_scr = refs
+    (ct0, ct1, near_ref, farx_ref, farc_ref, gains_ref, *refs) = refs
+    (n1_ref, r1_ref, act_ref, slope_ref, n2_ref, r2_ref, tok_ref, next_ref, *refs) = refs
+    z_scr, fb_scr, far_scr, g_scr = refs
     half, seq_len = z_scr.shape[1:]
     wide = 2 * half
-    width = iw0.shape[0]
-    own = place[0]
-    sides = (own, 1 - own)
-    attention = mm(ow0[...], ct0[0], TN) + mm(ow1[...], ct1[0], TN)
+    width = half // 2
+    sides = (place[SELF], place[OTHER])
+
+    @pl.when(pl.program_id(0) == 0)
+    def _():
+        gather_far(place, farx_ref, farc_ref, far_scr)
+        spread_gains(gains_ref, layer, g_scr)
+
+    packs = (near_ref, far_scr)
+    attention = mm(out_rows(packs[0]), ct0[0], TN) + mm(out_rows(packs[1]), ct1[0], TN)
     z_scr[...] = attention.reshape(2, half, seq_len)
-    if first_layer:
+    if layer == 0:
         z_scr[sides[0]] += xt0[0].astype(f32)
         z_scr[sides[1]] += xt1[0].astype(f32)
         before = z_scr[...].reshape(wide, seq_len)
     else:
         before = (z_scr[...] + x_ref[0]).reshape(wide, seq_len)
     normal, inverse = normalize(before)
-    first = normal * gains[0]
+    first = normal * wide_gain(g_scr, 0, seq_len)
     n1_ref[0] = normal.reshape(2, half, seq_len)
     r1_ref[0] = inverse
     z_scr[...] = first.reshape(2, half, seq_len)
     fb_scr[...] = first.astype(bf16).reshape(2, half, seq_len)
-    for j, (iw, uw) in enumerate(((iw0, uw0), (iw1, uw1))):
-        hidden = iw.shape[1] // (half // width)
+    for j, pack in enumerate(packs):
         for group in range(half // width):
             span = slice(group * width, (group + 1) * width)
-            pre = mm(iw[:, group * hidden : (group + 1) * hidden], fb_scr[sides[j], span], TN)
+            pre = mm(inner_rows(pack, group), fb_scr[sides[j], span], TN)
             below = 0.5 + 0.5 * lax.erf(pre * 0.7071067811865476)
             act = (pre * below).astype(bf16)
             slope = below + pre * (jnp.exp(-0.5 * pre * pre) * 0.3989422804014327)
             act_ref[0, j, group] = act
             slope_ref[0, j, group] = slope.astype(bf16)
-            z_scr[sides[j], span] += mm(uw[:, span], act, TN)
+            z_scr[sides[j], span] += mm(outer_rows(pack, group, width), act, TN)
     normal, inverse = normalize(z_scr[...].reshape(wide, seq_len))
     n2_ref[0] = normal.reshape(2, half, seq_len)
     r2_ref[0] = inverse
-    output = normal * gains[1]
-    if first_layer:
+    output = normal * wide_gain(g_scr, 1, seq_len)
+    tok = output.astype(bf16).T
+    tok_ref[...] = tok
+    if more:
         next_ref[0] = output.reshape(2, half, seq_len)
-    tok_ref[...] = output.astype(bf16).T
-
-
-def ffn_back_kernel(last_layer, place, *refs):
-    if last_layer:
+    else:
+        next_ref[...] = tok
+
+
+def ffn_back_kernel(layer, more, place, *refs):
+    if more:
+        g0, g1, *refs = refs
+    else:
         cot_ref, *refs = refs
-    else:
-        g0, g1, *refs = refs
     (n2_ref, r2_ref, act_ref, slope_ref, n1_ref, r1_ref, ct0, ct1, *refs) = refs
-    (ow0, ow1, iw0, iw1, uw0, uw1, gains, *refs) = refs
-    (dz1_ref, dc0, dc1, outer_ref, inner_ref, out_ref, gain_ref, d_scr, b_scr, f_scr) = refs
+    (near_ref, farx_ref, farc_ref, gains_ref, *refs) = refs
+    (dz1_ref, dc0, dc1, keep_ref, send_ref, gain_ref, *refs) = refs
+    d_scr, b_scr, f_scr, far_scr, g_scr, acc, gain_acc = refs
     half, seq_len = d_scr.shape[1:]
     wide = 2 * half
-    width = iw0.shape[0]
-    own = place[0]
-    sides = (own, 1 - own)
+    width = half // 2
+    sides = (place[SELF], place[OTHER])
     step = pl.program_id(0)
 
     @pl.when(step == 0)
     def _():
-        outer_ref[...] = jnp.zeros_like(outer_ref)
-        inner_ref[...] = jnp.zeros_like(inner_ref)
-        out_ref[...] = jnp.zeros_like(out_ref)
-        gain_ref[...] = jnp.zeros_like(gain_ref)
-
-    if last_layer:
-        g = cot_ref[...].T.astype(f32)
-    else:
+        gather_far(place, farx_ref, farc_ref, far_scr)
+        spread_gains(gains_ref, layer, g_scr)
+        acc[...] = jnp.zeros_like(acc)
+        gain_acc[...] = jnp.zeros_like(gain_acc)
+
+    packs = (near_ref, far_scr)
+    if more:
         d_scr[sides[0]] = g0[0]
         d_scr[sides[1]] = g1[0]
         g = d_scr[...].reshape(wide, seq_len)
+    else:
+        g = cot_ref[...].T.astype(f32)
     normal = n2_ref[0].reshape(wide, seq_len)
-    gain_ref[1] += jnp.sum(g * normal, axis=1, keepdims=True)
-    d_second = normalize_back(g, gains[1], normal, r2_ref[0])
+    gain_acc[1] += lane_sum(g * normal)
+    d_second = normalize_back(g, wide_gain(g_scr, 1, seq_len), normal, r2_ref[0])
     d_scr[...] = d_second.reshape(2, half, seq_len)
     b_scr[...] = d_second.astype(bf16).reshape(2, half, seq_len)
     normal = n1_ref[0].reshape(wide, seq_len)
-    f_scr[...] = (normal * gains[0]).astype(bf16).reshape(2, half, seq_len)
-    for j, (iw, uw) in enumerate(((iw0, uw0), (iw1, uw1))):
-        hidden = iw.shape[1] // (half // width)
+    gain1 = wide_gain(g_scr, 0, seq_len)
+    f_scr[...] = (normal * gain1).astype(bf16).reshape(2, half, seq_len)
+    for j, pack in enumerate(packs):
         outers = []
         for group in range(half // width):
             span = slice(group * width, (group + 1) * width)
-            units = slice(group * hidden, (group + 1) * hidden)
             d_branch = b_scr[sides[j], span]
             first = f_scr[sides[j], span]
             outers.append(mm(act_ref[0, j, group], d_branch, NT))
-            d_act = mm(uw[:, span], d_branch, NN)
+            d_act = mm(outer_rows(pack, group, width), d_branch, NN)
             d_pre = (d_act * slope_ref[0, j, group].astype(f32)).astype(bf16)
-            inner_ref[j, :, units] += mm(first, d_pre, NT)
-            d_scr[sides[j], span] += mm(iw[:, units], d_pre, NN)
-        outer_ref[j] += jnp.concatenate(outers, axis=1)
+            acc[j, 1, span] += mm(first, d_pre, NT)
+            d_scr[sides[j], span] += mm(inner_rows(pack, group), d_pre, NN)
+        acc[j, 2] += jnp.concatenate(
+            [o[:half] for o in outers] + [o[half:] for o in outers], axis=1
+        )
     d_first = d_scr[...].reshape(wide, seq_len)
-    gain_ref[0] += jnp.sum(d_first * normal, axis=1, keepdims=True)
-    d_before = normalize_back(d_first, gains[0], normal, r1_ref[0])
+    gain_acc[0] += lane_sum(d_first * normal)
+    d_before = normalize_back(d_first, gain1, normal, r1_ref[0])
     dz1_ref[0] = d_before.reshape(2, half, seq_len)
     d_attention = d_before.astype(bf16)
-    for j, (ow, ct, dc) in enumerate(((ow0, ct0, dc0), (ow1, ct1, dc1))):
-        out_ref[j] += mm(ct[0], d_attention, NT)
-        dc[0] = mm(ow[...], d_attention, NN).astype(bf16)
+    for j, (pack, ct, dc) in enumerate(zip(packs, (ct0, ct1), (dc0, dc1))):
+        acc[j, 0] += mm(ct[0], d_attention, NT)
+        dc[0] = mm(out_rows(pack), d_attention, NN).astype(bf16)
+
+    @pl.when(step == pl.num_programs(0) - 1)
+    def _():
+        piece = half // 8
+        for c, out_ref in enumerate((keep_ref, send_ref)):
+            for s in range(2):
+                for j in range(2):
+                    for y in range(2):
+                        at = ((s * 2 + (place[CORE] ^ c)) * 2 + (place[ROW] ^ y)) * piece
+                        rows = pl.ds(pl.multiple_of(at, piece), piece)
+                        first, second = (j, y) if s == 0 else (y, j)
+                        for k in range(3):
+                            out_ref[s, first, second, k] = acc[j, k, rows].astype(bf16)
+        sums = [jnp.sum(gain_acc[i], axis=1, keepdims=True) for i in range(2)]
+        lane = lax.broadcasted_iota(jnp.int32, (wide, 128), 1)
+        gain_ref[...] = jnp.where(lane == 0, sums[0], sums[1]).T[:4]
+
+
+def lane_sum(values):
+    chunks = [values[:, at : at + 128] for at in range(0, values.shape[1], 128)]
+    return functools.reduce(jnp.add, chunks)
+
+
+def finish_kernel(place, *refs):
+    ffn_parts = [[refs[(layer * 2 + s) * 3 : (layer * 2 + s) * 3 + 3] for s in range(2)] for layer in range(2)]
+    qkv_parts = refs[12:15]
+    qkv_ref, out_ref, inner_ref, outer_ref, gain_ref = refs[15:]
+
+    def pieces(parts):
+        mine, row, core = parts
+        yield 0, 0, mine[...]
+        yield 0, 1, row[...]
+        yield 1, 0, core[0]
+        yield 1, 1, core[1]
+
+    half = out_ref.shape[1]
+    wide = out_ref.shape[2]
+    piece = half // 8
+    for layer in range(2):
+        for s in range(2):
+            for c, y, value in pieces(ffn_parts[layer][s]):
+                value = value.astype(f32)
+                at = ((place[CORE] ^ c) * 2 + (place[ROW] ^ y)) * piece
+                rows = pl.ds(pl.multiple_of(at, piece), piece)
+                low = pl.ds(pl.multiple_of(s * half // 2 + at, piece), piece)
+                high = pl.ds(pl.multiple_of(half + s * half // 2 + at, piece), piece)
+                out_ref[layer, low, :] = value[0]
+                inner_ref[layer, rows, s * wide : (s + 1) * wide] = value[1]
+                outer_ref[layer, low, :] = value[2][:, :half]
+                outer_ref[layer, high, :] = value[2][:, half:]
+    piece = qkv_ref.shape[2] // 4
+    for c, y, value in pieces(qkv_parts):
+        at = ((place[CORE] ^ c) * 2 + (place[ROW] ^ y)) * piece
+        rows = pl.ds(pl.multiple_of(at, piece), piece)
+        for layer in range(2):
+            for s in range(3):
+                index = (layer * 3 + s) * piece
+                qkv_ref[layer, s, rows, :] = value[index : index + piece].astype(f32)
+        if c == 0 and y == 0:
+            gains = value[6 * piece : 6 * piece + 16].astype(f32)
+            for layer in range(2):
+                for i in range(2):
+                    at = layer * 4 + i
+                    gain_ref[layer, i : i + 1, :half] = gains[at : at + 1]
+                    gain_ref[layer, i : i + 1, half:] = gains[8 + at : 9 + at]
 
 
 def whole(shape):
@@ -361,7 +493,7 @@
     return jax.ShapeDtypeStruct(shape, dtype)
 
 
-def call(kernel, rows, place, operands, in_specs, outs, out_specs, scratch, name):
+def call(kernel, rows, place, operands, in_specs, outs, out_specs, scratch, name, us, aliases=None):
     return pl.pallas_call(
         kernel,
         out_shape=outs,
@@ -373,14 +505,17 @@
             scratch_shapes=scratch,
         ),
         compiler_params=pltpu.CompilerParams(vmem_limit_bytes=60 * 2**20),
+        cost_estimate=pl.CostEstimate(
+            flops=int(us * 1.1e9), bytes_accessed=int(us * 1e6), transcendentals=0
+        ),
+        input_output_aliases=aliases or {},
         name=name,
     )(place, *operands)
 
 
-def attend(x_tok, w, segq, segk, place, rows):
-    seq_len = segq.shape[-1]
-    channels = w.shape[-1]
-    width = w.shape[1]
+def attend(x_tok, w, w_layer, segments, place, rows, j, from_input):
+    row_total, seq_len = segments.shape
+    width, channels = w.shape[-2:]
     heads = width // HEAD_DIM
     groups = channels // width
     tiles = seq_len // QUERY_TILE
@@ -393,59 +528,89 @@
         struct((rows, groups, tiles, window, heads * QUERY_TILE), bf16),
         struct((rows, channels, seq_len), bf16),
     ]
+    if from_input:
+        x_spec = pl.BlockSpec((seq_len, channels), lambda r, place: (place[OFFSET] + r, place[j]))
+    else:
+        x_spec = pl.BlockSpec((seq_len, channels), lambda r, place: (r, place[j]))
     return call(
         attend_kernel,
         rows,
         place,
-        (x_tok, w, segq, segk),
-        [
-            pl.BlockSpec((seq_len, channels), lambda r, place: (place[0] + r, place[1])),
-            whole(w.shape),
-            pl.BlockSpec((1, 1, seq_len), lambda r, place: (place[2] + r, 0, 0)),
-            pl.BlockSpec((1, seq_len, 1), lambda r, place: (place[2] + r, 0, 0)),
-        ],
+        (x_tok, w, segments),
+        [x_spec, layer_block(w.shape, w_layer), whole(segments.shape)],
         outs,
         [per_row(o.shape) for o in outs],
         [],
         "attend",
-    )
-
-
-def attend_back(d_context, saved, w, d_before, place, rows, last):
+        4.7 * rows,
+    )
+
+
+def layer_block(shape, layer):
+    rest = (0,) * (len(shape) - 1)
+    return pl.BlockSpec((None,) + tuple(shape[1:]), lambda r, place: (layer,) + rest)
+
+
+def attend_back(d_context, saved, w, w_layer, d_before, place, rows, j, extra):
     xt, qt, kt, values, probs, ct = saved
     channels, seq_len = xt.shape[1:]
     window = QUERY_TILE + REACH
-    heads = w.shape[1] // HEAD_DIM
-    if last:
-        dx = struct((rows * seq_len, channels), bf16)
-        dx_spec = pl.BlockSpec((seq_len, channels), lambda r, place: (r, 0))
-    else:
+    width = w.shape[-2]
+    heads = width // HEAD_DIM
+    operands = (d_context, ct, probs, qt, kt, values, xt)
+    in_specs = [per_row(o.shape) for o in operands] + [
+        layer_block(w.shape, w_layer),
+        pl.BlockSpec((1, 1, channels, seq_len), lambda r, place: (r, place[j], 0, 0)),
+    ]
+    operands += (w, d_before)
+    scratch = [pltpu.VMEM((window, heads * QUERY_TILE), bf16)]
+    aliases = {}
+    if extra is None:
         dx = struct((rows, channels, seq_len), f32)
-        dx_spec = per_row(dx.shape)
-    operands = (d_context, ct, probs, qt, kt, values, xt)
+        outs = [dx, struct(w.shape[1:], f32)]
+        out_specs = [per_row(dx.shape), whole(w.shape[1:])]
+    else:
+        later, gain0, gain1, full = extra
+        operands += (later, gain0, gain1)
+        in_specs += [whole(o.shape) for o in (later, gain0, gain1)]
+        if full is not None:
+            aliases = {len(operands) + 1: 1}
+            operands += (full,)
+            in_specs.append(pl.BlockSpec(memory_space=pl.ANY))
+        piece = struct((2, 6 * (width // 4) + 16, channels), bf16)
+        outs = [
+            struct((rows * seq_len, channels), bf16),
+            struct((2 * rows * seq_len, 2 * channels), bf16),
+            piece,
+            piece,
+        ]
+        out_specs = [
+            pl.BlockSpec((seq_len, channels), lambda r, place: (r, 0)),
+            pl.BlockSpec((seq_len, channels), lambda r, place: (place[OFFSET] + r, place[j])),
+            whole(piece.shape),
+            whole(piece.shape),
+        ]
+        scratch = [pltpu.VMEM(w.shape[1:], f32)] + scratch
     return call(
-        functools.partial(attend_back_kernel, last),
+        functools.partial(attend_back_kernel, extra is not None, bool(aliases)),
         rows,
         place,
-        operands + (w, d_before),
-        [per_row(o.shape) for o in operands]
-        + [
-            whole(w.shape),
-            pl.BlockSpec((1, 1, channels, seq_len), lambda r, place: (r, place[1], 0, 0)),
-        ],
-        [dx, struct(w.shape, f32)],
-        [dx_spec, whole(w.shape)],
-        [pltpu.VMEM((window, heads * QUERY_TILE), bf16)],
+        operands,
+        in_specs,
+        outs,
+        out_specs,
+        scratch,
         "attend_back",
-    )
-
-
-def ffn(x_parts, contexts, weights, gains, place, rows, first_layer):
+        6.5 * rows,
+        aliases,
+    )
+
+
+def ffn(x_parts, contexts, weights, gains, place, rows, layer, more):
     half, seq_len = contexts[0].shape[1:]
-    hidden = weights[2].shape[1] * 2 // (2 * (half // weights[2].shape[0]))
-    groups = half // weights[2].shape[0]
     stream = (rows, 2, half, seq_len)
-    acts = (rows, 2, groups, hidden, seq_len)
+    acts = (rows, 2, 2, 2 * half, seq_len)
+    tok = (rows * seq_len, 2 * half)
     outs = [
         struct(stream, f32),
         struct((rows, 1, seq_len), f32),
@@ -453,15 +618,20 @@
         struct(acts, bf16),
         struct(stream, f32),
         struct((rows, 1, seq_len), f32),
-        struct((rows * seq_len, 2 * half), bf16),
+        struct(tok, bf16),
     ]
     out_specs = [per_row(o.shape) for o in outs]
     out_specs[-1] = pl.BlockSpec((seq_len, 2 * half), lambda r, place: (r, 0))
-    if first_layer:
+    if more:
         outs.append(struct(stream, f32))
         out_specs.append(per_row(stream))
+    else:
+        outs.append(struct((2 * rows * seq_len, 2 * half), bf16))
+        out_specs.append(
+            pl.BlockSpec((seq_len, 2 * half), lambda r, place: (place[OFFSET] + r, 0))
+        )
     return call(
-        functools.partial(ffn_kernel, first_layer),
+        functools.partial(ffn_kernel, layer, more),
         rows,
         place,
         tuple(x_parts) + tuple(contexts) + tuple(weights) + (gains,),
@@ -471,30 +641,36 @@
         + [whole(gains.shape)],
         outs,
         out_specs,
-        [pltpu.VMEM((2, half, seq_len), f32), pltpu.VMEM((2, half, seq_len), bf16)],
+        [
+            pltpu.VMEM((2, half, seq_len), f32),
+            pltpu.VMEM((2, half, seq_len), bf16),
+            pltpu.VMEM(weights[0].shape, bf16),
+            pltpu.VMEM((2, 2 * half, 128), f32),
+        ],
         "ffn",
-    )
-
-
-def ffn_back(g_parts, saved, contexts, weights, gains, place, rows, last_layer):
+        10 * rows,
+    )
+
+
+def ffn_back(g_parts, saved, contexts, weights, gains, place, rows, layer, more):
     half, seq_len = contexts[0].shape[1:]
-    if last_layer:
-        g_specs = [pl.BlockSpec((seq_len, 2 * half), lambda r, place: (place[1] + r, 0))]
-    else:
+    if more:
         g_specs = [per_row(o.shape) for o in g_parts]
-    stream = (rows, 2, half, seq_len)
-    ow, iw, uw = weights[0], weights[2], weights[4]
-    grad_shapes = [(2,) + uw.shape, (2,) + iw.shape, (2,) + ow.shape, gains.shape]
+    else:
+        g_specs = [pl.BlockSpec((seq_len, 2 * half), lambda r, place: (place[OFFSET] + r, 0))]
+    piece = struct((2, 2, 2, 3, half // 8, 2 * half), bf16)
     outs = [
-        struct(stream, f32),
+        struct((rows, 2, half, seq_len), f32),
         struct(contexts[0].shape, bf16),
         struct(contexts[0].shape, bf16),
+        piece,
+        piece,
+        struct((4, 2 * half), f32),
     ]
-    out_specs = [per_row(o.shape) for o in outs] + [whole(s) for s in grad_shapes]
-    outs += [struct(s, f32) for s in grad_shapes]
+    out_specs = [per_row(o.shape) for o in outs[:3]] + [whole(o.shape) for o in outs[3:]]
     operands = tuple(saved) + tuple(contexts)
     return call(
-        functools.partial(ffn_back_kernel, last_layer),
+        functools.partial(ffn_back_kernel, layer, more),
         rows,
         place,
         tuple(g_parts) + operands + tuple(weights) + (gains,),
@@ -508,91 +684,190 @@
             pltpu.VMEM((2, half, seq_len), f32),
             pltpu.VMEM((2, half, seq_len), bf16),
             pltpu.VMEM((2, half, seq_len), bf16),
+            pltpu.VMEM(weights[0].shape, bf16),
+            pltpu.VMEM((2, 2 * half, 128), f32),
+            pltpu.VMEM((2, 3, half, 2 * half), f32),
+            pltpu.VMEM((2, 2 * half, 128), f32),
         ],
         "ffn_back",
+        11.5 * rows,
+    )
+
+
+def finish(ffn_parts, qkv_parts, place, width):
+    operands = []
+    for layer in ffn_parts:
+        for parts in layer:
+            operands += parts
+    operands += qkv_parts
+    half = qkv_parts[0].shape[-1]
+    layers = len(ffn_parts)
+    outs = [
+        struct((layers, 3, width, half), f32),
+        struct((layers, half, 2 * half), f32),
+        struct((layers, width, 4 * half), f32),
+        struct((layers, 2 * half, half), f32),
+        struct((layers, 2, 2 * half), f32),
+    ]
+    return call(
+        finish_kernel,
+        1,
+        place,
+        operands,
+        [whole(o.shape) for o in operands],
+        outs,
+        [whole(o.shape) for o in outs],
+        [],
+        "finish",
+        6,
     )
 
 
 def swap(values):
     return lax.ppermute(values, "head", [(0, 1), (1, 0)])
+
+
+def trade(values, stride):
+    count = lax.axis_size("dp")
+    return lax.ppermute(values, "dp", [(a, a ^ stride) for a in range(count)])
+
+
+def add(left, right):
+    return (left.astype(f32) + right.astype(f32)).astype(bf16)
+
+
+def far_strides():
+    count = lax.axis_size("dp")
+    strides = []
+    stride = 4
+    while stride < count:
+        strides.append(stride)
+        stride *= 2
+    return strides
+
+
+def pack_weights(out_w, inner_w, outer_w):
+    half = out_w.shape[0]
+    wide = out_w.shape[1]
+    inner = jnp.stack([inner_w[:, :wide], inner_w[:, wide:]])
+    out = out_w.reshape(2, half // 2, wide)
+    outer = jnp.concatenate([outer_w[:half], outer_w[half:]], axis=1).reshape(2, half // 2, wide)
+    return jnp.stack([out, inner, outer], axis=1)
+
+
+def spread_out(total):
+    row = trade(total, 2)
+    return [total, row, trade(jnp.stack([total, row]), 1)]
 
 
 def shards(
     tokens, segments, qkv_weight, out_weight, inner_weight, outer_weight, norm_gains, cotangent
 ):
-    head_place = lax.axis_index("head").astype(jnp.int32)
+    side = lax.axis_index("head").astype(jnp.int32)
+    spot = lax.axis_index("dp").astype(jnp.int32)
     layers = qkv_weight.shape[0]
     row_total, seq_len = segments.shape
     rows = row_total // 2
-    offset = head_place * rows
-    segq = segments.reshape(row_total, 1, seq_len)
-    segk = segments.reshape(row_total, seq_len, 1)
-    gains = norm_gains[..., None]
-    zero = jnp.zeros((), jnp.int32)
+    width = qkv_weight.shape[2]
+    place = jnp.stack([side, 1 - side, side * rows, spot & 1, (spot >> 1) & 1])
+    core = place[CORE]
+
     far_qkv = [swap(qkv_weight[i]) for i in range(layers)]
-    far_rest = [
-        [swap(w[i]) for w in (out_weight, inner_weight, outer_weight)] for i in range(layers)
-    ]
     ffn_weights = []
     for i in range(layers):
-        both = []
-        for near, far in zip((out_weight, inner_weight, outer_weight), far_rest[i]):
-            both += [near[i], far]
-        ffn_weights.append(both)
-    sides = (head_place, 1 - head_place)
+        near = pack_weights(out_weight[i], inner_weight[i], outer_weight[i])
+        crossed = swap(lax.dynamic_index_in_dim(near, core, 0, False))
+        ffn_weights.append((near, crossed, trade(crossed, 1)))
     x_tok = tokens
     x_stream = None
     saved_attend = []
     saved_ffn = []
     contexts = []
     for i in range(layers):
-        held = []
-        for j, w in enumerate((qkv_weight[i], far_qkv[i])):
-            place = jnp.stack([offset if i == 0 else zero, sides[j], offset])
-            held.append(attend(x_tok, w, segq, segk, place, rows))
+        held = [
+            attend(x_tok, qkv_weight, i, segments, place, rows, 0, i == 0),
+            attend(x_tok, far_qkv[i][None], 0, segments, place, rows, 1, i == 0),
+        ]
         saved_attend.append(held)
         contexts.append([h[5] for h in held])
-        first_layer = i == 0
-        x_parts = [h[0] for h in held] if first_layer else [x_stream]
-        place = jnp.stack([head_place, offset])
-        results = ffn(x_parts, contexts[i], ffn_weights[i], gains[i], place, rows, i < layers - 1)
-        n1, r1, act, slope, n2, r2, x_tok = results[:7]
-        if i < layers - 1:
-            x_stream = results[7]
+        x_parts = [h[0] for h in held] if i == 0 else [x_stream]
+        results = ffn(
+            x_parts, contexts[i], ffn_weights[i], norm_gains, place, rows, i, i < layers - 1
+        )
+        n1, r1, act, slope, n2, r2, x_tok, x_stream = results
         saved_ffn.append((n2, r2, act, slope, n1, r1))
-    far_tok = swap(x_tok)
-    activations = in_order(x_tok, far_tok, head_place)
-    g_parts = [cotangent]
-    grads = [None] * layers
-    for i in reversed(range(layers)):
-        place = jnp.stack([head_place, offset])
-        d_before, dc0, dc1, outer, inner, out, gain = ffn_back(
-            g_parts, saved_ffn[i], contexts[i], ffn_weights[i], gains[i], place, rows, i == layers - 1
-        )
-        g_parts = []
-        qkv = []
-        for j, (w, dc) in enumerate(((qkv_weight[i], dc0), (far_qkv[i], dc1))):
-            place = jnp.stack([zero, sides[j], zero])
-            dx, grad = attend_back(dc, saved_attend[i][j], w, d_before, place, rows, i == 0)
-            g_parts.append(dx)
-            qkv.append(grad)
-        grads[i] = (qkv, out, inner, outer, gain[..., 0])
-    mine = jnp.where(head_place == 0, jnp.concatenate(g_parts, 1), jnp.concatenate(g_parts[::-1], 1))
-    input_grad = in_order(mine, swap(mine), head_place)
-    totals = []
-    for at in range(4):
-        near = jnp.stack([g[at][0] for g in grads])
-        far = jnp.stack([g[at][1] for g in grads])
-        totals.append(near + swap(far.astype(bf16)).astype(f32))
-    totals = lax.psum(tuple(totals), "dp")
-    gain_total = lax.psum(jnp.stack([g[4] for g in grads]), ("dp", "head"))
-    return (activations, input_grad, *totals, gain_total)
-
-
-def in_order(near, far, head_place):
-    return jnp.where(
-        head_place == 0, jnp.concatenate([near, far]), jnp.concatenate([far, near])
-    )
+    other_rows = (1 - side) * rows * seq_len
+    activations = lax.dynamic_update_slice(x_stream, swap(x_tok), (other_rows, jnp.int32(0)))
+
+    d_before, dc0, dc1, keep, send, gain1 = ffn_back(
+        [cotangent], saved_ffn[1], contexts[1], ffn_weights[1], norm_gains, place, rows, 1, False
+    )
+    late = reduce_parts(keep, send)
+    dx1, later1 = attend_back(
+        dc1, saved_attend[1][1], far_qkv[1][None], 0, d_before, place, rows, 1, None
+    )
+    dx0, later0 = attend_back(
+        dc0, saved_attend[1][0], qkv_weight, 1, d_before, place, rows, 0, None
+    )
+    d_before, dc0, dc1, keep, send, gain0 = ffn_back(
+        [dx0, dx1], saved_ffn[0], contexts[0], ffn_weights[0], norm_gains, place, rows, 0, True
+    )
+    early = reduce_parts(keep, send)
+    dx1, full, keep1, send1 = attend_back(
+        dc1,
+        saved_attend[0][1],
+        far_qkv[0][None],
+        0,
+        d_before,
+        place,
+        rows,
+        1,
+        (later1, gain0, gain1, None),
+    )
+    crossed = swap(add(keep1, trade(send1, 1)))
+    far_dx1 = swap(dx1)
+    dx0, full, keep0, send0 = attend_back(
+        dc0, saved_attend[0][0], qkv_weight, 0, d_before, place, rows, 0, (later0, gain0, gain1, full)
+    )
+    core_part = trade(send0, 1)
+    far_dx0 = swap(dx0)
+    total = add3(keep0[0], core_part[0], crossed[0])
+    total = add(total, trade(add3(keep0[1], core_part[1], crossed[1]), 2))
+    for stride in far_strides():
+        total = add(total, trade(total, stride))
+    qkv_parts = spread_out(total)
+    half = qkv_weight.shape[-1]
+    input_grad = lax.dynamic_update_slice(full, far_dx1, (other_rows, side * half))
+    input_grad = lax.dynamic_update_slice(input_grad, far_dx0, (other_rows, (1 - side) * half))
+    totals = finish([early, late], qkv_parts, place, width)
+    return (activations, input_grad, *totals)
+
+
+def add3(a, b, c):
+    return (a.astype(f32) + b.astype(f32) + c.astype(f32)).astype(bf16)
+
+
+def reduce_parts(keep, send):
+    received = trade(send, 1)
+    results = []
+    for s in range(2):
+        steps = [swap, lambda v: trade(v, 2)]
+        strides = far_strides()
+        if s == 1:
+            steps = steps[::-1]
+            strides = strides[::-1]
+        mine, got = keep[s], received[s]
+        crossed = steps[0](add(mine[1], got[1]))
+        low = add3(mine[0, 0], got[0, 0], crossed[0])
+        high = add3(mine[0, 1], got[0, 1], crossed[1])
+        total = add(low, steps[1](high))
+        for stride in strides:
+            total = add(total, trade(total, stride))
+        results.append(total)
+    both = jnp.stack(results)
+    row = trade(both, 2)
+    core = trade(jnp.stack([both, row]), 1)
+    return [[both[s], row[s], core[:, s]] for s in range(2)]
 
 
 def solution(mesh):

time: 519 us -> 489 us (0.942)
  blocking collectives: 98.4 us -> 0 us
  waiting for transfers between devices: 142 us -> 202 us
  other arithmetic: 34.3 us -> 7.26 us
  starting transfers between devices: 18 us -> 41.7 us
  Pallas kernels: 179 us -> 199 us
  between operations: 14.8 us -> 1.38 us
    psum x1 -> x0, blocking collectives: 98.4 us -> none  [shards(): gain_total = lax.psum(jnp.stack([g[4] for g in grads]), ('dp', 'head'))]
    ppermute x0 -> x27, waiting for transfers between devices: none -> 89.7 us  [trade(): return lax.ppermute(values, 'dp', [(a, a ^ stride) for a in range(count)])]
    psum x1 -> x0, waiting for transfers between devices: 66.6 us -> none  [shards(): totals = lax.psum(tuple(totals), 'dp')]
    ppermute x14 -> x12, waiting for transfers between devices: 75.6 us -> 112 us  [swap(): return lax.ppermute(values, 'head', [(0, 1), (1, 0)])]
    ppermute x0 -> x27, starting transfers between devices: none -> 24.4 us  [trade(): return lax.ppermute(values, 'dp', [(a, a ^ stride) for a in range(count)])]
    pallas_call x12 -> x13, Pallas kernels: 179 us -> 199 us  [call(): pl.pallas_call(kernel, out_shape=outs, grid_spec=pltpu.PrefetchScalarGrid...]
    dynamic_update_slice x0 -> x3, local copies, waits for them, and re-layouts: none -> 16 us  [the longest x1 8.25 us: shards(): lax.dynamic_update_slice(full, far_dx1, (other_rows, side * half))]
    add x4 -> x0, other arithmetic: 12 us -> none  [shards(): totals.append(near + swap(far.astype(bf16)).astype(f32))]
  transfers between devices with their start and end apart: 15 -> 39, of which waited for: 7 -> 20; matrix products, arithmetic and copies ran while one was open for 8% -> 7% of each run, Pallas kernels for 16% -> 15%
where the time goes in v2:
time: 489 us; the launch traced here: 482 us
  waiting for transfers between devices  202 us (41%)
  Pallas kernels  199 us (41%)
  starting transfers between devices  41.7 us (9%)
  local copies, waits for them, and re-layouts  30.8 us (6%)
  other arithmetic  7.26 us (1%)
    pallas_call x13, Pallas kernels, call(): pl.pallas_call(kernel, out_shape=outs, grid_spec=pltpu.PrefetchScalarGrid...  199 us
    ppermute x12, waiting for transfers between devices, swap(): return lax.ppermute(values, 'head', [(0, 1), (1, 0)])  112 us
    ppermute x27, waiting for transfers between devices, trade(): return lax.ppermute(values, 'dp', [(a, a ^ stride) for a in range(count)])  89.7 us
    ppermute x27, starting transfers between devices, trade(): return lax.ppermute(values, 'dp', [(a, a ^ stride) for a in range(count)])  24.4 us
    ppermute x12, starting transfers between devices, swap(): return lax.ppermute(values, 'head', [(0, 1), (1, 0)])  17.4 us
  transfers between devices with their start and end apart: 39, of which 20 were waited for; matrix products, arithmetic and copies ran while one was open for 7% of the time, Pallas kernels for 15%

profile of v2, /device:TPU:0, one launch (start us, length us, event | category | flops | bytes accessed | tf_op | source)
XLA Modules:
  0.0 482.2 jit_solution(2076259171015646352)
XLA Ops:
  14.2 9.1 %attend.4 = (bf16[2,384,512]{2,1,0:T(8,128)(2,1)}, bf16[2,384,512]{2,1,0:T(8,128)(2,1)}, bf16[2,384,512]{2,1,0:T(8,128)(2,1)}, bf16[2,2,512,192]{3,2,1,0:T(8,128...) custom-call(s32[5]{0:T(128)} %stack.98.place, bf16[2048,768]{1,0:T(8,128)(2,1)} %x_ref.3, ...), custom_call_target="tpu_custom_call" | custom-call | flops 10339999744 | bytes 9400000 | tf_op jit(solution)/shard_map/attend/pallas_call | solution.py:497
  23.4 39.3 %collective-permute-done.1.refs_5_.refs_11_ = bf16[3,192,768]{2,1,0:T(8,128)(2,1)S(1)} collective-permute-done((bf16[3,192,768]{2,1,0:T(8,128)(2,1)}, bf16[3,192,768]{2,1,0:T(8,128)(2,1)S(1)}, u32[]{:S(2)}, u32[]{:S(2)}) %collective-permute-start.1) | collective-permute-done | bytes 884768 | tf_op jit(solution)/shard_map/ppermute | solution.py:727
  62.6 9.1 %attend.5 = (bf16[2,384,512]{2,1,0:T(8,128)(2,1)}, bf16[2,384,512]{2,1,0:T(8,128)(2,1)}, bf16[2,384,512]{2,1,0:T(8,128)(2,1)}, bf16[2,2,512,192]{3,2,1,0:T(8,128...) custom-call(s32[5]{0:T(128)} %stack.98.place, bf16[2048,768]{1,0:T(8,128)(2,1)} %x_ref.3, ...), custom_call_target="tpu_custom_call" | custom-call | flops 10339999744 | bytes 9400000 | tf_op jit(solution)/shard_map/attend/pallas_call | solution.py:497
  73.2 20.8 %ffn.2 = (f32[2,2,384,512]{3,2,1,0:T(8,128)}, f32[2,1,512]{2,1,0:T(1,128)}, bf16[2,2,2,768,512]{4,3,2,1,0:T(8,128)(2,1)}, bf16[2,2,2,768,512]{4,3,2,1,0:T(8,128)...) custom-call(s32[5]{0:T(128)} %stack.98.place, ...), custom_call_target="tpu_custom_call" | custom-call | flops 22000001024 | bytes 20000000 | tf_op jit(solution)/shard_map/ffn/pallas_call | solution.py:497
  94.0 9.1 %attend.6 = (bf16[2,384,512]{2,1,0:T(8,128)(2,1)}, bf16[2,384,512]{2,1,0:T(8,128)(2,1)}, bf16[2,384,512]{2,1,0:T(8,128)(2,1)}, bf16[2,2,512,192]{3,2,1,0:T(8,128...) custom-call(s32[5]{0:T(128)} %stack.98.place, bf16[1024,768]{1,0:T(8,128)(2,1)} %get-tuple-element.81.x_ref, ...), custom_call_target="tpu_custom_call" | custom-call | flops 10339999744 | bytes 9400000 | tf_op jit(solution)/shard_map/attend/pallas_call | solution.py:497
  103.1 9.1 %attend.7 = (bf16[2,384,512]{2,1,0:T(8,128)(2,1)}, bf16[2,384,512]{2,1,0:T(8,128)(2,1)}, bf16[2,384,512]{2,1,0:T(8,128)(2,1)}, bf16[2,2,512,192]{3,2,1,0:T(8,128...) custom-call(s32[5]{0:T(128)} %stack.98.place, bf16[1024,768]{1,0:T(8,128)(2,1)} %get-tuple-element.81.x_ref, ...), custom_call_target="tpu_custom_call" | custom-call | flops 10339999744 | bytes 9400000 | tf_op jit(solution)/shard_map/attend/pallas_call | solution.py:497
  113.1 31.7 %ffn.3 = (f32[2,2,384,512]{3,2,1,0:T(8,128)}, f32[2,1,512]{2,1,0:T(1,128)}, bf16[2,2,2,768,512]{4,3,2,1,0:T(8,128)(2,1)}, bf16[2,2,2,768,512]{4,3,2,1,0:T(8,128)...) custom-call(s32[5]{0:T(128)} %stack.98.place, ...), custom_call_target="tpu_custom_call" | custom-call | flops 22000001024 | bytes 20000000 | tf_op jit(solution)/shard_map/ffn/pallas_call | solution.py:497
  144.8 25.3 %ffn_back.2 = (f32[2,2,384,512]{3,2,1,0:T(8,128)}, bf16[2,384,512]{2,1,0:T(8,128)(2,1)}, bf16[2,384,512]{2,1,0:T(8,128)(2,1)}, bf16[2,2,2,3,48,768]{5,4,3,2,1,0:...) custom-call(s32[5]{0:T(128)} %stack.98.place, bf16[2048,768]{1,0:T(8,128)(2,1)} %refs_0_.1, ...), custom_call_target="tpu_custom_call" | custom-call | flops 25300000768 | bytes 23000000 | tf_op jit(solution)/shard_map/ffn_back/pallas_call | solution.py:497
  170.1 12.9 %attend_back.5 = (f32[2,384,512]{2,1,0:T(8,128)}, f32[3,192,384]{2,1,0:T(8,128)}) custom-call(s32[5]{0:T(128)} %stack.98.place, bf16[2,384,512]{2,1,0:T(8,128)(2,1)} %get-tuple-element.100.dc_ref, bf16[2,384,512]{2,1,0:T(8,128)(2,1)} %get-tuple-element.83.refs_2_.refs_8_.ct_ref, bf16[2,2,2,384,768]{4,3,2,1,0:T(8,128)(2,1)} %get-tuple-element.101.p_ref, ...), custom_call_target="tpu_custom_call" | custom-call | flops 14300000256 | bytes 13000000 | tf_op jit(solution)/shard_map/attend_back/pallas_call | solution.py:497
  183.0 13.0 %attend_back.4 = (f32[2,384,512]{2,1,0:T(8,128)}, f32[3,192,384]{2,1,0:T(8,128)}) custom-call(s32[5]{0:T(128)} %stack.98.place, bf16[2,384,512]{2,1,0:T(8,128)(2,1)} %get-tuple-element.92.dc_ref, bf16[2,384,512]{2,1,0:T(8,128)(2,1)} %get-tuple-element.82.refs_1_.refs_7_.ct_ref, bf16[2,2,2,384,768]{4,3,2,1,0:T(8,128)(2,1)} %get-tuple-element.93.p_ref, ...), custom_call_target="tpu_custom_call" | custom-call | flops 14300000256 | bytes 13000000 | tf_op jit(solution)/shard_map/attend_back/pallas_call | solution.py:497
  196.0 25.1 %ffn_back.3 = (f32[2,2,384,512]{3,2,1,0:T(8,128)}, bf16[2,384,512]{2,1,0:T(8,128)(2,1)}, bf16[2,384,512]{2,1,0:T(8,128)(2,1)}, bf16[2,2,2,3,48,768]{5,4,3,2,1,0:...) custom-call(s32[5]{0:T(128)} %stack.98.place, f32[2,384,512]{2,1,0:T(8,128)} %get-tuple-element.99.refs_0_, ...), custom_call_target="tpu_custom_call" | custom-call | flops 25300000768 | bytes 23000000 | tf_op jit(solution)/shard_map/ffn_back/pallas_call | solution.py:497
  221.1 13.8 %attend_back.6 = (bf16[1024,384]{1,0:T(8,128)(2,1)}, bf16[2048,768]{1,0:T(8,128)(2,1)}, bf16[2,304,384]{2,1,0:T(8,128)(2,1)}, bf16[2,304,384]{2,1,0:T(8,128)(2,1)}) custom-call(s32[5]{0:T(128)} %stack.98.place, bf16[2,384,512]{2,1,0:T(8,128)(2,1)} %get-tuple-element.122.dc_ref, bf16[2,384,512]{2,1,0:T(8,128)(2,1)} %get-tuple-element.79.refs_3_.refs_9_.ct_ref, ...), custom_call_target="tpu_custom_call" | custom-call | flops 14300000256 | bytes 13000000 | tf_op jit(solution)/shard_map/attend_back/pallas_call | solution.py:497
  235.0 13.7 %attend_back.7 = (bf16[1024,384]{1,0:T(8,128)(2,1)}, bf16[2048,768]{1,0:T(8,128)(2,1)}, bf16[2,304,384]{2,1,0:T(8,128)(2,1)}, bf16[2,304,384]{2,1,0:T(8,128)(2,1)}) custom-call(s32[5]{0:T(128)} %stack.98.place, bf16[2,384,512]{2,1,0:T(8,128)(2,1)} %get-tuple-element.113.dc_ref, ...), custom_call_target="tpu_custom_call", output_to_operand_aliasing={{1}: (13, {})} | custom-call | flops 14300000256 | bytes 13000000 | tf_op jit(solution)/shard_map/attend_back/pallas_call | solution.py:497
  253.2 9.7 %collective-permute-done.33 = bf16[2,304,384]{2,1,0:T(8,128)(2,1)S(1)} collective-permute-done((bf16[2,304,384]{2,1,0:T(8,128)(2,1)S(1)}, bf16[2,304,384]{2,1,0:T(8,128)(2,1)S(1)}, u32[]{:S(2)}, u32[]{:S(2)}) %collective-permute-start.33) | collective-permute-done | bytes 466976 | tf_op jit(solution)/shard_map/ppermute | solution.py:727
  266.0 4.1 collective-permute-done.34
  281.8 7.8 %collective-permute-done.14 = bf16[2,3,48,768]{3,2,1,0:T(8,128)(2,1)S(1)} collective-permute-done((bf16[2,3,48,768]{3,2,1,0:T(8,128)(2,1)S(1)}, bf16[2,3,48,768]{3,2,1,0:T(8,128)(2,1)S(1)}, u32[]{:S(2)}, u32[]{:S(2)}) %collective-permute-start.14) | collective-permute-done | bytes 442400 | tf_op jit(solution)/shard_map/ppermute | solution.py:732
  291.1 47.8 %collective-permute-done.10 = bf16[2,3,48,768]{3,2,1,0:T(8,128)(2,1)S(1)} collective-permute-done((bf16[2,3,48,768]{3,2,1,0:T(8,128)(2,1)S(1)}, bf16[2,3,48,768]{3,2,1,0:T(8,128)(2,1)S(1)}, u32[]{:S(2)}, u32[]{:S(2)}) %collective-permute-start.10) | collective-permute-done | bytes 442400 | tf_op jit(solution)/shard_map/ppermute | solution.py:727
  343.5 6.8 %collective-permute-done.21 = bf16[2,3,48,768]{3,2,1,0:T(8,128)(2,1)S(1)} collective-permute-done((bf16[2,3,48,768]{3,2,1,0:T(8,128)(2,1)S(1)}, bf16[2,3,48,768]{3,2,1,0:T(8,128)(2,1)S(1)}, u32[]{:S(2)}, u32[]{:S(2)}) %collective-permute-start.21) | collective-permute-done | bytes 442400 | tf_op jit(solution)/shard_map/ppermute | solution.py:727
  352.1 4.2 collective-permute-done.15
  358.0 4.2 collective-permute-done.11
  369.9 4.2 collective-permute-done.22
  376.9 6.1 %collective-permute-done.16 = bf16[3,48,768]{2,1,0:T(8,128)(2,1)S(1)} collective-permute-done((bf16[3,48,768]{2,1,0:T(8,128)(2,1)S(1)}, bf16[3,48,768]{2,1,0:T(8,128)(2,1)S(1)}, u32[]{:S(2)}, u32[]{:S(2)}) %collective-permute-start.16) | collective-permute-done | bytes 221216 | tf_op jit(solution)/shard_map/ppermute | solution.py:732
  384.2 7.1 %collective-permute-done.12 = bf16[3,48,768]{2,1,0:T(8,128)(2,1)S(1)} collective-permute-done((bf16[3,48,768]{2,1,0:T(8,128)(2,1)S(1)}, bf16[3,48,768]{2,1,0:T(8,128)(2,1)S(1)}, u32[]{:S(2)}, u32[]{:S(2)}) %collective-permute-start.12) | collective-permute-done | bytes 221216 | tf_op jit(solution)/shard_map/ppermute | solution.py:732
  393.4 7.2 %collective-permute-done.27 = bf16[3,48,768]{2,1,0:T(8,128)(2,1)S(1)} collective-permute-done((bf16[3,48,768]{2,1,0:T(8,128)(2,1)S(1)}, bf16[3,48,768]{2,1,0:T(8,128)(2,1)S(1)}, u32[]{:S(2)}, u32[]{:S(2)}) %collective-permute-start.27) | collective-permute-done | bytes 221216 | tf_op jit(solution)/shard_map/ppermute | solution.py:732
  401.1 7.7 %collective-permute-done.23 = bf16[3,48,768]{2,1,0:T(8,128)(2,1)S(1)} collective-permute-done((bf16[3,48,768]{2,1,0:T(8,128)(2,1)S(1)}, bf16[3,48,768]{2,1,0:T(8,128)(2,1)S(1)}, u32[]{:S(2)}, u32[]{:S(2)}) %collective-permute-start.23) | collective-permute-done | bytes 221216 | tf_op jit(solution)/shard_map/ppermute | solution.py:732
  408.9 7.5 %collective-permute-done.17 = bf16[3,48,768]{2,1,0:T(8,128)(2,1)S(1)} collective-permute-done((bf16[3,48,768]{2,1,0:T(8,128)(2,1)S(1)}, bf16[3,48,768]{2,1,0:T(8,128)(2,1)S(1)}, u32[]{:S(2)}, u32[]{:S(2)}) %collective-permute-start.17) | collective-permute-done | bytes 221216 | tf_op jit(solution)/shard_map/ppermute | solution.py:732
  416.5 12.3 %collective-permute-done.13 = bf16[3,48,768]{2,1,0:T(8,128)(2,1)S(1)} collective-permute-done((bf16[3,48,768]{2,1,0:T(8,128)(2,1)S(1)}, bf16[3,48,768]{2,1,0:T(8,128)(2,1)S(1)}, u32[]{:S(2)}, u32[]{:S(2)}) %collective-permute-start.13) | collective-permute-done | bytes 221216 | tf_op jit(solution)/shard_map/ppermute | solution.py:732
  429.8 5.0 %collective-permute-done.28 = bf16[3,48,768]{2,1,0:T(8,128)(2,1)S(1)} collective-permute-done((bf16[3,48,768]{2,1,0:T(8,128)(2,1)S(1)}, bf16[3,48,768]{2,1,0:T(8,128)(2,1)S(1)}, u32[]{:S(2)}, u32[]{:S(2)}) %collective-permute-start.28) | collective-permute-done | bytes 221216 | tf_op jit(solution)/shard_map/ppermute | solution.py:732
  434.9 8.6 %collective-permute-done.24 = bf16[3,48,768]{2,1,0:T(8,128)(2,1)S(1)} collective-permute-done((bf16[3,48,768]{2,1,0:T(8,128)(2,1)S(1)}, bf16[3,48,768]{2,1,0:T(8,128)(2,1)S(1)}, u32[]{:S(2)}, u32[]{:S(2)}) %collective-permute-start.24) | collective-permute-done | bytes 221216 | tf_op jit(solution)/shard_map/ppermute | solution.py:732
  447.3 8.2 %dynamic_update_slice.10 = bf16[2048,768]{1,0:T(8,128)(2,1)} dynamic-update-slice(bf16[2048,768]{1,0:T(8,128)(2,1)} %get-tuple-element.129, bf16[1024,384]{1,0:T(8,128)(2,1)} %copy-done.17, s32[]{:T(128)S(6)} %select_n.17, s32[]{:T(128)S(6)} %select_n.18) | dynamic-update-slice | bytes 1572868 | tf_op jit(solution)/shard_map/dynamic_update_slice | solution.py:840
  455.5 7.6 %dynamic_update_slice.11 = bf16[2048,768]{1,0:T(8,128)(2,1)} dynamic-update-slice(bf16[2048,768]{1,0:T(8,128)(2,1)} %dynamic_update_slice.10, bf16[1024,384]{1,0:T(8,128)(2,1)} %collective-permute-done.8, s32[]{:T(128)S(6)} %select_n.17, s32[]{:T(128)S(6)} %select_n.19) | dynamic-update-slice | bytes 1572868 | tf_op jit(solution)/shard_map/dynamic_update_slice | solution.py:841
  475.1 6.9 %finish.1 = (f32[2,3,192,384]{3,2,1,0:T(8,128)}, f32[2,384,768]{2,1,0:T(8,128)}, f32[2,192,1536]{2,1,0:T(8,128)}, f32[2,768,384]{2,1,0:T(8,128)}, f32[2,2,768]{2,1,0:T(2,128)}) custom-call(s32[5]{0:T(128)} %stack.98.place, bf16[3,48,768]{2,1,0:T(8,128)(2,1)} %copy-done.14, bf16[3,48,768]{2,1,0:T(8,128)(2,1)} %get-tuple-element.180.refs_1_, ...), custom_call_target="tpu_custom_call" | custom-call | flops 6600000000 | bytes 6000000 | tf_op jit(solution)/shard_map/finish/pallas_call | solution.py:497
  (168 shorter events, 76.0 us)
Async XLA Ops:
  2.0 101.1 %collective-permute-start.3 = (bf16[3,192,384]{2,1,0:T(8,128)(2,1)S(1)}, bf16[3,192,384]{2,1,0:T(8,128)(2,1)}, u32[]{:S(2)}, u32[]{:S(2)}) collective-permute-start(bf16[3,192,384]{2,1,0:T(8,128)(2,1)S(1)} %get-tuple-element.169), channel_id=1, source_target_pairs={{0,1},{1,0},{2,3},{3,2},{4,5},{5,4},{6,7},{7,6},{8,9},{9,8},{10,11... | collective-permute-start | bytes 1327112 | tf_op jit(solution)/shard_map/ppermute | solution.py:727
  5.1 57.6 %collective-permute-start = (bf16[3,192,384]{2,1,0:T(8,128)(2,1)S(1)}, bf16[3,192,384]{2,1,0:T(8,128)(2,1)}, u32[]{:S(2)}, u32[]{:S(2)}) collective-permute-start(bf16[3,192,384]{2,1,0:T(8,128)(2,1)S(1)} %get-tuple-element.170), channel_id=1, source_target_pairs={{0,1},{1,0},{2,3},{3,2},{4,5},{5,4},{6,7},{7,6},{8,9},{9,8},{10,11... | collective-permute-start | bytes 1327112 | tf_op jit(solution)/shard_map/ppermute | solution.py:727
  9.4 62.3 %collective-permute-start.4 = (bf16[3,192,768]{2,1,0:T(8,128)(2,1)}, bf16[3,192,768]{2,1,0:T(8,128)(2,1)}, u32[]{:S(2)}, u32[]{:S(2)}) collective-permute-start(bf16[3,192,768]{2,1,0:T(8,128)(2,1)} %dynamic-slice_bitcast_fusion), channel_id=1, source_target_pairs={{0,1},{1,0},{2,3},{3,2},{4,5},{5,4},{6,7},{7,6},{8,9},{9,8},{10,11... | collective-permute-start | bytes 2654216 | tf_op jit(solution)/shard_map/ppermute | solution.py:727
  12.6 50.0 %collective-permute-start.1 = (bf16[3,192,768]{2,1,0:T(8,128)(2,1)}, bf16[3,192,768]{2,1,0:T(8,128)(2,1)S(1)}, u32[]{:S(2)}, u32[]{:S(2)}) collective-permute-start(bf16[3,192,768]{2,1,0:T(8,128)(2,1)} %dynamic-slice_bitcast_fusion.1), channel_id=1, source_target_pairs={{0,1},{1,0},{2,3},{3,2},{4,5},{5,4},{6,7},{7,6},{8,9},{9,8},{10,11... | collective-permute-start | bytes 2654216 | tf_op jit(solution)/shard_map/ppermute | solution.py:727
  62.6 9.7 %collective-permute-start.2 = (bf16[3,192,768]{2,1,0:T(8,128)(2,1)S(1)}, bf16[3,192,768]{2,1,0:T(8,128)(2,1)S(1)}, u32[]{:S(2)}, u32[]{:S(2)}) collective-permute-start(bf16[3,192,768]{2,1,0:T(8,128)(2,1)S(1)} %collective-permute-done.1.refs_5_.refs_11_), channel_id=1, source_target_pairs={{0,2},{2,0},{4,6},{6,4},{8,10},{10,8},{12,14},{14,12},{16,18},{18,... | collective-permute-start | bytes 2654216 | tf_op jit(solution)/shard_map/ppermute | solution.py:732
  71.7 40.5 %collective-permute-start.5 = (bf16[3,192,768]{2,1,0:T(8,128)(2,1)}, bf16[3,192,768]{2,1,0:T(8,128)(2,1)S(1)}, u32[]{:S(2)}, u32[]{:S(2)}) collective-permute-start(bf16[3,192,768]{2,1,0:T(8,128)(2,1)} %collective-permute-done.4.refs_4_.refs_10_), channel_id=1, source_target_pairs={{0,2},{2,0},{4,6},{6,4},{8,10},{10,8},{12,14},{14,12},{16,18},{18,... | collective-permute-start | bytes 2654216 | tf_op jit(solution)/shard_map/ppermute | solution.py:732
  234.9 14.3 %collective-permute-start.32 = (bf16[2,304,384]{2,1,0:T(8,128)(2,1)}, bf16[2,304,384]{2,1,0:T(8,128)(2,1)S(1)}, u32[]{:S(2)}, u32[]{:S(2)}) collective-permute-start(bf16[2,304,384]{2,1,0:T(8,128)(2,1)} %get-tuple-element.139), channel_id=1, source_target_pairs={{0,2},{2,0},{4,6},{6,4},{8,10},{10,8},{12,14},{14,12},{16,18},{18,... | collective-permute-start | bytes 1400840 | tf_op jit(solution)/shard_map/ppermute | solution.py:732
  249.3 13.6 %collective-permute-start.33 = (bf16[2,304,384]{2,1,0:T(8,128)(2,1)S(1)}, bf16[2,304,384]{2,1,0:T(8,128)(2,1)S(1)}, u32[]{:S(2)}, u32[]{:S(2)}) collective-permute-start(bf16[2,304,384]{2,1,0:T(8,128)(2,1)S(1)} %add_convert_fusion), channel_id=1, source_target_pairs={{0,1},{1,0},{2,3},{3,2},{4,5},{5,4},{6,7},{7,6},{8,9},{9,8},{10,11... | collective-permute-start | bytes 1400840 | tf_op jit(solution)/shard_map/ppermute | solution.py:727
  251.2 27.8 %collective-permute-start.9 = (bf16[2,2,2,3,48,768]{5,4,3,2,1,0:T(8,128)(2,1)}, bf16[2,2,2,3,48,768]{5,4,3,2,1,0:T(8,128)(2,1)S(1)}, u32[]{:S(2)}, u32[]{:S(2)}) collective-permute-start(bf16[2,2,2,3,48,768]{5,4,3,2,1,0:T(8,128)(2,1)} %get-tuple-element.133), channel_id=1, source_target_pairs={{0,2},{2,0},{4,6},{6,4},{8,10},{10,8},{12,14},{14,12},{16,18},{18,... | collective-permute-start | bytes 5308424 | tf_op jit(solution)/shard_map/ppermute | solution.py:732
  251.2 215.3 %collective-permute-start.6 = (bf16[1024,768]{1,0:T(8,128)(2,1)}, bf16[1024,768]{1,0:T(8,128)(2,1)S(1)}, u32[]{:S(2)}, u32[]{:S(2)}) collective-permute-start(bf16[1024,768]{1,0:T(8,128)(2,1)} %get-tuple-element.85), channel_id=1, source_target_pairs={{0,1},{1,0},{2,3},{3,2},{4,5},{5,4},{6,7},{7,6},{8,9},{9,8},{10,11... | collective-permute-start | bytes 4718600 | tf_op jit(solution)/shard_map/ppermute | solution.py:727
  251.4 204.1 %collective-permute-start.8 = (bf16[1024,384]{1,0:T(8,128)(2,1)}, bf16[1024,384]{1,0:T(8,128)(2,1)}, u32[]{:S(2)}, u32[]{:S(2)}) collective-permute-start(bf16[1024,384]{1,0:T(8,128)(2,1)} %get-tuple-element.131), channel_id=1, source_target_pairs={{0,1},{1,0},{2,3},{3,2},{4,5},{5,4},{6,7},{7,6},{8,9},{9,8},{10,11... | collective-permute-start | bytes 2359304 | tf_op jit(solution)/shard_map/ppermute | solution.py:727
  253.2 27.7 %collective-permute-start.20 = (bf16[2,2,2,3,48,768]{5,4,3,2,1,0:T(8,128)(2,1)S(1)}, bf16[2,2,2,3,48,768]{5,4,3,2,1,0:T(8,128)(2,1)S(1)}, u32[]{:S(2)}, u32[]{:S(2)}) collective-permute-start(bf16[2,2,2,3,48,768]{5,4,3,2,1,0:T(8,128)(2,1)S(1)} %copy-done.23), channel_id=1, source_target_pairs={{0,2},{2,0},{4,6},{6,4},{8,10},{10,8},{12,14},{14,12},{16,18},{18,... | collective-permute-start | bytes 5308424 | tf_op jit(solution)/shard_map/ppermute | solution.py:732
  264.0 6.1 %collective-permute-start.34 = (bf16[304,384]{1,0:T(8,128)(2,1)S(1)}, bf16[304,384]{1,0:T(8,128)(2,1)S(1)}, u32[]{:S(2)}, u32[]{:S(2)}) collective-permute-start(bf16[304,384]{1,0:T(8,128)(2,1)S(1)} %fusion.14), channel_id=1, source_target_pairs={{0,4},{2,6},{4,0},{6,2},{8,12},{10,14},{12,8},{14,10},{16,20},{18,... | collective-permute-start | bytes 700424 | tf_op jit(solution)/shard_map/ppermute | solution.py:732
  270.2 6.1 %collective-permute-start.35 = (bf16[304,384]{1,0:T(8,128)(2,1)S(1)}, bf16[304,384]{1,0:T(8,128)(2,1)S(1)}, u32[]{:S(2)}, u32[]{:S(2)}) collective-permute-start(bf16[304,384]{1,0:T(8,128)(2,1)S(1)} %fusion), channel_id=1, source_target_pairs={{0,8},{2,10},{4,12},{6,14},{8,0},{10,2},{12,4},{14,6},{16,24},{18,... | collective-permute-start | bytes 700424 | tf_op jit(solution)/shard_map/ppermute | solution.py:732
  276.4 169.1 %collective-permute-start.7 = (bf16[1024,384]{1,0:T(8,128)(2,1)S(1)}, bf16[1024,384]{1,0:T(8,128)(2,1)S(1)}, u32[]{:S(2)}, u32[]{:S(2)}) collective-permute-start(bf16[1024,384]{1,0:T(8,128)(2,1)S(1)} %copy-done.27), channel_id=1, source_target_pairs={{0,1},{1,0},{2,3},{3,2},{4,5},{5,4},{6,7},{7,6},{8,9},{9,8},{10,11... | collective-permute-start | bytes 2359304 | tf_op jit(solution)/shard_map/ppermute | solution.py:727
  279.1 10.4 %collective-permute-start.14 = (bf16[2,3,48,768]{3,2,1,0:T(8,128)(2,1)S(1)}, bf16[2,3,48,768]{3,2,1,0:T(8,128)(2,1)S(1)}, u32[]{:S(2)}, u32[]{:S(2)}) collective-permute-start(bf16[2,3,48,768]{3,2,1,0:T(8,128)(2,1)S(1)} %get-tuple-element.147), channel_id=1, source_target_pairs={{0,4},{2,6},{4,0},{6,2},{8,12},{10,14},{12,8},{14,10},{16,20},{18,... | collective-permute-start | bytes 1327112 | tf_op jit(solution)/shard_map/ppermute | solution.py:732
  280.9 58.1 %collective-permute-start.10 = (bf16[2,3,48,768]{3,2,1,0:T(8,128)(2,1)S(1)}, bf16[2,3,48,768]{3,2,1,0:T(8,128)(2,1)S(1)}, u32[]{:S(2)}, u32[]{:S(2)}) collective-permute-start(bf16[2,3,48,768]{3,2,1,0:T(8,128)(2,1)S(1)} %get-tuple-element.148), channel_id=1, source_target_pairs={{0,1},{1,0},{2,3},{3,2},{4,5},{5,4},{6,7},{7,6},{8,9},{9,8},{10,11... | collective-permute-start | bytes 1327112 | tf_op jit(solution)/shard_map/ppermute | solution.py:727
  289.5 51.3 %collective-permute-start.25 = (bf16[2,3,48,768]{3,2,1,0:T(8,128)(2,1)S(1)}, bf16[2,3,48,768]{3,2,1,0:T(8,128)(2,1)S(1)}, u32[]{:S(2)}, u32[]{:S(2)}) collective-permute-start(bf16[2,3,48,768]{3,2,1,0:T(8,128)(2,1)S(1)} %get-tuple-element.145), channel_id=1, source_target_pairs={{0,4},{2,6},{4,0},{6,2},{8,12},{10,14},{12,8},{14,10},{16,20},{18,... | collective-permute-start | bytes 1327112 | tf_op jit(solution)/shard_map/ppermute | solution.py:732
  339.0 11.3 %collective-permute-start.21 = (bf16[2,3,48,768]{3,2,1,0:T(8,128)(2,1)S(1)}, bf16[2,3,48,768]{3,2,1,0:T(8,128)(2,1)S(1)}, u32[]{:S(2)}, u32[]{:S(2)}) collective-permute-start(bf16[2,3,48,768]{3,2,1,0:T(8,128)(2,1)S(1)} %get-tuple-element.146), channel_id=1, source_target_pairs={{0,1},{1,0},{2,3},{3,2},{4,5},{5,4},{6,7},{7,6},{8,9},{9,8},{10,11... | collective-permute-start | bytes 1327112 | tf_op jit(solution)/shard_map/ppermute | solution.py:727
  340.8 122.3 %collective-permute-start.36 = (bf16[304,384]{1,0:T(8,128)(2,1)}, bf16[304,384]{1,0:T(8,128)(2,1)}, u32[]{:S(2)}, u32[]{:S(2)}) collective-permute-start(bf16[304,384]{1,0:T(8,128)(2,1)} %add_convert_fusion.6), channel_id=1, source_target_pairs={{0,16},{2,18},{4,20},{6,22},{8,24},{10,26},{12,28},{14,30},{16,0},... | collective-permute-start | bytes 700424 | tf_op jit(solution)/shard_map/ppermute | solution.py:732
  374.0 8.9 %collective-permute-start.16 = (bf16[3,48,768]{2,1,0:T(8,128)(2,1)S(1)}, bf16[3,48,768]{2,1,0:T(8,128)(2,1)S(1)}, u32[]{:S(2)}, u32[]{:S(2)}) collective-permute-start(bf16[3,48,768]{2,1,0:T(8,128)(2,1)S(1)} %add_convert_fusion.17), channel_id=1, source_target_pairs={{0,16},{2,18},{4,20},{6,22},{8,24},{10,26},{12,28},{14,30},{16,0},... | collective-permute-start | bytes 663560 | tf_op jit(solution)/shard_map/ppermute | solution.py:732
  383.0 8.3 %collective-permute-start.12 = (bf16[3,48,768]{2,1,0:T(8,128)(2,1)S(1)}, bf16[3,48,768]{2,1,0:T(8,128)(2,1)S(1)}, u32[]{:S(2)}, u32[]{:S(2)}) collective-permute-start(bf16[3,48,768]{2,1,0:T(8,128)(2,1)S(1)} %add_convert_fusion.20), channel_id=1, source_target_pairs={{0,8},{2,10},{4,12},{6,14},{8,0},{10,2},{12,4},{14,6},{16,24},{18,... | collective-permute-start | bytes 663560 | tf_op jit(solution)/shard_map/ppermute | solution.py:732
  391.3 9.3 %collective-permute-start.27 = (bf16[3,48,768]{2,1,0:T(8,128)(2,1)S(1)}, bf16[3,48,768]{2,1,0:T(8,128)(2,1)S(1)}, u32[]{:S(2)}, u32[]{:S(2)}) collective-permute-start(bf16[3,48,768]{2,1,0:T(8,128)(2,1)S(1)} %add_convert_fusion.11), channel_id=1, source_target_pairs={{0,16},{2,18},{4,20},{6,22},{8,24},{10,26},{12,28},{14,30},{16,0},... | collective-permute-start | bytes 663560 | tf_op jit(solution)/shard_map/ppermute | solution.py:732
  400.6 8.3 %collective-permute-start.23 = (bf16[3,48,768]{2,1,0:T(8,128)(2,1)S(1)}, bf16[3,48,768]{2,1,0:T(8,128)(2,1)S(1)}, u32[]{:S(2)}, u32[]{:S(2)}) collective-permute-start(bf16[3,48,768]{2,1,0:T(8,128)(2,1)S(1)} %add_convert_fusion.14), channel_id=1, source_target_pairs={{0,8},{2,10},{4,12},{6,14},{8,0},{10,2},{12,4},{14,6},{16,24},{18,... | collective-permute-start | bytes 663560 | tf_op jit(solution)/shard_map/ppermute | solution.py:732
  408.9 7.6 %collective-permute-start.17 = (bf16[3,48,768]{2,1,0:T(8,128)(2,1)S(1)}, bf16[3,48,768]{2,1,0:T(8,128)(2,1)S(1)}, u32[]{:S(2)}, u32[]{:S(2)}) collective-permute-start(bf16[3,48,768]{2,1,0:T(8,128)(2,1)S(1)} %add_convert_fusion.16), channel_id=1, source_target_pairs={{0,8},{2,10},{4,12},{6,14},{8,0},{10,2},{12,4},{14,6},{16,24},{18,... | collective-permute-start | bytes 663560 | tf_op jit(solution)/shard_map/ppermute | solution.py:732
  416.5 12.4 %collective-permute-start.13 = (bf16[3,48,768]{2,1,0:T(8,128)(2,1)S(1)}, bf16[3,48,768]{2,1,0:T(8,128)(2,1)S(1)}, u32[]{:S(2)}, u32[]{:S(2)}) collective-permute-start(bf16[3,48,768]{2,1,0:T(8,128)(2,1)S(1)} %add_convert_fusion.19), channel_id=1, source_target_pairs={{0,16},{2,18},{4,20},{6,22},{8,24},{10,26},{12,28},{14,30},{16,0},... | collective-permute-start | bytes 663560 | tf_op jit(solution)/shard_map/ppermute | solution.py:732
  434.8 8.6 %collective-permute-start.24 = (bf16[3,48,768]{2,1,0:T(8,128)(2,1)S(1)}, bf16[3,48,768]{2,1,0:T(8,128)(2,1)S(1)}, u32[]{:S(2)}, u32[]{:S(2)}) collective-permute-start(bf16[3,48,768]{2,1,0:T(8,128)(2,1)S(1)} %add_convert_fusion.13), channel_id=1, source_target_pairs={{0,16},{2,18},{4,20},{6,22},{8,24},{10,26},{12,28},{14,30},{16,0},... | collective-permute-start | bytes 663560 | tf_op jit(solution)/shard_map/ppermute | solution.py:732
  443.4 22.2 %collective-permute-start.18 = (bf16[2,3,48,768]{3,2,1,0:T(8,128)(2,1)}, bf16[2,3,48,768]{3,2,1,0:T(8,128)(2,1)S(1)}, u32[]{:S(2)}, u32[]{:S(2)}) collective-permute-start(bf16[2,3,48,768]{3,2,1,0:T(8,128)(2,1)} %get-tuple-element.182), channel_id=1, source_target_pairs={{0,4},{2,6},{4,0},{6,2},{8,12},{10,14},{12,8},{14,10},{16,20},{18,... | collective-permute-start | bytes 1327112 | tf_op jit(solution)/shard_map/ppermute | solution.py:732
  446.4 19.4 %collective-permute-start.29 = (bf16[2,3,48,768]{3,2,1,0:T(8,128)(2,1)}, bf16[2,3,48,768]{3,2,1,0:T(8,128)(2,1)S(1)}, u32[]{:S(2)}, u32[]{:S(2)}) collective-permute-start(bf16[2,3,48,768]{3,2,1,0:T(8,128)(2,1)} %get-tuple-element.178), channel_id=1, source_target_pairs={{0,4},{2,6},{4,0},{6,2},{8,12},{10,14},{12,8},{14,10},{16,20},{18,... | collective-permute-start | bytes 1327112 | tf_op jit(solution)/shard_map/ppermute | solution.py:732
  464.4 6.1 %collective-permute-start.37 = (bf16[304,384]{1,0:T(8,128)(2,1)S(1)}, bf16[304,384]{1,0:T(8,128)(2,1)S(1)}, u32[]{:S(2)}, u32[]{:S(2)}) collective-permute-start(bf16[304,384]{1,0:T(8,128)(2,1)S(1)} %add_convert_fusion.5.refs_12_), channel_id=1, source_target_pairs={{0,4},{2,6},{4,0},{6,2},{8,12},{10,14},{12,8},{14,10},{16,20},{18,... | collective-permute-start | bytes 700424 | tf_op jit(solution)/shard_map/ppermute | solution.py:732
  465.7 6.6 %collective-permute-start.19 = (bf16[2,2,3,48,768]{4,3,2,0,1:T(8,128)(2,1)S(1)}, bf16[2,2,3,48,768]{4,3,2,0,1:T(8,128)(2,1)S(1)}, u32[]{:S(2)}, u32[]{:S(2)}) collective-permute-start(bf16[2,2,3,48,768]{4,3,2,0,1:T(8,128)(2,1)S(1)} %pad_maximum_fusion), channel_id=1, source_target_pairs={{0,2},{2,0},{4,6},{6,4},{8,10},{10,8},{12,14},{14,12},{16,18},{18,... | collective-permute-start | bytes 2654216 | tf_op jit(solution)/shard_map/ppermute | solution.py:732
  465.9 7.4 %collective-permute-start.30 = (bf16[2,2,3,48,768]{4,3,2,0,1:T(8,128)(2,1)S(1)}, bf16[2,2,3,48,768]{4,3,2,0,1:T(8,128)(2,1)S(1)}, u32[]{:S(2)}, u32[]{:S(2)}) collective-permute-start(bf16[2,2,3,48,768]{4,3,2,0,1:T(8,128)(2,1)S(1)} %pad_maximum_fusion.1), channel_id=1, source_target_pairs={{0,2},{2,0},{4,6},{6,4},{8,10},{10,8},{12,14},{14,12},{16,18},{18,... | collective-permute-start | bytes 2654216 | tf_op jit(solution)/shard_map/ppermute | solution.py:732
  (36 other events, 255.6 us)

commit v3 on v2

--- a/solution.py
+++ b/solution.py
@@ -63,9 +63,25 @@
     return jnp.broadcast_to(row, (128, row.shape[1])).T
 
 
-def attend_kernel(place, x_ref, w_ref, seg_ref, xt_ref, qt_ref, kt_ref, v_ref, p_ref, ct_ref):
+def take_weights(place, far, refs):
+    if not far:
+        return (lambda s: refs[0][s]), refs[1:]
+    crossed, traded, *refs = refs
+    scr = refs.pop()
+
+    @pl.when(pl.program_id(0) == 0)
+    def _():
+        scr[:, place[CORE]] = crossed[...]
+        scr[:, 1 - place[CORE]] = traded[...]
+
+    return (lambda s: scr[s].reshape(2 * scr.shape[2], scr.shape[3])), refs
+
+
+def attend_kernel(far, place, x_ref, *refs):
+    weight, refs = take_weights(place, far, refs)
+    seg_ref, xt_ref, qt_ref, kt_ref, v_ref, p_ref, ct_ref = refs
     seq_len, channels = x_ref.shape
-    width = w_ref.shape[1]
+    width = v_ref.shape[-1]
     window = QUERY_TILE + REACH
     heads = width // HEAD_DIM
     tiles = seq_len // QUERY_TILE
@@ -86,7 +102,7 @@
         span = slice(group * width, (group + 1) * width)
         xg = x[:, span]
         xtg = xt[span]
-        wq, wk, wv = (w_ref[s][:, span] for s in range(3))
+        wq, wk, wv = (weight(s)[:, span] for s in range(3))
         qt = mm(wq, xtg, TN).astype(bf16) * jnp.asarray(HEAD_DIM**-0.5, bf16)
         kt = mm(wk, xtg, TN).astype(bf16)
         vt = mm(wv, xtg, TN).astype(bf16)
@@ -125,6 +141,7 @@
 def attend_back_kernel(
     last,
     aliased,
+    far,
     place,
     dc_ref,
     ct_ref,
@@ -133,10 +150,10 @@
     kt_ref,
     v_ref,
     xt_ref,
-    w_ref,
     dz_ref,
     *refs,
 ):
+    weight, refs = take_weights(place, far, refs)
     if last:
         later_ref, gain0_ref, gain1_ref, *refs = refs
         if aliased:
@@ -145,7 +162,7 @@
     else:
         dx_ref, grad_ref, ds_ref = refs
     channels, seq_len = xt_ref.shape[1:]
-    width = w_ref.shape[1]
+    width = v_ref.shape[-1]
     window = QUERY_TILE + REACH
     heads = width // HEAD_DIM
     tiles = seq_len // QUERY_TILE
@@ -199,7 +216,7 @@
         grads[0].append(mm(xtg, dq, NT))
         grads[1].append(mm(xtg, dk, NN))
         grads[2].append(mm(xtg, dv, NN))
-        wq, wk, wv = (w_ref[s][:, span] for s in range(3))
+        wq, wk, wv = (weight(s)[:, span] for s in range(3))
         d_inputs.append(
             dz_ref[0, 0, span] + mm(wq, dq, NN) + mm(wk, dk, NT) + mm(wv, dv, NT)
         )
@@ -436,48 +453,59 @@
     return functools.reduce(jnp.add, chunks)
 
 
-def finish_kernel(place, *refs):
-    ffn_parts = [[refs[(layer * 2 + s) * 3 : (layer * 2 + s) * 3 + 3] for s in range(2)] for layer in range(2)]
-    qkv_parts = refs[12:15]
-    qkv_ref, out_ref, inner_ref, outer_ref, gain_ref = refs[15:]
-
-    def pieces(parts):
-        mine, row, core = parts
-        yield 0, 0, mine[...]
-        yield 0, 1, row[...]
-        yield 1, 0, core[0]
-        yield 1, 1, core[1]
-
-    half = out_ref.shape[1]
-    wide = out_ref.shape[2]
-    piece = half // 8
-    for layer in range(2):
-        for s in range(2):
-            for c, y, value in pieces(ffn_parts[layer][s]):
-                value = value.astype(f32)
-                at = ((place[CORE] ^ c) * 2 + (place[ROW] ^ y)) * piece
-                rows = pl.ds(pl.multiple_of(at, piece), piece)
-                low = pl.ds(pl.multiple_of(s * half // 2 + at, piece), piece)
-                high = pl.ds(pl.multiple_of(half + s * half // 2 + at, piece), piece)
-                out_ref[layer, low, :] = value[0]
-                inner_ref[layer, rows, s * wide : (s + 1) * wide] = value[1]
-                outer_ref[layer, low, :] = value[2][:, :half]
-                outer_ref[layer, high, :] = value[2][:, half:]
-    piece = qkv_ref.shape[2] // 4
-    for c, y, value in pieces(qkv_parts):
-        at = ((place[CORE] ^ c) * 2 + (place[ROW] ^ y)) * piece
-        rows = pl.ds(pl.multiple_of(at, piece), piece)
+def placed_pieces(place, parts, size):
+    mine, row, core = parts
+    for c, y, value in ((0, 0, mine[...]), (0, 1, row[...]), (1, 0, core[0]), (1, 1, core[1])):
+        yield ((place[CORE] ^ c) * 2 + (place[ROW] ^ y)) * size, value
+
+
+def rows_at(at, size):
+    return pl.ds(pl.multiple_of(at, size), size)
+
+
+def finish_ffn_kernel(place, *refs):
+    out_ref, inner_ref, outer_ref = refs[-3:]
+    half, wide = out_ref.shape[1:]
+    size = half // 8
+    for s in range(2):
+        for at, value in placed_pieces(place, refs[3 * s : 3 * s + 3], size):
+            value = value.astype(f32)
+            low = s * (half // 2) + at
+            out_ref[0, rows_at(low, size), :] = value[0]
+            inner_ref[0, rows_at(at, size), s * wide : (s + 1) * wide] = value[1]
+            outer_ref[0, rows_at(low, size), :] = value[2][:, :half]
+            outer_ref[0, rows_at(half + low, size), :] = value[2][:, half:]
+
+
+def finish_qkv_kernel(place, mine, row, core, qkv_ref, gain_ref):
+    half = qkv_ref.shape[3]
+    size = qkv_ref.shape[2] // 4
+    for at, value in placed_pieces(place, (mine, row, core), size):
         for layer in range(2):
             for s in range(3):
-                index = (layer * 3 + s) * piece
-                qkv_ref[layer, s, rows, :] = value[index : index + piece].astype(f32)
-        if c == 0 and y == 0:
-            gains = value[6 * piece : 6 * piece + 16].astype(f32)
-            for layer in range(2):
-                for i in range(2):
-                    at = layer * 4 + i
-                    gain_ref[layer, i : i + 1, :half] = gains[at : at + 1]
-                    gain_ref[layer, i : i + 1, half:] = gains[8 + at : 9 + at]
+                index = (layer * 3 + s) * size
+                qkv_ref[layer, s, rows_at(at, size), :] = value[index : index + size].astype(f32)
+    gains = mine[6 * size : 6 * size + 16].astype(f32)
+    for layer in range(2):
+        for i in range(2):
+            at = layer * 4 + i
+            gain_ref[layer, i : i + 1, :half] = gains[at : at + 1]
+            gain_ref[layer, i : i + 1, half:] = gains[8 + at : 9 + at]
+
+
+def pack_kernel(place, out_ref, inner_ref, outer_ref, qkv_ref, near_ref, piece_ref, part_ref):
+    half, wide = out_ref.shape[1:]
+    depth = half // 2
+    for i in range(2):
+        rows = slice(i * depth, (i + 1) * depth)
+        near_ref[i, 0] = out_ref[0, rows]
+        near_ref[i, 1] = inner_ref[0, :, i * wide : (i + 1) * wide]
+        near_ref[i, 2, :, :half] = outer_ref[0, rows]
+        near_ref[i, 2, :, half:] = outer_ref[0, half + i * depth : half + (i + 1) * depth]
+    piece_ref[...] = near_ref[place[CORE]]
+    size = qkv_ref.shape[2] // 2
+    for s in range(3):
+        part_ref[s] = qkv_ref[0, s, rows_at(place[CORE] * size, size), :]
 
 
 def whole(shape):
@@ -493,9 +521,18 @@
     return jax.ShapeDtypeStruct(shape, dtype)
 
 
-def call(kernel, rows, place, operands, in_specs, outs, out_specs, scratch, name, us, aliases=None):
-    return pl.pallas_call(
-        kernel,
+def call(
+    kernel, rows, place, operands, in_specs, outs, out_specs, scratch, name, us, aliases=None, after=()
+):
+    count = len(operands)
+    in_specs = list(in_specs) + [pl.BlockSpec(memory_space=pl.ANY)] * len(after)
+    operands = tuple(operands) + tuple(after)
+
+    def body(place, *refs):
+        kernel(place, *refs[:count], *refs[count + len(after) :])
+
+    results = pl.pallas_call(
+        body,
         out_shape=outs,
         grid_spec=pltpu.PrefetchScalarGridSpec(
             num_scalar_prefetch=1,
@@ -506,16 +543,19 @@
         ),
         compiler_params=pltpu.CompilerParams(vmem_limit_bytes=60 * 2**20),
         cost_estimate=pl.CostEstimate(
-            flops=int(us * 1.1e9), bytes_accessed=int(us * 1e6), transcendentals=0
+            flops=int(us * 5e9), bytes_accessed=int(us * 1e7), transcendentals=0
         ),
         input_output_aliases=aliases or {},
         name=name,
     )(place, *operands)
-
-
-def attend(x_tok, w, w_layer, segments, place, rows, j, from_input):
+    return list(results)
+
+
+def attend(x_tok, w, segments, place, rows, j, layer, after=()):
     row_total, seq_len = segments.shape
-    width, channels = w.shape[-2:]
+    far = j == 1
+    channels = w[0].shape[-1]
+    width = channels // 2
     heads = width // HEAD_DIM
     groups = channels // width
     tiles = seq_len // QUERY_TILE
@@ -528,22 +568,34 @@
         struct((rows, groups, tiles, window, heads * QUERY_TILE), bf16),
         struct((rows, channels, seq_len), bf16),
     ]
-    if from_input:
+    if layer == 0:
         x_spec = pl.BlockSpec((seq_len, channels), lambda r, place: (place[OFFSET] + r, place[j]))
     else:
         x_spec = pl.BlockSpec((seq_len, channels), lambda r, place: (r, place[j]))
     return call(
-        attend_kernel,
+        functools.partial(attend_kernel, far),
         rows,
         place,
-        (x_tok, w, segments),
-        [x_spec, layer_block(w.shape, w_layer), whole(segments.shape)],
+        (x_tok, *w, segments),
+        [x_spec, *weight_blocks(w, far, layer), whole(segments.shape)],
         outs,
         [per_row(o.shape) for o in outs],
-        [],
+        weight_scratch(w, far),
         "attend",
-        4.7 * rows,
-    )
+        0.2 if far and layer == 0 else 4.7 * rows,
+        after=after,
+    )
+
+
+def weight_blocks(w, far, layer):
+    return [whole(o.shape) for o in w] if far else [layer_block(w[0].shape, layer)]
+
+
+def weight_scratch(w, far):
+    if not far:
+        return []
+    three, depth, channels = w[0].shape
+    return [pltpu.VMEM((three, 2, depth, channels), bf16)]
 
 
 def layer_block(shape, layer):
@@ -551,24 +603,26 @@
     return pl.BlockSpec((None,) + tuple(shape[1:]), lambda r, place: (layer,) + rest)
 
 
-def attend_back(d_context, saved, w, w_layer, d_before, place, rows, j, extra):
+def attend_back(d_context, saved, w, d_before, place, rows, j, layer, extra, after=()):
     xt, qt, kt, values, probs, ct = saved
     channels, seq_len = xt.shape[1:]
     window = QUERY_TILE + REACH
-    width = w.shape[-2]
+    width = values.shape[-1]
+    far = j == 1
     heads = width // HEAD_DIM
     operands = (d_context, ct, probs, qt, kt, values, xt)
     in_specs = [per_row(o.shape) for o in operands] + [
-        layer_block(w.shape, w_layer),
         pl.BlockSpec((1, 1, channels, seq_len), lambda r, place: (r, place[j], 0, 0)),
+        *weight_blocks(w, far, layer),
     ]
-    operands += (w, d_before)
-    scratch = [pltpu.VMEM((window, heads * QUERY_TILE), bf16)]
+    operands += (d_before, *w)
+    scratch = [pltpu.VMEM((window, heads * QUERY_TILE), bf16)] + weight_scratch(w, far)
+    grad = (3, width, channels)
     aliases = {}
     if extra is None:
         dx = struct((rows, channels, seq_len), f32)
-        outs = [dx, struct(w.shape[1:], f32)]
-        out_specs = [per_row(dx.shape), whole(w.shape[1:])]
+        outs = [dx, struct(grad, f32)]
+        out_specs = [per_row(dx.shape), whole(grad)]
     else:
         later, gain0, gain1, full = extra
         operands += (later, gain0, gain1)
@@ -590,9 +644,9 @@
             whole(piece.shape),
             whole(piece.shape),
         ]
-        scratch = [pltpu.VMEM(w.shape[1:], f32)] + scratch
+        scratch = [pltpu.VMEM(grad, f32)] + scratch
     return call(
-        functools.partial(attend_back_kernel, extra is not None, bool(aliases)),
+        functools.partial(attend_back_kernel, extra is not None, bool(aliases), far),
         rows,
         place,
         operands,
@@ -603,10 +657,11 @@
         "attend_back",
         6.5 * rows,
         aliases,
-    )
-
-
-def ffn(x_parts, contexts, weights, gains, place, rows, layer, more):
+        after,
+    )
+
+
+def ffn(x_parts, contexts, weights, gains, place, rows, layer, more, after=()):
     half, seq_len = contexts[0].shape[1:]
     stream = (rows, 2, half, seq_len)
     acts = (rows, 2, 2, 2 * half, seq_len)
@@ -649,10 +704,11 @@
         ],
         "ffn",
         10 * rows,
-    )
-
-
-def ffn_back(g_parts, saved, contexts, weights, gains, place, rows, layer, more):
+        after=after,
+    )
+
+
+def ffn_back(g_parts, saved, contexts, weights, gains, place, rows, layer, more, after=()):
     half, seq_len = contexts[0].shape[1:]
     if more:
         g_specs = [per_row(o.shape) for o in g_parts]
@@ -691,36 +747,127 @@
         ],
         "ffn_back",
         11.5 * rows,
-    )
-
-
-def finish(ffn_parts, qkv_parts, place, width):
-    operands = []
-    for layer in ffn_parts:
-        for parts in layer:
-            operands += parts
-    operands += qkv_parts
-    half = qkv_parts[0].shape[-1]
-    layers = len(ffn_parts)
+        after=after,
+    )
+
+
+def one_layer(shape, layer):
+    rest = (0,) * (len(shape) - 1)
+    return pl.BlockSpec((1,) + tuple(shape[1:]), lambda r, place: (layer,) + rest)
+
+
+def finish_ffn(parts, place, layer, layers, held=()):
+    operands = [p for part in parts for p in part]
+    half = operands[0].shape[-1] // 2
     outs = [
-        struct((layers, 3, width, half), f32),
         struct((layers, half, 2 * half), f32),
-        struct((layers, width, 4 * half), f32),
+        struct((layers, half // 2, 4 * half), f32),
         struct((layers, 2 * half, half), f32),
-        struct((layers, 2, 2 * half), f32),
     ]
     return call(
-        finish_kernel,
+        finish_ffn_kernel,
         1,
         place,
-        operands,
-        [whole(o.shape) for o in operands],
+        operands + list(held),
+        [whole(o.shape) for o in operands] + [pl.BlockSpec(memory_space=pl.ANY)] * len(held),
+        outs,
+        [one_layer(o.shape, layer) for o in outs],
+        [],
+        "finish_ffn",
+        3,
+        {7 + i: i for i in range(len(held))},
+    )
+
+
+def finish_qkv(parts, place, layers, width):
+    half = parts[0].shape[-1]
+    outs = [struct((layers, 3, width, half), f32), struct((layers, 2, 2 * half), f32)]
+    return call(
+        finish_qkv_kernel,
+        1,
+        place,
+        parts,
+        [whole(o.shape) for o in parts],
         outs,
         [whole(o.shape) for o in outs],
         [],
-        "finish",
-        6,
-    )
+        "finish_qkv",
+        3,
+    )
+
+
+def pack(weights, place, layer, after=()):
+    out_w, inner_w, outer_w, qkv_w = weights
+    half, wide = out_w.shape[1:]
+    three, depth, channels = qkv_w.shape[1:]
+    outs = [
+        struct((2, 3, half // 2, wide), bf16),
+        struct((3, half // 2, wide), bf16),
+        struct((three, depth // 2, channels), bf16),
+    ]
+    return call(
+        pack_kernel,
+        1,
+        place,
+        weights,
+        [one_layer(o.shape, layer) for o in weights],
+        outs,
+        [whole(o.shape) for o in outs],
+        [],
+        "pack",
+        3,
+        after=after,
+    )
+
+
+def hold(values, place, after):
+    anywhere = pl.BlockSpec(memory_space=pl.ANY)
+    return call(
+        lambda place, *refs: None,
+        1,
+        place,
+        values,
+        [anywhere] * len(values),
+        [struct(v.shape, v.dtype) for v in values],
+        [anywhere] * len(values),
+        [],
+        "hold",
+        1,
+        {i + 1: i for i in range(len(values))},
+        after,
+    )
+
+
+def fill_input_kernel(place, full_ref, own_ref, far_ref, out_ref):
+    column = pl.program_id(1)
+
+    @pl.when(column == 0)
+    def _():
+        out_ref[...] = own_ref[...]
+
+    @pl.when(column == 1)
+    def _():
+        out_ref[...] = far_ref[...]
+
+
+def fill_input(full, from_own, from_far, place, rows, seq_len):
+    half = from_own.shape[1]
+    block = pl.BlockSpec((seq_len, half), lambda r, j, place: (r, 0))
+    return pl.pallas_call(
+        fill_input_kernel,
+        out_shape=struct(full.shape, full.dtype),
+        grid_spec=pltpu.PrefetchScalarGridSpec(
+            num_scalar_prefetch=1,
+            grid=(rows, 2),
+            in_specs=[pl.BlockSpec(memory_space=pl.ANY), block, block],
+            out_specs=pl.BlockSpec(
+                (seq_len, half),
+                lambda r, j, place: (rows - place[OFFSET] + r, (1 - place[SELF]) ^ j),
+            ),
+        ),
+        input_output_aliases={1: 0},
+        name="fill_input",
+    )(place, full, from_own, from_far)
 
 
 def swap(values):
@@ -730,10 +877,6 @@
 def trade(values, stride):
     count = lax.axis_size("dp")
     return lax.ppermute(values, "dp", [(a, a ^ stride) for a in range(count)])
-
-
-def add(left, right):
-    return (left.astype(f32) + right.astype(f32)).astype(bf16)
 
 
 def far_strides():
@@ -746,18 +889,59 @@
     return strides
 
 
-def pack_weights(out_w, inner_w, outer_w):
-    half = out_w.shape[0]
-    wide = out_w.shape[1]
-    inner = jnp.stack([inner_w[:, :wide], inner_w[:, wide:]])
-    out = out_w.reshape(2, half // 2, wide)
-    outer = jnp.concatenate([outer_w[:half], outer_w[half:]], axis=1).reshape(2, half // 2, wide)
-    return jnp.stack([out, inner, outer], axis=1)
-
-
-def spread_out(total):
-    row = trade(total, 2)
-    return [total, row, trade(jnp.stack([total, row]), 1)]
+def sums(groups, place, after=(), casts=None):
+    operands = []
+    plan = []
+    for group in groups:
+        terms = []
+        for term in group:
+            value, *index = term if isinstance(term, tuple) else (term,)
+            terms.append((len(operands), tuple(index)))
+            operands.append(value)
+        plan.append(terms)
+    outs = [
+        struct(operands[terms[0][0]].shape[len(terms[0][1]) :], operands[terms[0][0]].dtype)
+        for terms in plan
+    ]
+
+    def kernel(place, *refs):
+        for terms, out in zip(plan, refs[len(operands) :]):
+            out[...] = functools.reduce(
+                jnp.add, [refs[at][...].astype(f32) for at, _ in terms]
+            ).astype(out.dtype)
+
+    def spec(value, index):
+        shape = value.shape[len(index) :]
+        return pl.BlockSpec(
+            (None,) * len(index) + tuple(shape),
+            lambda r, place: tuple(index) + (0,) * len(shape),
+        )
+
+    return call(
+        kernel,
+        1,
+        place,
+        operands,
+        [spec(operands[at], index) for terms in plan for at, index in terms],
+        outs,
+        [whole(o.shape) for o in outs],
+        [],
+        "sums",
+        2,
+        after=after,
+    )
+
+
+def first_sums(keep, got):
+    return [[(keep, s, 1), (got, s, 1)] for s in range(2)]
+
+
+def second_sums(keep, got, crossed):
+    return [
+        [(keep, s, 0, second), (got, s, 0, second), (crossed[s], second)]
+        for second in (1, 0)
+        for s in range(2)
+    ]
 
 
 def shards(
@@ -770,104 +954,152 @@
     rows = row_total // 2
     width = qkv_weight.shape[2]
     place = jnp.stack([side, 1 - side, side * rows, spot & 1, (spot >> 1) & 1])
-    core = place[CORE]
-
-    far_qkv = [swap(qkv_weight[i]) for i in range(layers)]
-    ffn_weights = []
-    for i in range(layers):
-        near = pack_weights(out_weight[i], inner_weight[i], outer_weight[i])
-        crossed = swap(lax.dynamic_index_in_dim(near, core, 0, False))
-        ffn_weights.append((near, crossed, trade(crossed, 1)))
-    x_tok = tokens
-    x_stream = None
-    saved_attend = []
-    saved_ffn = []
-    contexts = []
-    for i in range(layers):
-        held = [
-            attend(x_tok, qkv_weight, i, segments, place, rows, 0, i == 0),
-            attend(x_tok, far_qkv[i][None], 0, segments, place, rows, 1, i == 0),
-        ]
-        saved_attend.append(held)
-        contexts.append([h[5] for h in held])
-        x_parts = [h[0] for h in held] if i == 0 else [x_stream]
-        results = ffn(
-            x_parts, contexts[i], ffn_weights[i], norm_gains, place, rows, i, i < layers - 1
-        )
-        n1, r1, act, slope, n2, r2, x_tok, x_stream = results
-        saved_ffn.append((n2, r2, act, slope, n1, r1))
-    other_rows = (1 - side) * rows * seq_len
-    activations = lax.dynamic_update_slice(x_stream, swap(x_tok), (other_rows, jnp.int32(0)))
-
+    far_qkv = [None, None]
+    ffn_weights = [None, None]
+
+    def fetch(i, after=()):
+        weights = (out_weight, inner_weight, outer_weight, qkv_weight)
+        near, piece, part = pack(weights, place, i, after)
+        return near, swap(part), swap(piece)
+
+    packed, part, piece = fetch(0)
+    near = attend(tokens, (qkv_weight,), segments, place, rows, 0, 0)
+    (part,) = hold([part], place, [near[5]])
+    far_qkv[0] = (part, trade(part, 1))
+    ffn_weights[0] = (packed, piece, trade(piece, 1))
+    far = attend(tokens, far_qkv[0], segments, place, rows, 1, 0, [near[5]])
+    held = [near, far]
+    packed, part, piece = fetch(1, [far[5], ffn_weights[0][1]])
+    ffn_weights[1] = (packed, piece, trade(piece, 1))
+    saved_attend = [held]
+    contexts = [[h[5] for h in held]]
+    n1, r1, act, slope, n2, r2, x_tok, x_stream = ffn(
+        [h[0] for h in held], contexts[0], ffn_weights[0], norm_gains, place, rows, 0, True
+    )
+    (part,) = hold([part], place, [x_tok])
+    far_qkv[1] = (part, trade(part, 1))
+    saved_ffn = [(n2, r2, act, slope, n1, r1)]
+    held = [
+        attend(x_tok, (qkv_weight,), segments, place, rows, 0, 1),
+        attend(x_tok, far_qkv[1], segments, place, rows, 1, 1),
+    ]
+    saved_attend.append(held)
+    contexts.append([h[5] for h in held])
+    n1, r1, act, slope, n2, r2, x_tok, x_full = ffn(
+        [x_stream], contexts[1], ffn_weights[1], norm_gains, place, rows, 1, False
+    )
+    saved_ffn.append((n2, r2, act, slope, n1, r1))
+    part = x_tok.shape[0] // 2
+    far_tok = [swap(x_tok[:part])]
     d_before, dc0, dc1, keep, send, gain1 = ffn_back(
         [cotangent], saved_ffn[1], contexts[1], ffn_weights[1], norm_gains, place, rows, 1, False
     )
-    late = reduce_parts(keep, send)
+
+    strides = far_strides()
+    orders = (strides, strides[::-1])
+    got = trade(send, 1)
     dx1, later1 = attend_back(
-        dc1, saved_attend[1][1], far_qkv[1][None], 0, d_before, place, rows, 1, None
-    )
+        dc1, saved_attend[1][1], far_qkv[1], d_before, place, rows, 1, 1, None, [far_tok[0]]
+    )
+    late = sums(first_sums(keep, got), place, [dx1])
+    crossed = [swap(late[0]), trade(late[1], 2)]
     dx0, later0 = attend_back(
-        dc0, saved_attend[1][0], qkv_weight, 1, d_before, place, rows, 0, None
-    )
+        dc0, saved_attend[1][0], (qkv_weight,), d_before, place, rows, 0, 1, None, late
+    )
+    late = sums(second_sums(keep, got, crossed), place, [dx0])
+    crossed = [trade(late[0], 2), swap(late[1])]
+    far_tok.append(swap(x_tok[part:]))
     d_before, dc0, dc1, keep, send, gain0 = ffn_back(
-        [dx0, dx1], saved_ffn[0], contexts[0], ffn_weights[0], norm_gains, place, rows, 0, True
-    )
-    early = reduce_parts(keep, send)
+        [dx0, dx1],
+        saved_ffn[0],
+        contexts[0],
+        ffn_weights[0],
+        norm_gains,
+        place,
+        rows,
+        0,
+        True,
+        late,
+    )
+    late = sums([[late[2 + s], crossed[s]] for s in range(2)], place, [d_before])
+    crossed = [trade(late[s], orders[s][0]) for s in range(2)]
+    got = trade(send, 1)
     dx1, full, keep1, send1 = attend_back(
         dc1,
         saved_attend[0][1],
-        far_qkv[0][None],
-        0,
+        far_qkv[0],
         d_before,
         place,
         rows,
         1,
+        0,
         (later1, gain0, gain1, None),
-    )
-    crossed = swap(add(keep1, trade(send1, 1)))
+        late + [far_tok[1]],
+    )
     far_dx1 = swap(dx1)
+    early = sums(
+        first_sums(keep, got) + [[late[s], crossed[s]] for s in range(2)], place, [dx1]
+    )
+    early, late = early[:2], early[2:]
+    crossed = [swap(early[0]), trade(early[1], 2)]
+    received = [trade(late[s], orders[s][1]) for s in range(2)]
+    far_part = sums([[keep1, trade(send1, 1)]], place, early)
+    far_part = swap(far_part[0])
     dx0, full, keep0, send0 = attend_back(
-        dc0, saved_attend[0][0], qkv_weight, 0, d_before, place, rows, 0, (later0, gain0, gain1, full)
+        dc0,
+        saved_attend[0][0],
+        (qkv_weight,),
+        d_before,
+        place,
+        rows,
+        0,
+        0,
+        (later0, gain0, gain1, full),
+        early,
     )
     core_part = trade(send0, 1)
     far_dx0 = swap(dx0)
-    total = add3(keep0[0], core_part[0], crossed[0])
-    total = add(total, trade(add3(keep0[1], core_part[1], crossed[1]), 2))
-    for stride in far_strides():
-        total = add(total, trade(total, stride))
-    qkv_parts = spread_out(total)
-    half = qkv_weight.shape[-1]
-    input_grad = lax.dynamic_update_slice(full, far_dx1, (other_rows, side * half))
-    input_grad = lax.dynamic_update_slice(input_grad, far_dx0, (other_rows, (1 - side) * half))
-    totals = finish([early, late], qkv_parts, place, width)
-    return (activations, input_grad, *totals)
-
-
-def add3(a, b, c):
-    return (a.astype(f32) + b.astype(f32) + c.astype(f32)).astype(bf16)
-
-
-def reduce_parts(keep, send):
-    received = trade(send, 1)
-    results = []
-    for s in range(2):
-        steps = [swap, lambda v: trade(v, 2)]
-        strides = far_strides()
-        if s == 1:
-            steps = steps[::-1]
-            strides = strides[::-1]
-        mine, got = keep[s], received[s]
-        crossed = steps[0](add(mine[1], got[1]))
-        low = add3(mine[0, 0], got[0, 0], crossed[0])
-        high = add3(mine[0, 1], got[0, 1], crossed[1])
-        total = add(low, steps[1](high))
-        for stride in strides:
-            total = add(total, trade(total, stride))
-        results.append(total)
-    both = jnp.stack(results)
-    row = trade(both, 2)
-    core = trade(jnp.stack([both, row]), 1)
-    return [[both[s], row[s], core[:, s]] for s in range(2)]
+    results = sums(
+        second_sums(keep, got, crossed) + [[late[s], received[s]] for s in range(2)],
+        place,
+        [dx0],
+    )
+    early, late = results[:4], results[4:]
+    for at in range(2, len(strides)):
+        late = sums([[late[s], trade(late[s], orders[s][at])] for s in range(2)], place)
+    crossed = [trade(early[0], 2), swap(early[1])]
+    late_row = [trade(v, 2) for v in late]
+    total = sums(
+        [[(keep0, y), (core_part, y), (far_part, y)] for y in (1, 0)], place, early[:1]
+    )
+    row = trade(total[0], 2)
+    early = sums([[early[2 + s], crossed[s]] for s in range(2)], place, [total[0]])
+    late_core = [trade(jnp.stack([a, b]), 1) for a, b in zip(late, late_row)]
+    total = sums([[total[1], row]], place, early)
+    for at in range(len(strides)):
+        crossed = [trade(early[s], orders[s][at]) for s in range(2)]
+        row = trade(total[0], strides[at])
+        early = sums([[early[s], crossed[s]] for s in range(2)], place, total)
+        total = sums([[total[0], row]], place, early)
+    early_row = [trade(v, 2) for v in early]
+    row = trade(total[0], 2)
+    grads = finish_ffn(
+        [[late[s], late_row[s], late_core[s]] for s in range(2)], place, 1, layers
+    )
+    early_core = [trade(jnp.stack([a, b]), 1) for a, b in zip(early, early_row)]
+    core_part = trade(jnp.stack([total[0], row]), 1)
+    input_grad = fill_input(full, far_dx0, far_dx1, place, rows, seq_len)
+    other_rows = (1 - side) * rows * seq_len
+    activations = x_full
+    for at in range(2):
+        activations = lax.dynamic_update_slice(
+            activations, far_tok[at], (other_rows + at * part, jnp.int32(0))
+        )
+    qkv_grad, gain_grad = finish_qkv([total[0], row, core_part], place, layers, width)
+    out_grad, inner_grad, outer_grad = finish_ffn(
+        [[early[s], early_row[s], early_core[s]] for s in range(2)], place, 0, layers, grads
+    )
+    return (activations, input_grad, qkv_grad, out_grad, inner_grad, outer_grad, gain_grad)
 
 
 def solution(mesh):

time: 489 us -> 367 us (0.75)
  the two profiles are of different devices: /device:TPU:0 before, /device:TPU:25 now
where the time goes in v3:
time: 367 us; the launch traced here: 360 us
  Pallas kernels  244 us (66%)
  starting transfers between devices  48.1 us (13%)
  waiting for transfers between devices  43.1 us (12%)
  local copies, waits for them, and re-layouts  22.9 us (6%)
    pallas_call x32, Pallas kernels, call(): pl.pallas_call(body, out_shape=outs, grid_spec=pltpu.PrefetchScalarGridSp...  240 us
    ppermute x33, starting transfers between devices, trade(): return lax.ppermute(values, 'dp', [(a, a ^ stride) for a in range(count)])  37.9 us
    ppermute x13, waiting for transfers between devices, swap(): return lax.ppermute(values, 'head', [(0, 1), (1, 0)])  25.4 us
    ppermute x33, waiting for transfers between devices, trade(): return lax.ppermute(values, 'dp', [(a, a ^ stride) for a in range(count)])  17.8 us
    unnamed x88, local copies, waits for them, and re-layouts  15.8 us
    ppermute x13, starting transfers between devices, swap(): return lax.ppermute(values, 'head', [(0, 1), (1, 0)])  10.2 us
  transfers between devices with their start and end apart: 46, of which 9 were waited for; matrix products, arithmetic and copies ran while one was open for 1% of the time, Pallas kernels for 58%

profile of v3, /device:TPU:25, one launch (start us, length us, event | category | flops | bytes accessed | tf_op | source)
XLA Modules:
  0.0 360.3 jit_solution(10825535280899835190)
XLA Ops:
  1.2 4.0 %pack.2 = (bf16[2,3,192,768]{3,2,1,0:T(8,128)(2,1)}, bf16[3,192,768]{2,1,0:T(8,128)(2,1)}, bf16[3,96,384]{2,1,0:T(8,128)(2,1)}) custom-call(s32[5]{0:T(128)} %stack.68.place, bf16[2,384,768]{2,1,0:T(8,128)(2,1)} %refs_0_.8, bf16[2,192,1536]{2,1,0:T(8,128)(2,1)} %refs_1_.7, bf16[2,768,384]{2,1,0:T(8,128)(2,1)} %refs_2_.7, bf16[2,3,192,384]{3,2,1,0:T(8,128)(2,1)} %refs_8_.3), custom_call_target="tpu_custom_call" | custom-call | flops 15000000512 | bytes 30000000 | tf_op jit(solution)/shard_map/pack/pallas_call | solution.py:534
  6.7 9.1 %attend.4 = (bf16[2,384,512]{2,1,0:T(8,128)(2,1)}, bf16[2,384,512]{2,1,0:T(8,128)(2,1)}, bf16[2,384,512]{2,1,0:T(8,128)(2,1)}, bf16[2,2,512,192]{3,2,1,0:T(8,128...) custom-call(s32[5]{0:T(128)} %stack.68.place, bf16[2048,768]{1,0:T(8,128)(2,1)} %refs_0_.7, ...), custom_call_target="tpu_custom_call" | custom-call | flops 46999998464 | bytes 94000000 | tf_op jit(solution)/shard_map/attend/pallas_call | solution.py:534
  20.4 9.1 %attend.5 = (bf16[2,384,512]{2,1,0:T(8,128)(2,1)}, bf16[2,384,512]{2,1,0:T(8,128)(2,1)}, bf16[2,384,512]{2,1,0:T(8,128)(2,1)}, bf16[2,2,512,192]{3,2,1,0:T(8,128...) custom-call(s32[5]{0:T(128)} %stack.68.place, bf16[2048,768]{1,0:T(8,128)(2,1)} %refs_0_.7, ...), custom_call_target="tpu_custom_call" | custom-call | flops 1000000000 | bytes 2000000 | tf_op jit(solution)/shard_map/attend/pallas_call | solution.py:534
  32.2 4.0 %pack.3 = (bf16[2,3,192,768]{3,2,1,0:T(8,128)(2,1)}, bf16[3,192,768]{2,1,0:T(8,128)(2,1)}, bf16[3,96,384]{2,1,0:T(8,128)(2,1)}) custom-call(s32[5]{0:T(128)} %stack.68.place, bf16[2,384,768]{2,1,0:T(8,128)(2,1)} %refs_0_.8, bf16[2,192,1536]{2,1,0:T(8,128)(2,1)} %refs_1_.7, bf16[2,768,384]{2,1,0:T(8,128)(2,1)} %refs_2_.7, bf16[2,3,192,384]{3,2,1,0:T(8,128)(2,1)} %refs_8_.3, ...), custom_call_target="tpu_custom_call" | custom-call | flops 15000000512 | bytes 30000000 | tf_op jit(solution)/shard_map/pack/pallas_call | solution.py:534
  38.6 20.7 %ffn.2 = (f32[2,2,384,512]{3,2,1,0:T(8,128)}, f32[2,1,512]{2,1,0:T(1,128)}, bf16[2,2,2,768,512]{4,3,2,1,0:T(8,128)(2,1)}, bf16[2,2,2,768,512]{4,3,2,1,0:T(8,128)...) custom-call(s32[5]{0:T(128)} %stack.68.place, ...), custom_call_target="tpu_custom_call" | custom-call | flops 99999997952 | bytes 200000000 | tf_op jit(solution)/shard_map/ffn/pallas_call | solution.py:534
  62.2 9.1 %attend.6 = (bf16[2,384,512]{2,1,0:T(8,128)(2,1)}, bf16[2,384,512]{2,1,0:T(8,128)(2,1)}, bf16[2,384,512]{2,1,0:T(8,128)(2,1)}, bf16[2,2,512,192]{3,2,1,0:T(8,128...) custom-call(s32[5]{0:T(128)} %stack.68.place, ...), custom_call_target="tpu_custom_call" | custom-call | flops 46999998464 | bytes 94000000 | tf_op jit(solution)/shard_map/attend/pallas_call | solution.py:534
  72.0 9.5 %attend.7 = (bf16[2,384,512]{2,1,0:T(8,128)(2,1)}, bf16[2,384,512]{2,1,0:T(8,128)(2,1)}, bf16[2,384,512]{2,1,0:T(8,128)(2,1)}, bf16[2,2,512,192]{3,2,1,0:T(8,128...) custom-call(s32[5]{0:T(128)} %stack.68.place, ...), custom_call_target="tpu_custom_call" | custom-call | flops 46999998464 | bytes 94000000 | tf_op jit(solution)/shard_map/attend/pallas_call | solution.py:534
  82.5 20.0 %ffn.3 = (f32[2,2,384,512]{3,2,1,0:T(8,128)}, f32[2,1,512]{2,1,0:T(1,128)}, bf16[2,2,2,768,512]{4,3,2,1,0:T(8,128)(2,1)}, bf16[2,2,2,768,512]{4,3,2,1,0:T(8,128)...) custom-call(s32[5]{0:T(128)} %stack.68.place, ...), custom_call_target="tpu_custom_call" | custom-call | flops 99999997952 | bytes 200000000 | tf_op jit(solution)/shard_map/ffn/pallas_call | solution.py:534
  106.4 25.4 %ffn_back.2 = (f32[2,2,384,512]{3,2,1,0:T(8,128)}, bf16[2,384,512]{2,1,0:T(8,128)(2,1)}, bf16[2,384,512]{2,1,0:T(8,128)(2,1)}, bf16[2,2,2,3,48,768]{5,4,3,2,1,0:...) custom-call(s32[5]{0:T(128)} %stack.68.place, bf16[2048,768]{1,0:T(8,128)(2,1)} %refs_0_.9, ...), custom_call_target="tpu_custom_call" | custom-call | flops 115000000512 | bytes 230000000 | tf_op jit(solution)/shard_map/ffn_back/pallas_call | solution.py:534
  132.9 7.7 %collective-permute-done.8.refs_10_ = bf16[512,768]{1,0:T(8,128)(2,1)S(1)} collective-permute-done((bf16[512,768]{1,0:T(8,128)(2,1)S(1)}, bf16[512,768]{1,0:T(8,128)(2,1)S(1)}, u32[]{:S(2)}, u32[]{:S(2)}) %collective-permute-start.8) | collective-permute-done | bytes 786464 | tf_op jit(solution)/shard_map/ppermute | solution.py:874
  141.5 12.8 %attend_back.4 = (f32[2,384,512]{2,1,0:T(8,128)}, f32[3,192,384]{2,1,0:T(8,128)}) custom-call(s32[5]{0:T(128)} %stack.68.place, bf16[2,384,512]{2,1,0:T(8,128)(2,1)} %get-tuple-element.142.refs_0_, bf16[2,384,512]{2,1,0:T(8,128)(2,1)} %get-tuple-element.122.refs_2_.refs_8_.refs_1_, bf16[2,2,2,384,768]{4,3,2,1,0:T(8,128)(2,1)} %get-tuple-element.143.refs_2_, ...), custom_call_target="tpu_custom_call" | custom-call | flops 65000001536 | bytes 130000000 | tf_op jit(solution)/shard_map/attend_back/pallas_call | solution.py:534
  159.6 3.1 sums.13
  165.2 12.9 %attend_back.5 = (f32[2,384,512]{2,1,0:T(8,128)}, f32[3,192,384]{2,1,0:T(8,128)}) custom-call(s32[5]{0:T(128)} %stack.68.place, bf16[2,384,512]{2,1,0:T(8,128)(2,1)} %get-tuple-element.133.refs_0_, bf16[2,384,512]{2,1,0:T(8,128)(2,1)} %get-tuple-element.120.refs_1_.refs_7_, bf16[2,2,2,384,768]{4,3,2,1,0:T(8,128)(2,1)} %get-tuple-element.134.refs_2_, ...), custom_call_target="tpu_custom_call" | custom-call | flops 65000001536 | bytes 130000000 | tf_op jit(solution)/shard_map/attend_back/pallas_call | solution.py:534
  179.1 3.5 sums.14
  183.1 25.1 %ffn_back.3 = (f32[2,2,384,512]{3,2,1,0:T(8,128)}, bf16[2,384,512]{2,1,0:T(8,128)(2,1)}, bf16[2,384,512]{2,1,0:T(8,128)(2,1)}, bf16[2,2,2,3,48,768]{5,4,3,2,1,0:...) custom-call(s32[5]{0:T(128)} %stack.68.place, ...), custom_call_target="tpu_custom_call" | custom-call | flops 115000000512 | bytes 230000000 | tf_op jit(solution)/shard_map/ffn_back/pallas_call | solution.py:534
  214.3 13.7 %attend_back.6 = (bf16[1024,384]{1,0:T(8,128)(2,1)}, bf16[2048,768]{1,0:T(8,128)(2,1)}, bf16[2,304,384]{2,1,0:T(8,128)(2,1)}, bf16[2,304,384]{2,1,0:T(8,128)(2,1)}) custom-call(s32[5]{0:T(128)} %stack.68.place, bf16[2,384,512]{2,1,0:T(8,128)(2,1)} %get-tuple-element.171.refs_0_, bf16[2,384,512]{2,1,0:T(8,128)(2,1)} %get-tuple-element.115.refs_3_.refs_4_.refs_9_.refs_1_, ...), custom_call_target="tpu_custom_call" | custom-call | flops 65000001536 | bytes 130000000 | tf_op jit(solution)/shard_map/attend_back/pallas_call | solution.py:534
  231.3 3.5 sums.16
  238.7 13.5 %attend_back.7 = (bf16[1024,384]{1,0:T(8,128)(2,1)}, bf16[2048,768]{1,0:T(8,128)(2,1)}, bf16[2,304,384]{2,1,0:T(8,128)(2,1)}, bf16[2,304,384]{2,1,0:T(8,128)(2,1)}) custom-call(s32[5]{0:T(128)} %stack.68.place, bf16[2,384,512]{2,1,0:T(8,128)(2,1)} %get-tuple-element.162.refs_0_, ...), custom_call_target="tpu_custom_call", output_to_operand_aliasing={{1}: (13, {})} | custom-call | flops 65000001536 | bytes 130000000 | tf_op jit(solution)/shard_map/attend_back/pallas_call | solution.py:534
  253.6 2.9 sums.17
  260.8 3.9 %sums.18 = (bf16[3,48,768]{2,1,0:T(8,128)(2,1)}, bf16[3,48,768]{2,1,0:T(8,128)(2,1)}, bf16[3,48,768]{2,1,0:T(8,128)(2,1)}, bf16[3,48,768]{2,1,0:T(8,128)(2,1)}, ...) custom-call(s32[5]{0:T(128)} %stack.68.place, ...), custom_call_target="tpu_custom_call" | custom-call | flops 10000000000 | bytes 20000000 | tf_op jit(solution)/shard_map/sums/pallas_call | solution.py:534
  268.6 3.1 sums.19
  271.7 4.0 %collective-permute-done.42.refs_1_ = bf16[3,48,768]{2,1,0:T(8,128)(2,1)S(1)} collective-permute-done((bf16[3,48,768]{2,1,0:T(8,128)(2,1)}, bf16[3,48,768]{2,1,0:T(8,128)(2,1)S(1)}, u32[]{:S(2)}, u32[]{:S(2)}) %collective-permute-start.42) | collective-permute-done | bytes 221216 | tf_op jit(solution)/shard_map/ppermute | solution.py:879
  276.0 13.9 %collective-permute-done.29.refs_3_ = bf16[3,48,768]{2,1,0:T(8,128)(2,1)S(1)} collective-permute-done((bf16[3,48,768]{2,1,0:T(8,128)(2,1)}, bf16[3,48,768]{2,1,0:T(8,128)(2,1)S(1)}, u32[]{:S(2)}, u32[]{:S(2)}) %collective-permute-start.29) | collective-permute-done | bytes 221216 | tf_op jit(solution)/shard_map/ppermute | solution.py:874
  290.8 3.3 collective-permute-start.43
  294.1 2.8 sums.20
  304.4 4.2 %fill_input.1 = bf16[2048,768]{1,0:T(8,128)(2,1)} custom-call(s32[5]{0:T(128)} %stack.68.place, bf16[2048,768]{1,0:T(8,128)(2,1)} %get-tuple-element.185.full_ref, bf16[1024,384]{1,0:T(8,128)(2,1)} %copy-done.2, bf16[1024,384]{1,0:T(8,128)(2,1)} %copy-done.1), custom_call_target="tpu_custom_call", output_to_operand_aliasing={{}: (1, {})} | custom-call | tf_op jit(solution)/shard_map/fill_input/pallas_call | solution.py:856
  317.9 8.3 %collective-permute-done.34.refs_1_ = bf16[3,48,768]{2,1,0:T(8,128)(2,1)S(1)} collective-permute-done((bf16[3,48,768]{2,1,0:T(8,128)(2,1)}, bf16[3,48,768]{2,1,0:T(8,128)(2,1)S(1)}, u32[]{:S(2)}, u32[]{:S(2)}) %collective-permute-start.34) | collective-permute-done | bytes 221216 | tf_op jit(solution)/shard_map/ppermute | solution.py:879
  331.8 3.0 collective-permute-done.33.refs_1_
  341.7 4.6 %collective-permute-start.41 = (bf16[2,3,48,768]{3,2,1,0:T(8,128)(2,1)S(1)}, bf16[2,3,48,768]{3,2,1,0:T(8,128)(2,1)}, u32[]{:S(2)}, u32[]{:S(2)}) collective-permute-start(bf16[2,3,48,768]{3,2,1,0:T(8,128)(2,1)S(1)} %pad_maximum_fusion.2), channel_id=1, source_target_pairs={{0,2},{2,0},{4,6},{6,4},{8,10},{10,8},{12,14},{14,12},{16,18},{18,... | collective-permute-start | bytes 1327112 | tf_op jit(solution)/shard_map/ppermute | solution.py:879
  346.3 4.2 %finish_ffn.2 = (f32[2,384,768]{2,1,0:T(8,128)}, f32[2,192,1536]{2,1,0:T(8,128)}, f32[2,768,384]{2,1,0:T(8,128)}) custom-call(s32[5]{0:T(128)} %stack.68.place, bf16[3,48,768]{2,1,0:T(8,128)(2,1)} %get-tuple-element.206.refs_0_, bf16[3,48,768]{2,1,0:T(8,128)(2,1)} %copy-done.7, bf16[2,3,48,768]{3,2,1,0:T(8,128)(2,1)} %collective-permute-done.43.refs_2_, ...), custom_call_target="tpu_custom_call" | custom-call | flops 15000000512 | bytes 30000000 | tf_op jit(solution)/shard_map/finish_ffn/pallas_call | solution.py:534
  351.6 4.2 %finish_ffn.3 = (f32[2,384,768]{2,1,0:T(8,128)}, f32[2,192,1536]{2,1,0:T(8,128)}, f32[2,768,384]{2,1,0:T(8,128)}) custom-call(s32[5]{0:T(128)} %stack.68.place, bf16[3,48,768]{2,1,0:T(8,128)(2,1)} %get-tuple-element.203.refs_2_.refs_0_, bf16[3,48,768]{2,1,0:T(8,128)(2,1)} %copy-done.11, ...), custom_call_target="tpu_custom_call", output_to_operand_aliasing={{0}: (7, {}), {1}: (8, {}), {2}: (9, {})} | custom-call | flops 15000000512 | bytes 30000000 | tf_op jit(solution)/shard_map/finish_ffn/pallas_call | solution.py:534
  356.6 3.2 finish_qkv.1
  (190 shorter events, 86.5 us)
Async XLA Ops:
  6.4 24.3 %collective-permute-start.2 = (bf16[3,192,768]{2,1,0:T(8,128)(2,1)}, bf16[3,192,768]{2,1,0:T(8,128)(2,1)S(1)}, u32[]{:S(2)}, u32[]{:S(2)}) collective-permute-start(bf16[3,192,768]{2,1,0:T(8,128)(2,1)} %get-tuple-element.117), channel_id=1, source_target_pairs={{0,1},{1,0},{2,3},{3,2},{4,5},{5,4},{6,7},{7,6},{8,9},{9,8},{10,11... | collective-permute-start | bytes 2654216 | tf_op jit(solution)/shard_map/ppermute | solution.py:874
  36.2 23.1 %collective-permute-start.4 = (bf16[3,96,384]{2,1,0:T(8,128)(2,1)}, bf16[3,96,384]{2,1,0:T(8,128)(2,1)S(1)}, u32[]{:S(2)}, u32[]{:S(2)}) collective-permute-start(bf16[3,96,384]{2,1,0:T(8,128)(2,1)} %get-tuple-element.121), channel_id=1, source_target_pairs={{0,1},{1,0},{2,3},{3,2},{4,5},{5,4},{6,7},{7,6},{8,9},{9,8},{10,11... | collective-permute-start | bytes 663560 | tf_op jit(solution)/shard_map/ppermute | solution.py:874
  37.4 33.9 %collective-permute-start.6 = (bf16[3,192,768]{2,1,0:T(8,128)(2,1)}, bf16[3,192,768]{2,1,0:T(8,128)(2,1)}, u32[]{:S(2)}, u32[]{:S(2)}) collective-permute-start(bf16[3,192,768]{2,1,0:T(8,128)(2,1)} %get-tuple-element.124), channel_id=1, source_target_pairs={{0,1},{1,0},{2,3},{3,2},{4,5},{5,4},{6,7},{7,6},{8,9},{9,8},{10,11... | collective-permute-start | bytes 2654216 | tf_op jit(solution)/shard_map/ppermute | solution.py:874
  104.9 51.5 %collective-permute-start.9 = (bf16[512,768]{1,0:T(8,128)(2,1)}, bf16[512,768]{1,0:T(8,128)(2,1)}, u32[]{:S(2)}, u32[]{:S(2)}) collective-permute-start(bf16[512,768]{1,0:T(8,128)(2,1)} %get-tuple-element.215), channel_id=1, source_target_pairs={{0,1},{1,0},{2,3},{3,2},{4,5},{5,4},{6,7},{7,6},{8,9},{9,8},{10,11... | collective-permute-start | bytes 2359304 | tf_op jit(solution)/shard_map/ppermute | solution.py:874
  106.1 34.5 %collective-permute-start.8 = (bf16[512,768]{1,0:T(8,128)(2,1)S(1)}, bf16[512,768]{1,0:T(8,128)(2,1)S(1)}, u32[]{:S(2)}, u32[]{:S(2)}) collective-permute-start(bf16[512,768]{1,0:T(8,128)(2,1)S(1)} %get-tuple-element.216), channel_id=1, source_target_pairs={{0,1},{1,0},{2,3},{3,2},{4,5},{5,4},{6,7},{7,6},{8,9},{9,8},{10,11... | collective-permute-start | bytes 2359304 | tf_op jit(solution)/shard_map/ppermute | solution.py:874
  131.8 26.6 %collective-permute-start.10 = (bf16[2,2,2,3,48,768]{5,4,3,2,1,0:T(8,128)(2,1)}, bf16[2,2,2,3,48,768]{5,4,3,2,1,0:T(8,128)(2,1)S(1)}, u32[]{:S(2)}, u32[]{:S(2)}) collective-permute-start(bf16[2,2,2,3,48,768]{5,4,3,2,1,0:T(8,128)(2,1)} %get-tuple-element.141), channel_id=1, source_target_pairs={{0,2},{2,0},{4,6},{6,4},{8,10},{10,8},{12,14},{14,12},{16,18},{18,... | collective-permute-start | bytes 5308424 | tf_op jit(solution)/shard_map/ppermute | solution.py:879
  162.7 15.4 %collective-permute-start.11 = (bf16[2,3,48,768]{3,2,1,0:T(8,128)(2,1)}, bf16[2,3,48,768]{3,2,1,0:T(8,128)(2,1)S(1)}, u32[]{:S(2)}, u32[]{:S(2)}) collective-permute-start(bf16[2,3,48,768]{3,2,1,0:T(8,128)(2,1)} %get-tuple-element.149.refs_9_), channel_id=1, source_target_pairs={{0,1},{1,0},{2,3},{3,2},{4,5},{5,4},{6,7},{7,6},{8,9},{9,8},{10,11... | collective-permute-start | bytes 1327112 | tf_op jit(solution)/shard_map/ppermute | solution.py:874
  163.9 14.2 %collective-permute-start.12 = (bf16[2,3,48,768]{3,2,1,0:T(8,128)(2,1)}, bf16[2,3,48,768]{3,2,1,0:T(8,128)(2,1)S(1)}, u32[]{:S(2)}, u32[]{:S(2)}) collective-permute-start(bf16[2,3,48,768]{3,2,1,0:T(8,128)(2,1)} %get-tuple-element.150.refs_10_), channel_id=1, source_target_pairs={{0,4},{2,6},{4,0},{6,2},{8,12},{10,14},{12,8},{14,10},{16,20},{18,... | collective-permute-start | bytes 1327112 | tf_op jit(solution)/shard_map/ppermute | solution.py:879
  182.6 28.1 %collective-permute-start.13 = (bf16[3,48,768]{2,1,0:T(8,128)(2,1)}, bf16[3,48,768]{2,1,0:T(8,128)(2,1)S(1)}, u32[]{:S(2)}, u32[]{:S(2)}) collective-permute-start(bf16[3,48,768]{2,1,0:T(8,128)(2,1)} %get-tuple-element.158.refs_14_), channel_id=1, source_target_pairs={{0,4},{2,6},{4,0},{6,2},{8,12},{10,14},{12,8},{14,10},{16,20},{18,... | collective-permute-start | bytes 663560 | tf_op jit(solution)/shard_map/ppermute | solution.py:879
  182.8 27.9 %collective-permute-start.14 = (bf16[3,48,768]{2,1,0:T(8,128)(2,1)}, bf16[3,48,768]{2,1,0:T(8,128)(2,1)S(1)}, u32[]{:S(2)}, u32[]{:S(2)}) collective-permute-start(bf16[3,48,768]{2,1,0:T(8,128)(2,1)} %get-tuple-element.159.refs_15_), channel_id=1, source_target_pairs={{0,1},{1,0},{2,3},{3,2},{4,5},{5,4},{6,7},{7,6},{8,9},{9,8},{10,11... | collective-permute-start | bytes 663560 | tf_op jit(solution)/shard_map/ppermute | solution.py:874
  208.1 21.9 %collective-permute-start.15 = (bf16[2,2,2,3,48,768]{5,4,3,2,1,0:T(8,128)(2,1)}, bf16[2,2,2,3,48,768]{5,4,3,2,1,0:T(8,128)(2,1)S(1)}, u32[]{:S(2)}, u32[]{:S(2)}) collective-permute-start(bf16[2,2,2,3,48,768]{5,4,3,2,1,0:T(8,128)(2,1)} %get-tuple-element.181), channel_id=1, source_target_pairs={{0,2},{2,0},{4,6},{6,4},{8,10},{10,8},{12,14},{14,12},{16,18},{18,... | collective-permute-start | bytes 5308424 | tf_op jit(solution)/shard_map/ppermute | solution.py:879
  214.2 15.8 %collective-permute-start.16 = (bf16[3,48,768]{2,1,0:T(8,128)(2,1)}, bf16[3,48,768]{2,1,0:T(8,128)(2,1)S(1)}, u32[]{:S(2)}, u32[]{:S(2)}) collective-permute-start(bf16[3,48,768]{2,1,0:T(8,128)(2,1)} %get-tuple-element.177.refs_13_.refs_4_), channel_id=1, source_target_pairs={{0,8},{2,10},{4,12},{6,14},{8,0},{10,2},{12,4},{14,6},{16,24},{18,... | collective-permute-start | bytes 663560 | tf_op jit(solution)/shard_map/ppermute | solution.py:879
  214.3 15.7 %collective-permute-start.17 = (bf16[3,48,768]{2,1,0:T(8,128)(2,1)}, bf16[3,48,768]{2,1,0:T(8,128)(2,1)S(1)}, u32[]{:S(2)}, u32[]{:S(2)}) collective-permute-start(bf16[3,48,768]{2,1,0:T(8,128)(2,1)} %get-tuple-element.178.refs_14_.refs_6_), channel_id=1, source_target_pairs={{0,16},{2,18},{4,20},{6,22},{8,24},{10,26},{12,28},{14,30},{16,0},... | collective-permute-start | bytes 663560 | tf_op jit(solution)/shard_map/ppermute | solution.py:879
  228.1 24.1 %collective-permute-start.21 = (bf16[2,304,384]{2,1,0:T(8,128)(2,1)}, bf16[2,304,384]{2,1,0:T(8,128)(2,1)S(1)}, u32[]{:S(2)}, u32[]{:S(2)}) collective-permute-start(bf16[2,304,384]{2,1,0:T(8,128)(2,1)} %get-tuple-element.190), channel_id=1, source_target_pairs={{0,2},{2,0},{4,6},{6,4},{8,10},{10,8},{12,14},{14,12},{16,18},{18,... | collective-permute-start | bytes 1400840 | tf_op jit(solution)/shard_map/ppermute | solution.py:879
  228.5 73.0 %collective-permute-start.19 = (bf16[1024,384]{1,0:T(8,128)(2,1)}, bf16[1024,384]{1,0:T(8,128)(2,1)S(1)}, u32[]{:S(2)}, u32[]{:S(2)}) collective-permute-start(bf16[1024,384]{1,0:T(8,128)(2,1)} %get-tuple-element.182.refs_8_), channel_id=1, source_target_pairs={{0,1},{1,0},{2,3},{3,2},{4,5},{5,4},{6,7},{7,6},{8,9},{9,8},{10,11... | collective-permute-start | bytes 2359304 | tf_op jit(solution)/shard_map/ppermute | solution.py:874
  234.8 21.6 %collective-permute-start.25 = (bf16[3,48,768]{2,1,0:T(8,128)(2,1)}, bf16[3,48,768]{2,1,0:T(8,128)(2,1)S(1)}, u32[]{:S(2)}, u32[]{:S(2)}) collective-permute-start(bf16[3,48,768]{2,1,0:T(8,128)(2,1)} %get-tuple-element.191.refs_12_), channel_id=1, source_target_pairs={{0,16},{2,18},{4,20},{6,22},{8,24},{10,26},{12,28},{14,30},{16,0},... | collective-permute-start | bytes 663560 | tf_op jit(solution)/shard_map/ppermute | solution.py:879
  237.2 22.1 %collective-permute-start.23 = (bf16[2,3,48,768]{3,2,1,0:T(8,128)(2,1)}, bf16[2,3,48,768]{3,2,1,0:T(8,128)(2,1)S(1)}, u32[]{:S(2)}, u32[]{:S(2)}) collective-permute-start(bf16[2,3,48,768]{3,2,1,0:T(8,128)(2,1)} %get-tuple-element.183.refs_13_.refs_2_), channel_id=1, source_target_pairs={{0,1},{1,0},{2,3},{3,2},{4,5},{5,4},{6,7},{7,6},{8,9},{9,8},{10,11... | collective-permute-start | bytes 1327112 | tf_op jit(solution)/shard_map/ppermute | solution.py:874
  237.4 22.5 %collective-permute-start.24 = (bf16[2,3,48,768]{3,2,1,0:T(8,128)(2,1)}, bf16[2,3,48,768]{3,2,1,0:T(8,128)(2,1)S(1)}, u32[]{:S(2)}, u32[]{:S(2)}) collective-permute-start(bf16[2,3,48,768]{3,2,1,0:T(8,128)(2,1)} %get-tuple-element.184.refs_14_.refs_3_), channel_id=1, source_target_pairs={{0,4},{2,6},{4,0},{6,2},{8,12},{10,14},{12,8},{14,10},{16,20},{18,... | collective-permute-start | bytes 1327112 | tf_op jit(solution)/shard_map/ppermute | solution.py:879
  259.3 43.9 %collective-permute-start.18 = (bf16[1024,384]{1,0:T(8,128)(2,1)S(1)}, bf16[1024,384]{1,0:T(8,128)(2,1)S(1)}, u32[]{:S(2)}, u32[]{:S(2)}) collective-permute-start(bf16[1024,384]{1,0:T(8,128)(2,1)S(1)} %copy-done.20), channel_id=1, source_target_pairs={{0,1},{1,0},{2,3},{3,2},{4,5},{5,4},{6,7},{7,6},{8,9},{9,8},{10,11... | collective-permute-start | bytes 2359304 | tf_op jit(solution)/shard_map/ppermute | solution.py:874
  264.7 25.2 %collective-permute-start.29 = (bf16[3,48,768]{2,1,0:T(8,128)(2,1)}, bf16[3,48,768]{2,1,0:T(8,128)(2,1)S(1)}, u32[]{:S(2)}, u32[]{:S(2)}) collective-permute-start(bf16[3,48,768]{2,1,0:T(8,128)(2,1)} %get-tuple-element.198), channel_id=1, source_target_pairs={{0,1},{1,0},{2,3},{3,2},{4,5},{5,4},{6,7},{7,6},{8,9},{9,8},{10,11... | collective-permute-start | bytes 663560 | tf_op jit(solution)/shard_map/ppermute | solution.py:874
  265.5 25.3 %collective-permute-start.28 = (bf16[3,48,768]{2,1,0:T(8,128)(2,1)}, bf16[3,48,768]{2,1,0:T(8,128)(2,1)}, u32[]{:S(2)}, u32[]{:S(2)}) collective-permute-start(bf16[3,48,768]{2,1,0:T(8,128)(2,1)} %get-tuple-element.193.refs_6_), channel_id=1, source_target_pairs={{0,4},{2,6},{4,0},{6,2},{8,12},{10,14},{12,8},{14,10},{16,20},{18,... | collective-permute-start | bytes 663560 | tf_op jit(solution)/shard_map/ppermute | solution.py:879
  275.7 21.2 %collective-permute-start.44 = (bf16[3,48,768]{2,1,0:T(8,128)(2,1)S(1)}, bf16[3,48,768]{2,1,0:T(8,128)(2,1)S(1)}, u32[]{:S(2)}, u32[]{:S(2)}) collective-permute-start(bf16[3,48,768]{2,1,0:T(8,128)(2,1)S(1)} %copy-done.6), channel_id=1, source_target_pairs={{0,4},{2,6},{4,0},{6,2},{8,12},{10,14},{12,8},{14,10},{16,20},{18,... | collective-permute-start | bytes 663560 | tf_op jit(solution)/shard_map/ppermute | solution.py:879
  290.8 55.5 %collective-permute-start.43 = (bf16[2,3,48,768]{3,2,1,0:T(8,128)(2,1)S(1)}, bf16[2,3,48,768]{3,2,1,0:T(8,128)(2,1)}, u32[]{:S(2)}, u32[]{:S(2)}) collective-permute-start(bf16[2,3,48,768]{3,2,1,0:T(8,128)(2,1)S(1)} %pad_maximum_fusion.3), channel_id=1, source_target_pairs={{0,2},{2,0},{4,6},{6,4},{8,10},{10,8},{12,14},{14,12},{16,18},{18,... | collective-permute-start | bytes 1327112 | tf_op jit(solution)/shard_map/ppermute | solution.py:879
  296.9 11.7 %collective-permute-start.31 = (bf16[3,48,768]{2,1,0:T(8,128)(2,1)}, bf16[3,48,768]{2,1,0:T(8,128)(2,1)}, u32[]{:S(2)}, u32[]{:S(2)}) collective-permute-start(bf16[3,48,768]{2,1,0:T(8,128)(2,1)} %get-tuple-element.199.refs_2_.refs_0_), channel_id=1, source_target_pairs={{0,8},{2,10},{4,12},{6,14},{8,0},{10,2},{12,4},{14,6},{16,24},{18,... | collective-permute-start | bytes 663560 | tf_op jit(solution)/shard_map/ppermute | solution.py:879
  298.3 11.3 %collective-permute-start.32 = (bf16[3,48,768]{2,1,0:T(8,128)(2,1)}, bf16[3,48,768]{2,1,0:T(8,128)(2,1)}, u32[]{:S(2)}, u32[]{:S(2)}) collective-permute-start(bf16[3,48,768]{2,1,0:T(8,128)(2,1)} %get-tuple-element.200.refs_3_.refs_2_), channel_id=1, source_target_pairs={{0,16},{2,18},{4,20},{6,22},{8,24},{10,26},{12,28},{14,30},{16,0},... | collective-permute-start | bytes 663560 | tf_op jit(solution)/shard_map/ppermute | solution.py:879
  301.5 44.8 %collective-permute-start.45 = (bf16[2,3,48,768]{3,2,1,0:T(8,128)(2,1)S(1)}, bf16[2,3,48,768]{3,2,1,0:T(8,128)(2,1)}, u32[]{:S(2)}, u32[]{:S(2)}) collective-permute-start(bf16[2,3,48,768]{3,2,1,0:T(8,128)(2,1)S(1)} %pad_maximum_fusion.4), channel_id=1, source_target_pairs={{0,2},{2,0},{4,6},{6,4},{8,10},{10,8},{12,14},{14,12},{16,18},{18,... | collective-permute-start | bytes 1327112 | tf_op jit(solution)/shard_map/ppermute | solution.py:879
  303.1 11.1 %collective-permute-start.30 = (bf16[304,384]{1,0:T(8,128)(2,1)}, bf16[304,384]{1,0:T(8,128)(2,1)S(1)}, u32[]{:S(2)}, u32[]{:S(2)}) collective-permute-start(bf16[304,384]{1,0:T(8,128)(2,1)} %sums.21.refs_4_.refs_0_), channel_id=1, source_target_pairs={{0,8},{2,10},{4,12},{6,14},{8,0},{10,2},{12,4},{14,6},{16,24},{18,... | collective-permute-start | bytes 700424 | tf_op jit(solution)/shard_map/ppermute | solution.py:879
  312.4 13.9 %collective-permute-start.34 = (bf16[3,48,768]{2,1,0:T(8,128)(2,1)}, bf16[3,48,768]{2,1,0:T(8,128)(2,1)S(1)}, u32[]{:S(2)}, u32[]{:S(2)}) collective-permute-start(bf16[3,48,768]{2,1,0:T(8,128)(2,1)} %get-tuple-element.201.refs_2_.refs_0_), channel_id=1, source_target_pairs={{0,16},{2,18},{4,20},{6,22},{8,24},{10,26},{12,28},{14,30},{16,0},... | collective-permute-start | bytes 663560 | tf_op jit(solution)/shard_map/ppermute | solution.py:879
  314.0 12.2 %collective-permute-start.35 = (bf16[3,48,768]{2,1,0:T(8,128)(2,1)}, bf16[3,48,768]{2,1,0:T(8,128)(2,1)S(1)}, u32[]{:S(2)}, u32[]{:S(2)}) collective-permute-start(bf16[3,48,768]{2,1,0:T(8,128)(2,1)} %get-tuple-element.202.refs_3_.refs_2_), channel_id=1, source_target_pairs={{0,8},{2,10},{4,12},{6,14},{8,0},{10,2},{12,4},{14,6},{16,24},{18,... | collective-permute-start | bytes 663560 | tf_op jit(solution)/shard_map/ppermute | solution.py:879
  317.3 17.5 %collective-permute-start.33 = (bf16[304,384]{1,0:T(8,128)(2,1)}, bf16[304,384]{1,0:T(8,128)(2,1)S(1)}, u32[]{:S(2)}, u32[]{:S(2)}) collective-permute-start(bf16[304,384]{1,0:T(8,128)(2,1)} %sums.23.refs_4_.refs_0_), channel_id=1, source_target_pairs={{0,16},{2,18},{4,20},{6,22},{8,24},{10,26},{12,28},{14,30},{16,0},... | collective-permute-start | bytes 700424 | tf_op jit(solution)/shard_map/ppermute | solution.py:879
  338.0 12.5 %collective-permute-start.36 = (bf16[304,384]{1,0:T(8,128)(2,1)}, bf16[304,384]{1,0:T(8,128)(2,1)S(1)}, u32[]{:S(2)}, u32[]{:S(2)}) collective-permute-start(bf16[304,384]{1,0:T(8,128)(2,1)} %sums.25.refs_0_), channel_id=1, source_target_pairs={{0,4},{2,6},{4,0},{6,2},{8,12},{10,14},{12,8},{14,10},{16,20},{18,... | collective-permute-start | bytes 700424 | tf_op jit(solution)/shard_map/ppermute | solution.py:879
  339.1 11.7 %collective-permute-start.39 = (bf16[2,3,48,768]{3,2,1,0:T(8,128)(2,1)S(1)}, bf16[2,3,48,768]{3,2,1,0:T(8,128)(2,1)S(1)}, u32[]{:S(2)}, u32[]{:S(2)}) collective-permute-start(bf16[2,3,48,768]{3,2,1,0:T(8,128)(2,1)S(1)} %pad_maximum_fusion.1), channel_id=1, source_target_pairs={{0,2},{2,0},{4,6},{6,4},{8,10},{10,8},{12,14},{14,12},{16,18},{18,... | collective-permute-start | bytes 1327112 | tf_op jit(solution)/shard_map/ppermute | solution.py:879
  (58 other events, 261.1 us)

commit v4 on v3

v4 whole, which is shorter than its diff:
```python
import functools
import jax
import jax.numpy as jnp
from jax import lax
from jax.experimental import pallas as pl
from jax.experimental.pallas import tpu as pltpu
from jax.sharding import PartitionSpec as P

HEAD_DIM = 64
QUERY_TILE = 256
REACH = 128

SELF, OTHER, OFFSET, CORE, ROW = range(5)

epsilon = 1e-12
masked_score = -1e30
f32 = jnp.float32
bf16 = jnp.bfloat16

NN = (((1,), (0,)), ((), ()))
NT = (((1,), (1,)), ((), ()))
TN = (((0,), (0,)), ((), ()))


def mm(left, right, dims):
    return lax.dot_general(left, right, dims, preferred_element_type=f32)


def key_start(tile, seq_len):
    return min(max(tile * QUERY_TILE - REACH, 0), seq_len - QUERY_TILE - REACH)


def live_keys(tile, piece, seq_len):
    window = QUERY_TILE + REACH
    first_query = tile * QUERY_TILE + piece * REACH
    start = key_start(tile, seq_len)
    low = max(first_query - REACH - start, 0)
    high = min(first_query + 2 * REACH - start, window)
    return low, high


def block_diagonal(parts):
    rows = []
    for index, part in enumerate(parts):
        empty = jnp.zeros_like(part)
        rows.append(
            jnp.concatenate([part if at == index else empty for at in range(len(parts))], axis=1)
        )
    return jnp.concatenate(rows, axis=0)


def fill_rows(middle, low, high, total):
    pieces = []
    if low > 0:
        pieces.append(jnp.zeros((low, middle.shape[1]), middle.dtype))
    pieces.append(middle)
    if high < total:
        pieces.append(jnp.zeros((total - high, middle.shape[1]), middle.dtype))
    return jnp.concatenate(pieces, axis=0) if len(pieces) > 1 else middle


def across(row):
    return jnp.broadcast_to(row, (128, row.shape[1])).T


def take_weights(place, far, refs):
    if not far:
        return (lambda s: refs[0][s]), refs[1:]
    crossed, traded, *refs = refs
    scr = refs.pop()

    @pl.when(pl.program_id(0) == 0)
    def _():
        scr[:, place[CORE]] = crossed[...]
        scr[:, 1 - place[CORE]] = traded[...]

    return (lambda s: scr[s].reshape(2 * scr.shape[2], scr.shape[3])), refs


def attend_kernel(far, place, x_ref, *refs):
    weight, refs = take_weights(place, far, refs)
    seg_ref, *refs = refs
    xt_ref, qt_ref, kt_ref, v_ref, p_ref, ct_ref = refs[-6:]
    seq_len, channels = x_ref.shape
    width = v_ref.shape[-1]
    window = QUERY_TILE + REACH
    heads = width // HEAD_DIM
    tiles = seq_len // QUERY_TILE
    x = x_ref[...]
    xt = x.T
    xt_ref[0, 0] = xt
    segq = seg_ref[pl.ds(place[OFFSET] + pl.program_id(0), 1), :].astype(f32)
    segk = across(segq)
    masks = {}
    for tile in range(tiles):
        start = key_start(tile, seq_len)
        for piece in range(QUERY_TILE // REACH):
            low, high = live_keys(tile, piece, seq_len)
            at = tile * QUERY_TILE + piece * REACH
            same = segk[start + low : start + high] == segq[:, at : at + REACH]
            masks[tile, piece] = jnp.where(same, 0.0, masked_score)
    for group in range(channels // width):
        span = slice(group * width, (group + 1) * width)
        xg = x[:, span]
        xtg = xt[span]
        wq, wk, wv = (weight(s)[:, span] for s in range(3))
        qt = mm(wq, xtg, TN).astype(bf16) * jnp.asarray(HEAD_DIM**-0.5, bf16)
        kt = mm(wk, xtg, TN).astype(bf16)
        vt = mm(wv, xtg, TN).astype(bf16)
        keys = mm(xg, wk, NN).astype(bf16)
        values = mm(xg, wv, NN).astype(bf16)
        qt_ref[0, 0, span] = qt
        kt_ref[0, 0, span] = kt * jnp.asarray(HEAD_DIM**-0.5, bf16)
        v_ref[0, 0, group] = values
        for tile in range(tiles):
            start = key_start(tile, seq_len)
            asked = slice(tile * QUERY_TILE, (tile + 1) * QUERY_TILE)
            spread = block_diagonal(
                [qt[i * HEAD_DIM : (i + 1) * HEAD_DIM, asked] for i in range(heads)]
            )
            scores = mm(keys[start : start + window], spread, NN)
            for i in range(heads):
                probs = []
                for piece in range(QUERY_TILE // REACH):
                    low, high = live_keys(tile, piece, seq_len)
                    at = i * QUERY_TILE + piece * REACH
                    s = scores[low:high, at : at + REACH] + masks[tile, piece]
                    top = jnp.max(s, axis=0, keepdims=True)
                    e = jnp.exp(s - top)
                    total = jnp.sum(e, axis=0, keepdims=True)
                    p = (e * (1.0 / total)).astype(bf16)
                    probs.append(fill_rows(p, low, high, window))
                probs = jnp.concatenate(probs, axis=1)
                p_ref[0, 0, group, tile, :, i * QUERY_TILE : (i + 1) * QUERY_TILE] = probs
                context = mm(
                    vt[i * HEAD_DIM : (i + 1) * HEAD_DIM, start : start + window], probs, NN
                )
                at = group * width + i * HEAD_DIM
                ct_ref[0, 0, at : at + HEAD_DIM, asked] = context.astype(bf16)


def attend_back_kernel(
    last,
    aliased,
    sides,
    rows,
    place,
    dc_ref,
    ct_ref,
    p_ref,
    qt_ref,
    kt_ref,
    v_ref,
    xt_ref,
    dz_ref,
    *refs,
):
    step = pl.program_id(0)
    row = step % rows
    if len(sides) == 2:
        near_ref, crossed, traded, *refs = refs
        scr = refs.pop()

        @pl.when(step == 0)
        def _():
            scr[0] = near_ref[0].reshape(scr.shape[1:])
            scr[1, :, place[CORE]] = crossed[...]
            scr[1, :, 1 - place[CORE]] = traded[...]

        def weight(s):
            rows_of = scr[step // rows, s]
            return rows_of.reshape(2 * rows_of.shape[1], rows_of.shape[2])

    else:
        weight, refs = take_weights(place, sides[0] == 1, refs)
    if last:
        later_ref, gain0_ref, gain1_ref, *refs = refs
        if aliased:
            _, *refs = refs
        dx_ref, full_ref, keep_ref, send_ref, grad_ref, ds_ref = refs
    else:
        dx_ref, grad_ref, ds_ref = refs
        grad_ref = grad_ref.at[0]
    channels, seq_len = xt_ref.shape[2:]
    width = v_ref.shape[-1]
    window = QUERY_TILE + REACH
    heads = width // HEAD_DIM
    tiles = seq_len // QUERY_TILE
    grads = [[], [], []]
    d_inputs = []
    for group in range(channels // width):
        span = slice(group * width, (group + 1) * width)
        dq_tiles = []
        dk_tiles = []
        dv_tiles = []
        for tile in range(tiles):
            start = key_start(tile, seq_len)
            asked = slice(tile * QUERY_TILE, (tile + 1) * QUERY_TILE)
            d_context = dc_ref[0, 0, span, asked]
            context = ct_ref[0, 0, span, asked]
            both = d_context.astype(f32) * context.astype(f32)
            spread_dc = block_diagonal(
                [d_context[i * HEAD_DIM : (i + 1) * HEAD_DIM] for i in range(heads)]
            )
            qt = qt_ref[0, 0, span, asked]
            spread_q = block_diagonal(
                [qt[i * HEAD_DIM : (i + 1) * HEAD_DIM] for i in range(heads)]
            )
            d_probs = mm(v_ref[0, 0, group, start : start + window], spread_dc, NN)
            dq_heads = []
            for i in range(heads):
                shared = jnp.sum(both[i * HEAD_DIM : (i + 1) * HEAD_DIM], axis=0, keepdims=True)
                for piece in range(QUERY_TILE // REACH):
                    low, high = live_keys(tile, piece, seq_len)
                    at = i * QUERY_TILE + piece * REACH
                    p = p_ref[0, 0, group, tile, low:high, at : at + REACH].astype(f32)
                    dp = d_probs[low:high, at : at + REACH]
                    ds = (p * (dp - shared[:, piece * REACH : (piece + 1) * REACH])).astype(bf16)
                    ds_ref[:, at : at + REACH] = fill_rows(ds, low, high, window)
                of_head = slice(group * width + i * HEAD_DIM, group * width + (i + 1) * HEAD_DIM)
                dq_heads.append(
                    mm(
                        kt_ref[0, 0, of_head, start : start + window],
                        ds_ref[:, i * QUERY_TILE : (i + 1) * QUERY_TILE],
                        NN,
                    )
                )
            dq_tiles.append(jnp.concatenate(dq_heads, axis=0))
            dk_tiles.append(mm(ds_ref[...], spread_q, NT))
            dv_tiles.append(mm(p_ref[0, 0, group, tile], spread_dc, NT))
        dq = jnp.concatenate(dq_tiles, axis=1).astype(bf16)
        dk = join_windows(dk_tiles, seq_len).astype(bf16)
        dv = join_windows(dv_tiles, seq_len).astype(bf16)
        xtg = xt_ref[0, 0, span]
        grads[0].append(mm(xtg, dq, NT))
        grads[1].append(mm(xtg, dk, NN))
        grads[2].append(mm(xtg, dv, NN))
        wq, wk, wv = (weight(s)[:, span] for s in range(3))
        d_inputs.append(
            dz_ref[0, 0, span] + mm(wq, dq, NN) + mm(wk, dk, NT) + mm(wv, dv, NT)
        )
    joined = [jnp.concatenate(parts, axis=1) for parts in grads]

    @pl.when(row == 0)
    def _():
        for s in range(3):
            grad_ref[s] = joined[s]

    @pl.when(row > 0)
    def _():
        for s in range(3):
            grad_ref[s] += joined[s]

    d_input = jnp.concatenate(d_inputs, axis=0)
    if not last:
        dx_ref[0, 0] = d_input
        return
    tok = d_input.astype(bf16).T
    dx_ref[...] = tok
    full_ref[...] = tok

    @pl.when(step == pl.num_programs(0) - 1)
    def _():
        piece = width // 4
        gain_rows = jnp.concatenate([gain0_ref[...], gain1_ref[...]], axis=0).astype(bf16)
        gain_rows = jnp.concatenate([gain_rows[:, :channels], gain_rows[:, channels:]], axis=0)
        for c, out_ref in enumerate((keep_ref, send_ref)):
            for y in range(2):
                at = ((place[CORE] ^ c) * 2 + (place[ROW] ^ y)) * piece
                at_rows = pl.ds(pl.multiple_of(at, piece), piece)
                for layer, source in enumerate((grad_ref, later_ref.at[0])):
                    for s in range(3):
                        out_ref[y, pl.ds((layer * 3 + s) * piece, piece)] = source[
                            s, at_rows
                        ].astype(bf16)
                out_ref[y, pl.ds(6 * piece, 16)] = gain_rows


def join_windows(pieces, seq_len):
    window = QUERY_TILE + REACH
    rows = []
    for at in range(0, seq_len, REACH):
        held = []
        for tile, piece in enumerate(pieces):
            start = key_start(tile, seq_len)
            if start <= at < start + window:
                held.append(piece[at - start : at - start + REACH])
        rows.append(functools.reduce(jnp.add, held))
    return jnp.concatenate(rows, axis=0)


def feature_mean(values):
    return jnp.sum(values, axis=0, keepdims=True) * (1.0 / values.shape[0])


def normalize(before):
    centered = before - feature_mean(before)
    inverse = lax.rsqrt(feature_mean(centered * centered) + epsilon)
    return centered * inverse, inverse


def normalize_back(gradient, gains, normal, inverse):
    scaled = gradient * gains
    return inverse * (scaled - feature_mean(scaled) - normal * feature_mean(scaled * normal))


def gather_far(place, x_ref, c_ref, scr):
    scr[place[CORE]] = x_ref[...]
    scr[1 - place[CORE]] = c_ref[...]


class Near:
    def __init__(self, out_ref, inner_ref, outer_ref):
        self.refs = out_ref, inner_ref, outer_ref

    def out(self):
        return self.refs[0][0]

    def inner(self, group):
        hidden = self.refs[1].shape[2] // 2
        return self.refs[1][0, :, group * hidden : (group + 1) * hidden]

    def outer(self, group):
        width = self.refs[2].shape[2] // 2
        return self.refs[2][0, :, group * width : (group + 1) * width]


class Far:
    def __init__(self, pack):
        self.pack = pack

    def rows(self, k):
        rows = self.pack[:, k]
        return rows.reshape(2 * rows.shape[1], rows.shape[2])

    def out(self):
        return self.rows(0)

    def inner(self, group):
        return self.pack[group, 1]

    def outer(self, group):
        rows = self.rows(2)
        half = rows.shape[1] // 2
        width = half // 2
        at = group * width
        return jnp.concatenate(
            [rows[:, at : at + width], rows[:, half + at : half + at + width]], axis=0
        )


def spread_gains(gains_ref, layer, g_scr):
    for i in range(2):
        g_scr[i] = across(gains_ref[layer, i : i + 1, :])


def wide_gain(g_scr, i, seq_len):
    return jnp.concatenate([g_scr[i]] * (seq_len // 128), axis=1)


def split(values):
    return values.reshape(2, values.shape[0] // 2, values.shape[1])


def join(values):
    return values.reshape(2 * values.shape[1], values.shape[2])


def up(first, weights, group):
    pre = mm(weights.inner(group), first, TN)
    below = 0.5 + 0.5 * lax.erf(pre * 0.7071067811865476)
    slope = below + pre * (jnp.exp(-0.5 * pre * pre) * 0.3989422804014327)
    return (pre * below).astype(bf16), slope.astype(bf16)


def ffn_kernel(layer, place, *refs):
    (xt_ref, ct_ref, out_ref, inner_ref, outer_ref, farx_ref, farc_ref, gains_ref, *refs) = refs
    (n1_ref, r1_ref, act_ref, slope_ref, n2_ref, r2_ref, tok_ref, next_ref, *refs) = refs
    z_scr, fb_scr, far_scr, g_scr = refs
    half, tokens = z_scr.shape[1:]
    width = half // 2
    sides = (place[SELF], place[OTHER])

    @pl.when(pl.program_id(0) == 0)
    def _():
        gather_far(place, farx_ref, farc_ref, far_scr)
        spread_gains(gains_ref, layer, g_scr)

    weights = (Near(out_ref, inner_ref, outer_ref), Far(far_scr))
    z_scr[...] = split(sum(mm(weights[j].out(), ct_ref[j, 0], TN) for j in range(2)))
    for j in range(2):
        z_scr[sides[j]] += xt_ref[j, 0].astype(f32)
    normal, inverse = normalize(join(z_scr[...]))
    n1_ref[0] = split(normal.astype(bf16))
    r1_ref[0] = inverse
    first = normal * wide_gain(g_scr, 0, tokens)
    z_scr[...] = split(first)
    fb_scr[...] = split(first.astype(bf16))
    for j in range(2):
        for group in range(2):
            span = slice(group * width, (group + 1) * width)
            act, slope = up(fb_scr[sides[j], span], weights[j], group)
            act_ref[0, j, group] = act
            slope_ref[0, j, group] = slope
            z_scr[sides[j], span] += mm(weights[j].outer(group), act, TN)
    normal, inverse = normalize(join(z_scr[...]))
    n2_ref[0] = split(normal.astype(bf16))
    r2_ref[0] = inverse
    output = normal * wide_gain(g_scr, 1, tokens)
    tok_ref[...] = output.astype(bf16).T
    next_ref[0] = split(output)


def down(place, weights, acc, d_scr, b_scr, f_scr, act_of, slope_of):
    half = d_scr.shape[1]
    width = half // 2
    sides = (place[SELF], place[OTHER])
    for j in range(2):
        outers = []
        for group in range(2):
            span = slice(group * width, (group + 1) * width)
            d_branch = b_scr[sides[j], span]
            outers.append(mm(act_of(j, group), d_branch, NT))
            d_act = mm(weights[j].outer(group), d_branch, NN)
            d_pre = (d_act * slope_of(j, group).astype(f32)).astype(bf16)
            acc[j, 1, span] += mm(f_scr[sides[j], span], d_pre, NT)
            d_scr[sides[j], span] += mm(weights[j].inner(group), d_pre, NN)
        acc[j, 2] += jnp.concatenate(
            [o[:half] for o in outers] + [o[half:] for o in outers], axis=1
        )


def into_attention(d_before, weights, acc, ct_ref, dc_ref):
    d_attention = d_before.astype(bf16)
    for j in range(2):
        acc[j, 0] += mm(ct_ref[j, 0], d_attention, NT)
        dc_ref[j, 0] = mm(weights[j].out(), d_attention, NN).astype(bf16)


def hand_out(place, acc, keep_ref, send_ref):
    piece = acc.shape[2] // 8
    for c, out_ref in enumerate((keep_ref, send_ref)):
        for s in range(2):
            for j in range(2):
                for y in range(2):
                    at = ((s * 2 + (place[CORE] ^ c)) * 2 + (place[ROW] ^ y)) * piece
                    rows = pl.ds(pl.multiple_of(at, piece), piece)
                    spot = j, y, s
                    for k in range(3):
                        out_ref[(*spot, k)] = acc[j, k, rows].astype(bf16)


def hand_out_gains(gain_acc, gain_ref):
    sums = [jnp.sum(gain_acc[i], axis=1, keepdims=True) for i in range(2)]
    lane = lax.broadcasted_iota(jnp.int32, gain_acc.shape[1:], 1)
    gain_ref[...] = jnp.where(lane == 0, sums[0], sums[1]).T[:4]


def ffn_last_kernel(layer, place, *refs):
    (x_ref, ct_ref, cot_ref, out_ref, inner_ref, outer_ref, *refs) = refs
    (farx_ref, farc_ref, gains_ref, tok_ref, full_ref, *refs) = refs
    (dz1_ref, dc_ref, keep_ref, send_ref, gain_ref, *refs) = refs
    (z_scr, fb_scr, b_scr, n_scr, act_scr, slope_scr, far_scr, g_scr, acc, gain_acc) = refs
    half, tokens = z_scr.shape[1:]
    width = half // 2
    sides = (place[SELF], place[OTHER])
    step = pl.program_id(0)

    @pl.when(step == 0)
    def _():
        gather_far(place, farx_ref, farc_ref, far_scr)
        spread_gains(gains_ref, layer, g_scr)
        acc[...] = jnp.zeros_like(acc)
        gain_acc[...] = jnp.zeros_like(gain_acc)

    weights = (Near(out_ref, inner_ref, outer_ref), Far(far_scr))
    attention = sum(mm(weights[j].out(), ct_ref[j, 0], TN) for j in range(2))
    normal, inverse1 = normalize(attention + join(x_ref[0]))
    n_scr[...] = normal
    first = normal * wide_gain(g_scr, 0, tokens)
    z_scr[...] = split(first)
    fb_scr[...] = split(first.astype(bf16))
    for j in range(2):
        for group in range(2):
            span = slice(group * width, (group + 1) * width)
            act, slope = up(fb_scr[sides[j], span], weights[j], group)
            act_scr[j, group] = act
            slope_scr[j, group] = slope
            z_scr[sides[j], span] += mm(weights[j].outer(group), act, TN)
    normal, inverse = normalize(join(z_scr[...]))
    gain = wide_gain(g_scr, 1, tokens)
    tok = (normal * gain).astype(bf16).T
    tok_ref[...] = tok
    full_ref[...] = tok

    g = cot_ref[...].T.astype(f32)
    gain_acc[1] += lane_sum(g * normal)
    d_second = normalize_back(g, gain, normal, inverse)
    z_scr[...] = split(d_second)
    b_scr[...] = split(d_second.astype(bf16))
    down(
        place,
        weights,
        acc,
        z_scr,
        b_scr,
        fb_scr,
        lambda j, group: act_scr[j, group],
        lambda j, group: slope_scr[j, group],
    )
    d_first = join(z_scr[...])
    normal = n_scr[...]
    gain_acc[0] += lane_sum(d_first * normal)
    d_before = normalize_back(d_first, wide_gain(g_scr, 0, tokens), normal, inverse1)
    dz1_ref[0] = split(d_before)
    into_attention(d_before, weights, acc, ct_ref, dc_ref)

    @pl.when(step == pl.num_programs(0) - 1)
    def _():
        hand_out(place, acc, keep_ref, send_ref)
        hand_out_gains(gain_acc, gain_ref)


def ffn_back_kernel(layer, place, *refs):
    (g_ref, n2_ref, r2_ref, act_ref, slope_ref, n1_ref, r1_ref, ct_ref, *refs) = refs
    (out_ref, inner_ref, outer_ref, farx_ref, farc_ref, gains_ref, *refs) = refs
    (dz1_ref, dc_ref, keep_ref, send_ref, gain_ref, *refs) = refs
    d_scr, b_scr, f_scr, far_scr, g_scr, acc, gain_acc = refs
    tokens = d_scr.shape[2]
    sides = (place[SELF], place[OTHER])
    step = pl.program_id(0)

    @pl.when(step == 0)
    def _():
        gather_far(place, farx_ref, farc_ref, far_scr)
        spread_gains(gains_ref, layer, g_scr)
        acc[...] = jnp.zeros_like(acc)
        gain_acc[...] = jnp.zeros_like(gain_acc)

    weights = (Near(out_ref, inner_ref, outer_ref), Far(far_scr))
    for j in range(2):
        d_scr[sides[j]] = g_ref[j, 0]
    g = join(d_scr[...])
    normal = join(n2_ref[0]).astype(f32)
    gain_acc[1] += lane_sum(g * normal)
    d_second = normalize_back(g, wide_gain(g_scr, 1, tokens), normal, r2_ref[0])
    d_scr[...] = split(d_second)
    b_scr[...] = split(d_second.astype(bf16))
    normal = join(n1_ref[0]).astype(f32)
    gain = wide_gain(g_scr, 0, tokens)
    f_scr[...] = split((normal * gain).astype(bf16))
    down(
        place,
        weights,
        acc,
        d_scr,
        b_scr,
        f_scr,
        lambda j, group: act_ref[0, j, group],
        lambda j, group: slope_ref[0, j, group],
    )
    d_first = join(d_scr[...])
    gain_acc[0] += lane_sum(d_first * normal)
    d_before = normalize_back(d_first, gain, normal, r1_ref[0])
    dz1_ref[0] = split(d_before)
    into_attention(d_before, weights, acc, ct_ref, dc_ref)

    @pl.when(step == pl.num_programs(0) - 1)
    def _():
        hand_out(place, acc, keep_ref, send_ref)
        hand_out_gains(gain_acc, gain_ref)


def lane_sum(values):
    chunks = [values[:, at : at + 128] for at in range(0, values.shape[1], 128)]
    return functools.reduce(jnp.add, chunks)


def placed_pieces(place, parts, size):
    mine, row, core = parts
    for c, y, value in ((0, 0, mine[...]), (0, 1, row[...]), (1, 0, core[0]), (1, 1, core[1])):
        yield ((place[CORE] ^ c) * 2 + (place[ROW] ^ y)) * size, value


def rows_at(at, size):
    return pl.ds(pl.multiple_of(at, size), size)


def finish_ffn_kernel(place, *refs):
    out_ref, inner_ref, outer_ref = refs[-3:]
    half, wide = out_ref.shape[1:]
    size = half // 8
    for at, value in placed_pieces(place, refs[:3], size):
        value = value.astype(f32)
        for s in range(2):
            low = s * (half // 2) + at
            out_ref[0, rows_at(low, size), :] = value[s, 0]
            inner_ref[0, rows_at(at, size), s * wide : (s + 1) * wide] = value[s, 1]
            outer_ref[0, rows_at(low, size), :] = value[s, 2][:, :half]
            outer_ref[0, rows_at(half + low, size), :] = value[s, 2][:, half:]


def finish_qkv_kernel(place, mine, row, core, qkv_ref, gain_ref):
    half = qkv_ref.shape[3]
    size = qkv_ref.shape[2] // 4
    for at, value in placed_pieces(place, (mine, row, core), size):
        for layer in range(2):
            for s in range(3):
                index = (layer * 3 + s) * size
                qkv_ref[layer, s, rows_at(at, size), :] = value[index : index + size].astype(f32)
    gains = mine[6 * size : 6 * size + 16].astype(f32)
    for layer in range(2):
        for i in range(2):
            at = layer * 4 + i
            gain_ref[layer, i : i + 1, :half] = gains[at : at + 1]
            gain_ref[layer, i : i + 1, half:] = gains[8 + at : 9 + at]


def pack_kernel(place, out_ref, inner_ref, low_ref, high_ref, qkv_ref, piece_ref, part_ref):
    half = low_ref.shape[2]
    piece_ref[0] = out_ref[0]
    piece_ref[1] = inner_ref[0]
    piece_ref[2, :, :half] = low_ref[0]
    piece_ref[2, :, half:] = high_ref[0]
    part_ref[...] = qkv_ref[0]


def whole(shape):
    return pl.BlockSpec(shape, lambda r, place: (0,) * len(shape))


def per_row(shape):
    rest = (0,) * (len(shape) - 1)
    return pl.BlockSpec((1,) + tuple(shape[1:]), lambda r, place: (r,) + rest)


def struct(shape, dtype):
    return jax.ShapeDtypeStruct(shape, dtype)


def call(
    kernel, rows, place, operands, in_specs, outs, out_specs, scratch, name, us, aliases=None, after=()
):
    count = len(operands)
    in_specs = list(in_specs) + [pl.BlockSpec(memory_space=pl.ANY)] * len(after)
    operands = tuple(operands) + tuple(after)

    def body(place, *refs):
        kernel(place, *refs[:count], *refs[count + len(after) :])

    results = pl.pallas_call(
        body,
        out_shape=outs,
        grid_spec=pltpu.PrefetchScalarGridSpec(
            num_scalar_prefetch=1,
            grid=(rows,),
            in_specs=in_specs,
            out_specs=out_specs,
            scratch_shapes=scratch,
        ),
        compiler_params=pltpu.CompilerParams(vmem_limit_bytes=64 * 2**20 - 2**16),
        cost_estimate=pl.CostEstimate(
            flops=int(us * 5e9), bytes_accessed=int(us * 1e7), transcendentals=0
        ),
        input_output_aliases=aliases or {},
        name=name,
    )(place, *operands)
    return list(results)


def per_side(shape, side):
    rest = (0,) * (len(shape) - 2)
    return pl.BlockSpec((1, 1) + tuple(shape[2:]), lambda r, place: (side, r) + rest)


def both_sides(shape, parts=1):
    middle = (0,) * (len(shape) - 3)
    return pl.BlockSpec(
        (2, 1) + tuple(shape[2:-1]) + (shape[-1] // parts,),
        lambda t, place: (0, t // parts, *middle, t % parts),
    )


def attend(x_tok, w, segments, place, rows, j, layer, us, held=(), after=()):
    row_total, seq_len = segments.shape
    far = j == 1
    channels = w[0].shape[-1]
    width = channels // 2
    heads = width // HEAD_DIM
    groups = channels // width
    tiles = seq_len // QUERY_TILE
    window = QUERY_TILE + REACH
    outs = [
        struct((2, rows, channels, seq_len), bf16),
        struct((2, rows, channels, seq_len), bf16),
        struct((2, rows, channels, seq_len), bf16),
        struct((2, rows, groups, seq_len, width), bf16),
        struct((2, rows, groups, tiles, window, heads * QUERY_TILE), bf16),
        struct((2, rows, channels, seq_len), bf16),
    ]
    if layer == 0:
        x_spec = pl.BlockSpec((seq_len, channels), lambda r, place: (place[OFFSET] + r, place[j]))
    else:
        x_spec = pl.BlockSpec((seq_len, channels), lambda r, place: (r, place[j]))
    operands = (x_tok, *w, segments)
    return call(
        functools.partial(attend_kernel, far),
        rows,
        place,
        operands + tuple(held),
        [x_spec, *weight_blocks(w, far, layer), whole(segments.shape)]
        + [pl.BlockSpec(memory_space=pl.ANY)] * len(held),
        outs,
        [per_side(o.shape, j) for o in outs],
        weight_scratch(w, far),
        "attend",
        us,
        {len(operands) + 1 + i: i for i in range(len(held))},
        after,
    )


def weight_blocks(w, far, layer):
    return [whole(o.shape) for o in w] if far else [layer_block(w[0].shape, layer)]


def weight_scratch(w, far):
    if not far:
        return []
    three, depth, channels = w[0].shape
    return [pltpu.VMEM((three, 2, depth, channels), bf16)]


def layer_block(shape, layer):
    rest = (0,) * (len(shape) - 1)
    return pl.BlockSpec((None,) + tuple(shape[1:]), lambda r, place: (layer,) + rest)


def attend_back(d_context, saved, w, d_before, place, rows, sides, layer, extra, us, after=()):
    xt, qt, kt, values, probs, ct = saved
    channels, seq_len = xt.shape[2:]
    window = QUERY_TILE + REACH
    width = values.shape[-1]
    heads = width // HEAD_DIM
    operands = (d_context, ct, probs, qt, kt, values, xt)
    scratch = [pltpu.VMEM((window, heads * QUERY_TILE), bf16)]
    grad = (3, width, channels)
    if len(sides) == 2:
        near, *far = w
        w_specs = [layer_block4(near.shape, layer)] + [whole(o.shape) for o in far]
        scratch += [pltpu.VMEM((2, 3, 2, width // 2, channels), bf16)]
    else:
        w_specs = weight_blocks(w, sides[0] == 1, layer)
        scratch += weight_scratch(w, sides[0] == 1)

    def side(t):
        return t // rows if len(sides) == 2 else sides[0]

    def one(shape):
        rest = (0,) * (len(shape) - 2)
        return pl.BlockSpec(
            (1, 1) + tuple(shape[2:]), lambda t, place: (side(t), t % rows) + rest
        )

    in_specs = [one(o.shape) for o in operands] + [
        pl.BlockSpec(
            (1, 1, channels, seq_len), lambda t, place: (t % rows, place[side(t)], 0, 0)
        ),
        *w_specs,
    ]
    operands += (d_before, *w)
    aliases = {}
    if extra is None:
        outs = [struct((2, rows, channels, seq_len), f32), struct((2,) + grad, f32)]
        out_specs = [
            one(outs[0].shape),
            pl.BlockSpec((1,) + grad, lambda t, place: (side(t), 0, 0, 0)),
        ]
    else:
        later, gain0, gain1, full = extra
        operands += (later, gain0, gain1)
        in_specs += [one_layer(later.shape, sides[0]), whole(gain0.shape), whole(gain1.shape)]
        if full is not None:
            aliases = {len(operands) + 1: 1}
            operands += (full,)
            in_specs.append(pl.BlockSpec(memory_space=pl.ANY))
        piece = struct((2, 6 * (width // 4) + 16, channels), bf16)
        outs = [
            struct((rows * seq_len, channels), bf16),
            struct((2 * rows * seq_len, 2 * channels), bf16),
            piece,
            piece,
        ]
        out_specs = [
            pl.BlockSpec((seq_len, channels), lambda r, place: (r, 0)),
            pl.BlockSpec(
                (seq_len, channels), lambda r, place: (place[OFFSET] + r, place[sides[0]])
            ),
            whole(piece.shape),
            whole(piece.shape),
        ]
        scratch = [pltpu.VMEM(grad, f32)] + scratch
    return call(
        functools.partial(attend_back_kernel, extra is not None, bool(aliases), sides, rows),
        len(sides) * rows,
        place,
        operands,
        in_specs,
        outs,
        out_specs,
        scratch,
        "attend_back",
        us,
        aliases,
        after,
    )


def layer_block4(shape, layer):
    rest = (0,) * (len(shape) - 1)
    return pl.BlockSpec((1,) + tuple(shape[1:]), lambda t, place: (layer,) + rest)


def per_part(shape, parts):
    middle = (0,) * (len(shape) - 2)
    return pl.BlockSpec(
        (1,) + tuple(shape[1:-1]) + (shape[-1] // parts,),
        lambda t, place: (t // parts, *middle, t % parts),
    )


def weight_specs(weights, layer):
    return [one_layer(o.shape, layer) for o in weights[:3]] + [whole(o.shape) for o in weights[3:]]


def ffn(xts, contexts, weights, gains, place, rows, layer, us):
    half, seq_len = contexts.shape[2:]
    parts = 1
    tokens = seq_len // parts
    stream = (rows, 2, half, seq_len)
    acts = (rows, 2, 2, 2 * half, seq_len)
    outs = [
        struct(stream, bf16),
        struct((rows, 1, seq_len), f32),
        struct(acts, bf16),
        struct(acts, bf16),
        struct(stream, bf16),
        struct((rows, 1, seq_len), f32),
        struct((rows * seq_len, 2 * half), bf16),
        struct(stream, f32),
    ]
    out_specs = [per_part(o.shape, parts) for o in outs]
    out_specs[6] = pl.BlockSpec((tokens, 2 * half), lambda t, place: (t, 0))
    return call(
        functools.partial(ffn_kernel, layer),
        rows * parts,
        place,
        (xts, contexts, *weights, gains),
        [both_sides(xts.shape, parts), both_sides(contexts.shape, parts)]
        + weight_specs(weights, layer)
        + [whole(gains.shape)],
        outs,
        out_specs,
        [
            pltpu.VMEM((2, half, tokens), f32),
            pltpu.VMEM((2, half, tokens), bf16),
            pltpu.VMEM((2,) + weights[3].shape, bf16),
            pltpu.VMEM((2, 2 * half, 128), f32),
        ],
        "ffn",
        us,
    )


def sum_shapes(half):
    piece = struct((2, 2, 2, 3, half // 8, 2 * half), bf16)
    return [piece, piece, struct((4, 2 * half), f32)]


def sum_scratch(weights, half):
    return [
        pltpu.VMEM((2,) + weights[3].shape, bf16),
        pltpu.VMEM((2, 2 * half, 128), f32),
        pltpu.VMEM((2, 3, half, 2 * half), f32),
        pltpu.VMEM((2, 2 * half, 128), f32),
    ]


def ffn_last(x, contexts, cotangent, weights, gains, place, rows, layer, us):
    half, seq_len = contexts.shape[2:]
    wide = 2 * half
    outs = [
        struct((rows * seq_len, wide), bf16),
        struct((2 * rows * seq_len, wide), bf16),
        struct((rows, 2, half, seq_len), f32),
        struct(contexts.shape, bf16),
        *sum_shapes(half),
    ]
    own = pl.BlockSpec((seq_len, wide), lambda r, place: (place[OFFSET] + r, 0))
    out_specs = (
        [pl.BlockSpec((seq_len, wide), lambda r, place: (r, 0)), own]
        + [per_row(outs[2].shape), both_sides(outs[3].shape)]
        + [whole(o.shape) for o in outs[4:]]
    )
    stream = (2, half, seq_len)
    acts = (2, 2, wide, seq_len)
    return call(
        functools.partial(ffn_last_kernel, layer),
        rows,
        place,
        (x, contexts, cotangent, *weights, gains),
        [per_row(x.shape), both_sides(contexts.shape), own]
        + weight_specs(weights, layer)
        + [whole(gains.shape)],
        outs,
        out_specs,
        [
            pltpu.VMEM(stream, f32),
            pltpu.VMEM(stream, bf16),
            pltpu.VMEM(stream, bf16),
            pltpu.VMEM((wide, seq_len), f32),
            pltpu.VMEM(acts, bf16),
            pltpu.VMEM(acts, bf16),
            *sum_scratch(weights, half),
        ],
        "ffn_last",
        us,
    )


def ffn_back(g, saved, contexts, weights, gains, place, rows, layer, us, after=()):
    half, seq_len = contexts.shape[2:]
    stream = (2, half, seq_len)
    outs = [
        struct((rows,) + stream, f32),
        struct(contexts.shape, bf16),
        *sum_shapes(half),
    ]
    out_specs = [per_row(outs[0].shape), both_sides(outs[1].shape)] + [
        whole(o.shape) for o in outs[2:]
    ]
    return call(
        functools.partial(ffn_back_kernel, layer),
        rows,
        place,
        (g, *saved, contexts, *weights, gains),
        [both_sides(g.shape)]
        + [per_row(o.shape) for o in saved]
        + [both_sides(contexts.shape)]
        + weight_specs(weights, layer)
        + [whole(gains.shape)],
        outs,
        out_specs,
        [
            pltpu.VMEM(stream, f32),
            pltpu.VMEM(stream, bf16),
            pltpu.VMEM(stream, bf16),
            *sum_scratch(weights, half),
        ],
        "ffn_back",
        us,
        after=after,
    )


def one_layer(shape, layer):
    rest = (0,) * (len(shape) - 1)
    return pl.BlockSpec((1,) + tuple(shape[1:]), lambda r, place: (layer,) + rest)


def finish_ffn(parts, place, layer, layers, held=()):
    operands = list(parts)
    half = operands[0].shape[-1] // 2
    outs = [
        struct((layers, half, 2 * half), f32),
        struct((layers, half // 2, 4 * half), f32),
        struct((layers, 2 * half, half), f32),
    ]
    return call(
        finish_ffn_kernel,
        1,
        place,
        operands + list(held),
        [whole(o.shape) for o in operands] + [pl.BlockSpec(memory_space=pl.ANY)] * len(held),
        outs,
        [one_layer(o.shape, layer) for o in outs],
        [],
        "finish_ffn",
        3,
        {4 + i: i for i in range(len(held))},
    )


def finish_qkv(parts, place, layers, width):
    half = parts[0].shape[-1]
    outs = [struct((layers, 3, width, half), f32), struct((layers, 2, 2 * half), f32)]
    return call(
        finish_qkv_kernel,
        1,
        place,
        parts,
        [whole(o.shape) for o in parts],
        outs,
        [whole(o.shape) for o in outs],
        [],
        "finish_qkv",
        3,
    )


def pack(weights, place, layer, after=()):
    out_w, inner_w, outer_w, qkv_w = weights
    half, wide = out_w.shape[1:]
    three, depth, channels = qkv_w.shape[1:]
    rows = half // 2
    outs = [struct((3, rows, wide), bf16), struct((three, depth // 2, channels), bf16)]
    return call(
        pack_kernel,
        1,
        place,
        (out_w, inner_w, outer_w, outer_w, qkv_w),
        [
            pl.BlockSpec((1, rows, wide), lambda r, place: (layer, place[CORE], 0)),
            pl.BlockSpec((1, depth, wide), lambda r, place: (layer, 0, place[CORE])),
            pl.BlockSpec((1, rows, half), lambda r, place: (layer, place[CORE], 0)),
            pl.BlockSpec((1, rows, half), lambda r, place: (layer, 2 + place[CORE], 0)),
            pl.BlockSpec((1, three, depth // 2, channels), lambda r, place: (layer, 0, place[CORE], 0)),
        ],
        outs,
        [whole(o.shape) for o in outs],
        [],
        "pack",
        3,
        after=after,
    )


def hold(values, place, after):
    anywhere = pl.BlockSpec(memory_space=pl.ANY)
    return call(
        lambda place, *refs: None,
        1,
        place,
        values,
        [anywhere] * len(values),
        [struct(v.shape, v.dtype) for v in values],
        [anywhere] * len(values),
        [],
        "hold",
        1,
        {i + 1: i for i in range(len(values))},
        after,
    )


def fill_input_kernel(place, full_ref, own_ref, far_ref, out_ref):
    column = pl.program_id(1)

    @pl.when(column == 0)
    def _():
        out_ref[...] = own_ref[...]

    @pl.when(column == 1)
    def _():
        out_ref[...] = far_ref[...]


def fill_input(full, from_own, from_far, place, rows, seq_len):
    half = from_own.shape[1]
    block = pl.BlockSpec((seq_len, half), lambda r, j, place: (r, 0))
    return pl.pallas_call(
        fill_input_kernel,
        out_shape=struct(full.shape, full.dtype),
        grid_spec=pltpu.PrefetchScalarGridSpec(
            num_scalar_prefetch=1,
            grid=(rows, 2),
            in_specs=[pl.BlockSpec(memory_space=pl.ANY), block, block],
            out_specs=pl.BlockSpec(
                (seq_len, half),
                lambda r, j, place: (rows - place[OFFSET] + r, (1 - place[SELF]) ^ j),
            ),
        ),
        input_output_aliases={1: 0},
        name="fill_input",
    )(place, full, from_own, from_far)


def swap(values):
    return lax.ppermute(values, "head", [(0, 1), (1, 0)])


def cross(values):
    count = lax.axis_size("dp")
    return lax.ppermute(
        values, ("dp", "head"), [(2 * a + h, 2 * (a ^ 2) + 1 - h) for a in range(count) for h in range(2)]
    )


def scatter(parts):
    return [swap(parts[0]), trade(parts[1], 2), cross(parts[2])]


SHARES = ((1, 0), (0, 1), (1, 1))


def trade(values, stride):
    count = lax.axis_size("dp")
    return lax.ppermute(values, "dp", [(a, a ^ stride) for a in range(count)])


def far_strides():
    count = lax.axis_size("dp")
    strides = []
    stride = 4
    while stride < count:
        strides.append(stride)
        stride *= 2
    return strides


def sums(groups, place, after=(), casts=None):
    operands = []
    plan = []
    for group in groups:
        terms = []
        for term in group:
            value, *index = term if isinstance(term, tuple) else (term,)
            terms.append((len(operands), tuple(index)))
            operands.append(value)
        plan.append(terms)
    outs = [
        struct(operands[terms[0][0]].shape[len(terms[0][1]) :], operands[terms[0][0]].dtype)
        for terms in plan
    ]

    def kernel(place, *refs):
        for terms, out in zip(plan, refs[len(operands) :]):
            out[...] = functools.reduce(
                jnp.add, [refs[at][...].astype(f32) for at, _ in terms]
            ).astype(out.dtype)

    def spec(value, index):
        shape = value.shape[len(index) :]
        return pl.BlockSpec(
            (None,) * len(index) + tuple(shape),
            lambda r, place: tuple(index) + (0,) * len(shape),
        )

    return call(
        kernel,
        1,
        place,
        operands,
        [spec(operands[at], index) for terms in plan for at, index in terms],
        outs,
        [whole(o.shape) for o in outs],
        [],
        "sums",
        2,
        after=after,
    )


def add(*terms):
    return functools.reduce(jnp.add, [t.astype(f32) for t in terms]).astype(bf16)


def shards(
    tokens, segments, qkv_weight, out_weight, inner_weight, outer_weight, norm_gains, cotangent
):
    side = lax.axis_index("head").astype(jnp.int32)
    spot = lax.axis_index("dp").astype(jnp.int32)
    layers = qkv_weight.shape[0]
    row_total, seq_len = segments.shape
    rows = row_total // 2
    width = qkv_weight.shape[2]
    place = jnp.stack([side, 1 - side, side * rows, spot & 1, (spot >> 1) & 1])
    weights = (out_weight, inner_weight, outer_weight)
    one = (qkv_weight,)
    far_qkv = [None, None]
    ffn_weights = [None, None]

    piece, part = pack((*weights, qkv_weight), place, 0)
    part, piece = swap(part), swap(piece)
    near = attend(tokens, one, segments, place, rows, 0, 0, 9)
    (part,) = hold([part], place, [near[5]])
    far_qkv[0] = (part, trade(part, 1))
    next_piece, next_part = pack((*weights, qkv_weight), place, 1, [near[5]])
    held = attend(tokens, far_qkv[0], segments, place, rows, 1, 0, 0.2, near, [next_piece])
    piece, next_piece, next_part = hold([piece, next_piece, next_part], place, [held[5]])
    ffn_weights[0] = (*weights, piece, trade(piece, 1))
    part, piece = swap(next_part), swap(next_piece)
    ffn_weights[1] = (*weights, piece, trade(piece, 1))
    saved_attend = [held]
    n1, r1, act, slope, n2, r2, x_tok, x_stream = ffn(
        held[0], held[5], ffn_weights[0], norm_gains, place, rows, 0, 20
    )
    saved_ffn = (n2, r2, act, slope, n1, r1)
    (part,) = hold([part], place, [x_tok])
    far_qkv[1] = (part, trade(part, 1))
    near = attend(x_tok, one, segments, place, rows, 0, 1, 9)
    held = attend(x_tok, far_qkv[1], segments, place, rows, 1, 1, 9, near)
    saved_attend.append(held)
    x_tok, activations, d_before, d_context, keep, send, gain1 = ffn_last(
        x_stream, held[5], cotangent, ffn_weights[1], norm_gains, place, rows, 1, 40
    )

    strides = far_strides()
    far_tok = swap(x_tok)
    got = trade(send, 1)
    dx, later = attend_back(
        d_context, held, one + far_qkv[1], d_before, place, rows, (0, 1), 1, None, 0.2
    )
    parts = sums([[(keep, *at), (got, *at)] for at in SHARES], place, [dx])
    crossed = scatter(parts)
    d_before, d_context, next_keep, next_send, gain0 = ffn_back(
        dx, saved_ffn, saved_attend[0][5], ffn_weights[0], norm_gains, place, rows, 0, 0.2, parts
    )
    (late,) = sums([[(keep, 0, 0), (got, 0, 0), *crossed]], place, [d_before])
    late_got = trade(late, strides[0])
    keep, send = next_keep, next_send
    got = trade(send, 1)
    dx1, full, keep1, send1 = attend_back(
        d_context,
        saved_attend[0],
        far_qkv[0],
        d_before,
        place,
        rows,
        (1,),
        0,
        (later, gain0, gain1, None),
        13,
        [late, far_tok],
    )
    core1 = trade(send1, 1)
    *parts, late = sums(
        [[(keep, *at), (got, *at)] for at in SHARES] + [[late, late_got]], place, [dx1]
    )
    crossed = scatter(parts)
    late_got = trade(late, strides[1])
    dx0, full, keep0, send0 = attend_back(
        d_context,
        saved_attend[0],
        one,
        d_before,
        place,
        rows,
        (0,),
        0,
        (later, gain0, gain1, full),
        13,
        parts + [late],
    )
    core0 = trade(send0, 1)
    (core1,) = hold([core1], place, [dx0])
    shares = [add(keep1[0], core1[0]), add(keep0[1], core0[1]), add(keep1[1], core1[1])]
    shares = scatter(shares)
    total = add(keep0[0], core0[0], *shares)
    early = [add(keep[0, 0, s], got[0, 0, s], *[c[s] for c in crossed]) for s in range(2)]
    orders = (strides, strides[::-1])
    late = add(late, late_got)
    for stride in strides[2:]:
        late = add(late, trade(late, stride))
    late_row = trade(late, 2)
    late_core = trade(jnp.stack([late, late_row]), 1)
    dx0, dx1 = hold([dx0, dx1], place, early)
    far_dx0, far_dx1 = swap(dx0), swap(dx1)
    for at in range(len(strides)):
        early = [add(early[s], trade(early[s], orders[s][at])) for s in range(2)]
        total = add(total, trade(total, strides[at]))
    early = jnp.stack(early)
    grads = finish_ffn([late, late_row, late_core], place, 1, layers)
    early, total = hold([early, total], place, [grads[0]])
    early_row = trade(early, 2)
    row = trade(total, 2)
    input_grad = fill_input(full, far_dx0, far_dx1, place, rows, seq_len)
    both = jnp.stack([early, early_row])
    (both,) = hold([both], place, [input_grad])
    early_core = trade(both, 1)
    core_part = trade(jnp.stack([total, row]), 1)
    other_rows = (1 - side) * rows * seq_len
    activations = lax.dynamic_update_slice(activations, far_tok, (other_rows, jnp.int32(0)))
    out_grad, inner_grad, outer_grad = finish_ffn(
        [early, early_row, early_core], place, 0, layers, grads
    )
    qkv_grad, gain_grad = finish_qkv([total, row, core_part], place, layers, width)
    return (activations, input_grad, qkv_grad, out_grad, inner_grad, outer_grad, gain_grad)


def solution(mesh):
    return jax.shard_map(
        shards,
        mesh=mesh,
        in_specs=(
            P("dp", None),
            P("dp", None),
            P(None, None, None, "head"),
            P(None, "head", None),
            P(None, None, "head"),
            P(None, None, "head"),
            P(),
            P("dp", None),
        ),
        out_specs=(
            P("dp", None),
            P("dp", None),
            P(None, None, None, "head"),
            P(None, "head", None),
            P(None, None, "head"),
            P(None, None, "head"),
            P(),
        ),
        check_vma=False,
    )
```

time: 367 us -> 305 us (0.83)
  the two profiles are of different devices: /device:TPU:25 before, /device:TPU:0 now
where the time goes in v4:
time: 305 us; the launch traced here: 299 us
  Pallas kernels  198 us (65%)
  waiting for transfers between devices  47.6 us (16%)
  starting transfers between devices  32.8 us (11%)
  other arithmetic  15.1 us (5%)
  local copies, waits for them, and re-layouts  4.07 us (1%)
    pallas_call x25, Pallas kernels, call(): pl.pallas_call(body, out_shape=outs, grid_spec=pltpu.PrefetchScalarGridSp...  194 us
    ppermute x25, waiting for transfers between devices, trade(): return lax.ppermute(values, 'dp', [(a, a ^ stride) for a in range(count)])  41.3 us
    ppermute x25, starting transfers between devices, trade(): return lax.ppermute(values, 'dp', [(a, a ^ stride) for a in range(count)])  17.7 us
    convert_element_type x9, other arithmetic, add(): functools.reduce(jnp.add, [t.astype(f32) for t in terms]).astype(bf16)  12.3 us
    ppermute x10, starting transfers between devices, swap(): return lax.ppermute(values, 'head', [(0, 1), (1, 0)])  12.3 us
  transfers between devices with their start and end apart: 38, of which 11 were waited for; matrix products, arithmetic and copies ran while one was open for 6% of the time, Pallas kernels for 53%

profile of v4, /device:TPU:0, one launch (start us, length us, event | category | flops | bytes accessed | tf_op | source)
XLA Modules:
  0.0 299.0 jit_solution(6106385259964180535)
XLA Ops:
  1.3 2.9 pack.2
  4.2 2.9 collective-permute-start
  7.2 9.1 %attend.4 = (bf16[2,2,384,512]{3,2,1,0:T(8,128)(2,1)}, bf16[2,2,384,512]{3,2,1,0:T(8,128)(2,1)}, bf16[2,2,384,512]{3,2,1,0:T(8,128)(2,1)}, bf16[2,2,2,512,192]{4...) custom-call(s32[5]{0:T(128)} %stack.59.place, ...), custom_call_target="tpu_custom_call" | custom-call | flops 44999999488 | bytes 90000000 | tf_op jit(solution)/shard_map/attend/pallas_call | solution.py:651
  17.0 2.9 pack.3
  19.9 9.1 %attend.5 = (bf16[2,2,384,512]{3,2,1,0:T(8,128)(2,1)}, bf16[2,2,384,512]{3,2,1,0:T(8,128)(2,1)}, bf16[2,2,384,512]{3,2,1,0:T(8,128)(2,1)}, bf16[2,2,2,512,192]{4...) custom-call(s32[5]{0:T(128)} %stack.59.place, ...), custom_call_target="tpu_custom_call", output_to_operand_aliasing={{0}: (5, {}), {1}: (6, {}), {2}: (7, {}), {3}: (8, {}), {4}... | custom-call | flops 1000000000 | bytes 2000000 | tf_op jit(solution)/shard_map/attend/pallas_call | solution.py:651
  29.0 2.8 collective-permute-done.2.refs_0_
  35.3 20.2 %ffn.1 = (bf16[2,2,384,512]{3,2,1,0:T(8,128)(2,1)}, f32[2,1,512]{2,1,0:T(1,128)}, bf16[2,2,2,768,512]{4,3,2,1,0:T(8,128)(2,1)}, bf16[2,2,2,768,512]{4,3,2,1,0:T(...) custom-call(s32[5]{0:T(128)} %stack.59.place, ...), custom_call_target="tpu_custom_call" | custom-call | flops 99999997952 | bytes 200000000 | tf_op jit(solution)/shard_map/ffn/pallas_call | solution.py:651
  56.4 9.1 %attend.6 = (bf16[2,2,384,512]{3,2,1,0:T(8,128)(2,1)}, bf16[2,2,384,512]{3,2,1,0:T(8,128)(2,1)}, bf16[2,2,384,512]{3,2,1,0:T(8,128)(2,1)}, bf16[2,2,2,512,192]{4...) custom-call(s32[5]{0:T(128)} %stack.59.place, ...), custom_call_target="tpu_custom_call" | custom-call | flops 44999999488 | bytes 90000000 | tf_op jit(solution)/shard_map/attend/pallas_call | solution.py:651
  65.9 9.1 %attend.7 = (bf16[2,2,384,512]{3,2,1,0:T(8,128)(2,1)}, bf16[2,2,384,512]{3,2,1,0:T(8,128)(2,1)}, bf16[2,2,384,512]{3,2,1,0:T(8,128)(2,1)}, bf16[2,2,2,512,192]{4...) custom-call(s32[5]{0:T(128)} %stack.59.place, ...), custom_call_target="tpu_custom_call", output_to_operand_aliasing={{0}: (5, {}), {1}: (6, {}), {2}: (7, {}), {3}: (8, {}), {4}... | custom-call | flops 44999999488 | bytes 90000000 | tf_op jit(solution)/shard_map/attend/pallas_call | solution.py:651
  75.1 32.8 %ffn_last.1 = (bf16[1024,768]{1,0:T(8,128)(2,1)}, bf16[2048,768]{1,0:T(8,128)(2,1)}, f32[2,2,384,512]{3,2,1,0:T(8,128)}, bf16[2,2,384,512]{3,2,1,0:T(8,128)(2,1)...) custom-call(s32[5]{0:T(128)} %stack.59.place, ...), custom_call_target="tpu_custom_call" | custom-call | flops 199999995904 | bytes 400000000 | tf_op jit(solution)/shard_map/ffn_last/pallas_call | solution.py:651
  109.8 21.0 %attend_back.3 = (f32[2,2,384,512]{3,2,1,0:T(8,128)}, f32[2,3,192,384]{3,2,1,0:T(8,128)}) custom-call(s32[5]{0:T(128)} %stack.59.place, bf16[2,2,384,512]{3,2,1,0:T(8,128)(2,1)} %get-tuple-element.113.refs_0_, bf16[2,2,384,512]{3,2,1,0:T(8,128)(2,1)} %get-tuple-element.109.refs_1_, bf16[2,2,2,2,384,768]{5,4,3,2,1,0:T(8,128)(2,1)} %get-tuple-element.114.refs_2_, ...), custom_call_target="tpu_custom_call" | custom-call | flops 1000000000 | bytes 2000000 | tf_op jit(solution)/shard_map/attend_back/pallas_call | solution.py:651
  130.8 3.5 %sums.3 = (bf16[2,3,48,768]{3,2,1,0:T(8,128)(2,1)}, bf16[2,3,48,768]{3,2,1,0:T(8,128)(2,1)}, bf16[2,3,48,768]{3,2,1,0:T(8,128)(2,1)}) custom-call(s32[5]{0:T(128)} %stack.59.place, bf16[2,2,2,3,48,768]{5,4,3,2,1,0:T(8,128)(2,1)} %get-tuple-element.127.refs_0_.refs_2_.refs_4_, bf16[2,2,2,3,48,768]{5,4,3,2,1,0:T(8,128)(2,1)} %collective-permute-done.9.refs_1_.refs_3_.refs_5_, ...), custom_call_target="tpu_custom_call" | custom-call | flops 10000000000 | bytes 20000000 | tf_op jit(solution)/shard_map/sums/pallas_call | solution.py:651
  137.8 23.8 %ffn_back.1 = (f32[2,2,384,512]{3,2,1,0:T(8,128)}, bf16[2,2,384,512]{3,2,1,0:T(8,128)(2,1)}, bf16[2,2,2,3,48,768]{5,4,3,2,1,0:T(8,128)(2,1)}, bf16[2,2,2,3,48,768]{5,4,3,2,1,0:T(8,128)(2,1)}, f32[4,768]{1,0:T(4,128)}) custom-call(s32[5]{0:T(128)} %stack.59.place, f32[2,2,384,512]{3,2,1,0:T(8,128)} %get-tuple-element.120.refs_6_.refs_0_, ...), custom_call_target="tpu_custom_call" | custom-call | flops 1000000000 | bytes 2000000 | tf_op jit(solution)/shard_map/ffn_back/pallas_call | solution.py:651
  161.7 3.5 %collective-permute-done.12.refs_4_ = bf16[2,3,48,768]{3,2,1,0:T(8,128)(2,1)} collective-permute-done((bf16[2,3,48,768]{3,2,1,0:T(8,128)(2,1)}, bf16[2,3,48,768]{3,2,1,0:T(8,128)(2,1)}, u32[]{:S(2)}, u32[]{:S(2)}) %collective-permute-start.12) | collective-permute-done | bytes 442400 | tf_op jit(solution)/shard_map/ppermute | solution.py:1094
  165.2 3.3 %sums.4.refs_13_.refs_6_ = bf16[2,3,48,768]{3,2,1,0:T(8,128)(2,1)} custom-call(s32[5]{0:T(128)} %stack.59.place, bf16[2,2,2,3,48,768]{5,4,3,2,1,0:T(8,128)(2,1)} %get-tuple-element.127.refs_0_.refs_2_.refs_4_, bf16[2,2,2,3,48,768]{5,4,3,2,1,0:T(8,128)(2,1)} %collective-permute-done.9.refs_1_.refs_3_.refs_5_, ...), custom_call_target="tpu_custom_call" | custom-call | flops 10000000000 | bytes 20000000 | tf_op jit(solution)/shard_map/sums/pallas_call | solution.py:651
  170.0 13.6 %attend_back.4 = (bf16[1024,384]{1,0:T(8,128)(2,1)}, bf16[2048,768]{1,0:T(8,128)(2,1)}, bf16[2,304,384]{2,1,0:T(8,128)(2,1)}, bf16[2,304,384]{2,1,0:T(8,128)(2,1)}) custom-call(s32[5]{0:T(128)} %stack.59.place, bf16[2,2,384,512]{3,2,1,0:T(8,128)(2,1)} %get-tuple-element.132.refs_0_, bf16[2,2,384,512]{3,2,1,0:T(8,128)(2,1)} %get-tuple-element.96.refs_3_.refs_1_.refs_7_, ...), custom_call_target="tpu_custom_call" | custom-call | flops 65000001536 | bytes 130000000 | tf_op jit(solution)/shard_map/attend_back/pallas_call | solution.py:651
  183.8 4.0 %sums.5 = (bf16[2,3,48,768]{3,2,1,0:T(8,128)(2,1)}, bf16[2,3,48,768]{3,2,1,0:T(8,128)(2,1)}, bf16[2,3,48,768]{3,2,1,0:T(8,128)(2,1)}, bf16[2,3,48,768]{3,2,1,0:T(8,128)(2,1)}) custom-call(s32[5]{0:T(128)} %stack.59.place, bf16[2,2,2,3,48,768]{5,4,3,2,1,0:T(8,128)(2,1)} %get-tuple-element.142.refs_0_.refs_2_.refs_4_, ...), custom_call_target="tpu_custom_call" | custom-call | flops 10000000000 | bytes 20000000 | tf_op jit(solution)/shard_map/sums/pallas_call | solution.py:651
  187.7 2.6 collective-permute-start.31
  193.8 13.4 %attend_back.5 = (bf16[1024,384]{1,0:T(8,128)(2,1)}, bf16[2048,768]{1,0:T(8,128)(2,1)}, bf16[2,304,384]{2,1,0:T(8,128)(2,1)}, bf16[2,304,384]{2,1,0:T(8,128)(2,1)}) custom-call(s32[5]{0:T(128)} %stack.59.place, bf16[2,2,384,512]{3,2,1,0:T(8,128)(2,1)} %get-tuple-element.132.refs_0_, ...), custom_call_target="tpu_custom_call", output_to_operand_aliasing={{1}: (13, {})} | custom-call | flops 65000001536 | bytes 130000000 | tf_op jit(solution)/shard_map/attend_back/pallas_call | solution.py:651
  208.0 2.2 fusion.5
  213.6 2.7 fusion.3
  219.7 2.1 collective-permute-start.32
  222.9 3.7 %collective-permute-done.20 = bf16[3,48,768]{2,1,0:T(8,128)(2,1)} collective-permute-done((bf16[3,48,768]{2,1,0:T(8,128)(2,1)}, bf16[3,48,768]{2,1,0:T(8,128)(2,1)}, u32[]{:S(2)}, u32[]{:S(2)}) %collective-permute-start.20) | collective-permute-done | bytes 221216 | tf_op jit(solution)/shard_map/ppermute | solution.py:1108
  233.6 4.3 %collective-permute-done.27 = bf16[304,384]{1,0:T(8,128)(2,1)S(1)} collective-permute-done((bf16[304,384]{1,0:T(8,128)(2,1)S(1)}, bf16[304,384]{1,0:T(8,128)(2,1)S(1)}, u32[]{:S(2)}, u32[]{:S(2)}) %collective-permute-start.27) | collective-permute-done | bytes 233504 | tf_op jit(solution)/shard_map/ppermute | solution.py:1108
  242.3 9.6 %collective-permute-done.29 = bf16[304,384]{1,0:T(8,128)(2,1)S(1)} collective-permute-done((bf16[304,384]{1,0:T(8,128)(2,1)S(1)}, bf16[304,384]{1,0:T(8,128)(2,1)S(1)}, u32[]{:S(2)}, u32[]{:S(2)}) %collective-permute-start.29) | collective-permute-done | bytes 233504 | tf_op jit(solution)/shard_map/ppermute | solution.py:1108
  253.0 11.6 %collective-permute-done.30 = bf16[304,384]{1,0:T(8,128)(2,1)S(1)} collective-permute-done((bf16[304,384]{1,0:T(8,128)(2,1)S(1)}, bf16[304,384]{1,0:T(8,128)(2,1)S(1)}, u32[]{:S(2)}, u32[]{:S(2)}) %collective-permute-start.30) | collective-permute-done | bytes 233504 | tf_op jit(solution)/shard_map/ppermute | solution.py:1108
  265.3 4.1 %finish_ffn.2 = (f32[2,384,768]{2,1,0:T(8,128)}, f32[2,192,1536]{2,1,0:T(8,128)}, f32[2,768,384]{2,1,0:T(8,128)}) custom-call(s32[5]{0:T(128)} %stack.59.place, bf16[2,3,48,768]{3,2,1,0:T(8,128)(2,1)} %add_convert_fusion.refs_0_, bf16[2,3,48,768]{3,2,1,0:T(8,128)(2,1)} %copy-done.4, bf16[2,2,3,48,768]{4,3,2,1,0:T(8,128)(2,1)} %collective-permute-done.33.refs_2_), custom_call_target="tpu_custom_call" | custom-call | flops 15000000512 | bytes 30000000 | tf_op jit(solution)/shard_map/finish_ffn/pallas_call | solution.py:651
  272.2 2.7 constant_dynamic-update-slice_fusion
  274.9 4.3 %fill_input.1.refs_1_ = bf16[2048,768]{1,0:T(8,128)(2,1)} custom-call(s32[5]{0:T(128)} %stack.59.place, bf16[2048,768]{1,0:T(8,128)(2,1)} %get-tuple-element.149.full_ref, bf16[1024,384]{1,0:T(8,128)(2,1)} %collective-permute-done.18.own_ref, bf16[1024,384]{1,0:T(8,128)(2,1)} %collective-permute-done.19.far_ref), custom_call_target="tpu_custom_call", output_to_operand_aliasing={{}: (1, {})} | custom-call | tf_op jit(solution)/shard_map/fill_input/pallas_call | solution.py:1071
  279.2 8.3 %collective-permute-done.34.refs_1_ = bf16[304,384]{1,0:T(8,128)(2,1)S(1)} collective-permute-done((bf16[304,384]{1,0:T(8,128)(2,1)}, bf16[304,384]{1,0:T(8,128)(2,1)S(1)}, u32[]{:S(2)}, u32[]{:S(2)}) %collective-permute-start.34) | collective-permute-done | bytes 233504 | tf_op jit(solution)/shard_map/ppermute | solution.py:1108
  291.4 3.3 %finish_qkv.1 = (f32[2,3,192,384]{3,2,1,0:T(8,128)}, f32[2,2,768]{2,1,0:T(2,128)}) custom-call(s32[5]{0:T(128)} %stack.59.place, bf16[304,384]{1,0:T(8,128)(2,1)} %get-tuple-element.158.refs_0_, bf16[304,384]{1,0:T(8,128)(2,1)} %copy-done.7, bf16[2,304,384]{2,1,0:T(8,128)(2,1)} %collective-permute-done.35.refs_2_), custom_call_target="tpu_custom_call" | custom-call | flops 15000000512 | bytes 30000000 | tf_op jit(solution)/shard_map/finish_qkv/pallas_call | solution.py:651
  294.6 4.1 %finish_ffn.3 = (f32[2,384,768]{2,1,0:T(8,128)}, f32[2,192,1536]{2,1,0:T(8,128)}, f32[2,768,384]{2,1,0:T(8,128)}) custom-call(s32[5]{0:T(128)} %stack.59.place, bf16[2,3,48,768]{3,2,1,0:T(8,128)(2,1)} %get-tuple-element.160.refs_0_, bf16[2,3,48,768]{3,2,1,0:T(8,128)(2,1)} %copy-done.5, ...), custom_call_target="tpu_custom_call", output_to_operand_aliasing={{0}: (4, {}), {1}: (5, {}), {2}: (6, {})} | custom-call | flops 15000000512 | bytes 30000000 | tf_op jit(solution)/shard_map/finish_ffn/pallas_call | solution.py:651
  (103 shorter events, 45.3 us)
Async XLA Ops:
  4.2 12.0 %collective-permute-start = (bf16[3,96,384]{2,1,0:T(8,128)(2,1)}, bf16[3,96,384]{2,1,0:T(8,128)(2,1)}, u32[]{:S(2)}, u32[]{:S(2)}) collective-permute-start(bf16[3,96,384]{2,1,0:T(8,128)(2,1)} %get-tuple-element.87), channel_id=1, source_target_pairs={{0,1},{1,0},{2,3},{3,2},{4,5},{5,4},{6,7},{7,6},{8,9},{9,8},{10,11... | collective-permute-start | bytes 663560 | tf_op jit(solution)/shard_map/ppermute | solution.py:1089
  7.1 24.7 %collective-permute-start.2 = (bf16[3,192,768]{2,1,0:T(8,128)(2,1)}, bf16[3,192,768]{2,1,0:T(8,128)(2,1)}, u32[]{:S(2)}, u32[]{:S(2)}) collective-permute-start(bf16[3,192,768]{2,1,0:T(8,128)(2,1)} %get-tuple-element.97), channel_id=1, source_target_pairs={{0,1},{1,0},{2,3},{3,2},{4,5},{5,4},{6,7},{7,6},{8,9},{9,8},{10,11... | collective-permute-start | bytes 2654216 | tf_op jit(solution)/shard_map/ppermute | solution.py:1089
  32.6 23.0 %collective-permute-start.4 = (bf16[3,96,384]{2,1,0:T(8,128)(2,1)}, bf16[3,96,384]{2,1,0:T(8,128)(2,1)}, u32[]{:S(2)}, u32[]{:S(2)}) collective-permute-start(bf16[3,96,384]{2,1,0:T(8,128)(2,1)} %get-tuple-element.102), channel_id=1, source_target_pairs={{0,1},{1,0},{2,3},{3,2},{4,5},{5,4},{6,7},{7,6},{8,9},{9,8},{10,11... | collective-permute-start | bytes 663560 | tf_op jit(solution)/shard_map/ppermute | solution.py:1089
  34.4 31.1 %collective-permute-start.6 = (bf16[3,192,768]{2,1,0:T(8,128)(2,1)}, bf16[3,192,768]{2,1,0:T(8,128)(2,1)}, u32[]{:S(2)}, u32[]{:S(2)}) collective-permute-start(bf16[3,192,768]{2,1,0:T(8,128)(2,1)} %get-tuple-element.110), channel_id=1, source_target_pairs={{0,1},{1,0},{2,3},{3,2},{4,5},{5,4},{6,7},{7,6},{8,9},{9,8},{10,11... | collective-permute-start | bytes 2654216 | tf_op jit(solution)/shard_map/ppermute | solution.py:1089
  56.2 9.7 %collective-permute-start.5 = (bf16[3,96,384]{2,1,0:T(8,128)(2,1)}, bf16[3,96,384]{2,1,0:T(8,128)(2,1)}, u32[]{:S(2)}, u32[]{:S(2)}) collective-permute-start(bf16[3,96,384]{2,1,0:T(8,128)(2,1)} %hold.9.refs_1_.refs_9_), channel_id=1, source_target_pairs={{0,2},{2,0},{4,6},{6,4},{8,10},{10,8},{12,14},{14,12},{16,18},{18,... | collective-permute-start | bytes 663560 | tf_op jit(solution)/shard_map/ppermute | solution.py:1108
  65.5 9.6 %collective-permute-start.7 = (bf16[3,192,768]{2,1,0:T(8,128)(2,1)}, bf16[3,192,768]{2,1,0:T(8,128)(2,1)}, u32[]{:S(2)}, u32[]{:S(2)}) collective-permute-start(bf16[3,192,768]{2,1,0:T(8,128)(2,1)} %collective-permute-done.6.refs_6_), channel_id=1, source_target_pairs={{0,2},{2,0},{4,6},{6,4},{8,10},{10,8},{12,14},{14,12},{16,18},{18,... | collective-permute-start | bytes 2654216 | tf_op jit(solution)/shard_map/ppermute | solution.py:1108
  107.8 23.0 %collective-permute-start.9 = (bf16[2,2,2,3,48,768]{5,4,3,2,1,0:T(8,128)(2,1)}, bf16[2,2,2,3,48,768]{5,4,3,2,1,0:T(8,128)(2,1)}, u32[]{:S(2)}, u32[]{:S(2)}) collective-permute-start(bf16[2,2,2,3,48,768]{5,4,3,2,1,0:T(8,128)(2,1)} %get-tuple-element.128), channel_id=1, source_target_pairs={{0,2},{2,0},{4,6},{6,4},{8,10},{10,8},{12,14},{14,12},{16,18},{18,... | collective-permute-start | bytes 5308424 | tf_op jit(solution)/shard_map/ppermute | solution.py:1108
  108.0 62.0 %collective-permute-start.8 = (bf16[1024,768]{1,0:T(8,128)(2,1)}, bf16[1024,768]{1,0:T(8,128)(2,1)}, u32[]{:S(2)}, u32[]{:S(2)}) collective-permute-start(bf16[1024,768]{1,0:T(8,128)(2,1)} %get-tuple-element.112), channel_id=1, source_target_pairs={{0,1},{1,0},{2,3},{3,2},{4,5},{5,4},{6,7},{7,6},{8,9},{9,8},{10,11... | collective-permute-start | bytes 4718600 | tf_op jit(solution)/shard_map/ppermute | solution.py:1089
  134.3 27.3 %collective-permute-start.10 = (bf16[2,3,48,768]{3,2,1,0:T(8,128)(2,1)}, bf16[2,3,48,768]{3,2,1,0:T(8,128)(2,1)}, u32[]{:S(2)}, u32[]{:S(2)}) collective-permute-start(bf16[2,3,48,768]{3,2,1,0:T(8,128)(2,1)} %get-tuple-element.129.refs_14_), channel_id=1, source_target_pairs={{0,1},{1,0},{2,3},{3,2},{4,5},{5,4},{6,7},{7,6},{8,9},{9,8},{10,11... | collective-permute-start | bytes 1327112 | tf_op jit(solution)/shard_map/ppermute | solution.py:1089
  134.6 27.0 %collective-permute-start.11 = (bf16[2,3,48,768]{3,2,1,0:T(8,128)(2,1)}, bf16[2,3,48,768]{3,2,1,0:T(8,128)(2,1)}, u32[]{:S(2)}, u32[]{:S(2)}) collective-permute-start(bf16[2,3,48,768]{3,2,1,0:T(8,128)(2,1)} %get-tuple-element.130.refs_15_), channel_id=1, source_target_pairs={{0,4},{2,6},{4,0},{6,2},{8,12},{10,14},{12,8},{14,10},{16,20},{18,... | collective-permute-start | bytes 1327112 | tf_op jit(solution)/shard_map/ppermute | solution.py:1108
  136.4 28.8 %collective-permute-start.12 = (bf16[2,3,48,768]{3,2,1,0:T(8,128)(2,1)}, bf16[2,3,48,768]{3,2,1,0:T(8,128)(2,1)}, u32[]{:S(2)}, u32[]{:S(2)}) collective-permute-start(bf16[2,3,48,768]{3,2,1,0:T(8,128)(2,1)} %get-tuple-element.131.refs_16_), channel_id=1, source_target_pairs={{0,5},{1,4},{2,7},{3,6},{4,1},{5,0},{6,3},{7,2},{8,13},{9,12},{10,... | collective-permute-start | bytes 1327112 | tf_op jit(solution)/shard_map/ppermute | solution.py:1094
  161.6 22.2 %collective-permute-start.13 = (bf16[2,2,2,3,48,768]{5,4,3,2,1,0:T(8,128)(2,1)}, bf16[2,2,2,3,48,768]{5,4,3,2,1,0:T(8,128)(2,1)}, u32[]{:S(2)}, u32[]{:S(2)}) collective-permute-start(bf16[2,2,2,3,48,768]{5,4,3,2,1,0:T(8,128)(2,1)} %get-tuple-element.143), channel_id=1, source_target_pairs={{0,2},{2,0},{4,6},{6,4},{8,10},{10,8},{12,14},{14,12},{16,18},{18,... | collective-permute-start | bytes 5308424 | tf_op jit(solution)/shard_map/ppermute | solution.py:1108
  168.4 15.3 %collective-permute-start.14 = (bf16[2,3,48,768]{3,2,1,0:T(8,128)(2,1)}, bf16[2,3,48,768]{3,2,1,0:T(8,128)(2,1)}, u32[]{:S(2)}, u32[]{:S(2)}) collective-permute-start(bf16[2,3,48,768]{3,2,1,0:T(8,128)(2,1)} %sums.4.refs_13_.refs_6_), channel_id=1, source_target_pairs={{0,8},{2,10},{4,12},{6,14},{8,0},{10,2},{12,4},{14,6},{16,24},{18,... | collective-permute-start | bytes 1327112 | tf_op jit(solution)/shard_map/ppermute | solution.py:1108
  183.7 23.5 %collective-permute-start.25 = (bf16[2,304,384]{2,1,0:T(8,128)(2,1)}, bf16[2,304,384]{2,1,0:T(8,128)(2,1)}, u32[]{:S(2)}, u32[]{:S(2)}) collective-permute-start(bf16[2,304,384]{2,1,0:T(8,128)(2,1)} %get-tuple-element.156), channel_id=1, source_target_pairs={{0,2},{2,0},{4,6},{6,4},{8,10},{10,8},{12,14},{14,12},{16,18},{18,... | collective-permute-start | bytes 1400840 | tf_op jit(solution)/shard_map/ppermute | solution.py:1108
  187.7 29.0 %collective-permute-start.31 = (bf16[2,3,48,768]{3,2,1,0:T(8,128)(2,1)}, bf16[2,3,48,768]{3,2,1,0:T(8,128)(2,1)}, u32[]{:S(2)}, u32[]{:S(2)}) collective-permute-start(bf16[2,3,48,768]{3,2,1,0:T(8,128)(2,1)} %get-tuple-element.148.refs_16_), channel_id=1, source_target_pairs={{0,16},{2,18},{4,20},{6,22},{8,24},{10,26},{12,28},{14,30},{16,0},... | collective-permute-start | bytes 1327112 | tf_op jit(solution)/shard_map/ppermute | solution.py:1108
  190.3 19.9 %collective-permute-start.15 = (bf16[2,3,48,768]{3,2,1,0:T(8,128)(2,1)}, bf16[2,3,48,768]{3,2,1,0:T(8,128)(2,1)}, u32[]{:S(2)}, u32[]{:S(2)}) collective-permute-start(bf16[2,3,48,768]{3,2,1,0:T(8,128)(2,1)} %get-tuple-element.145.refs_13_), channel_id=1, source_target_pairs={{0,1},{1,0},{2,3},{3,2},{4,5},{5,4},{6,7},{7,6},{8,9},{9,8},{10,11... | collective-permute-start | bytes 1327112 | tf_op jit(solution)/shard_map/ppermute | solution.py:1089
  191.8 21.8 %collective-permute-start.16 = (bf16[2,3,48,768]{3,2,1,0:T(8,128)(2,1)}, bf16[2,3,48,768]{3,2,1,0:T(8,128)(2,1)}, u32[]{:S(2)}, u32[]{:S(2)}) collective-permute-start(bf16[2,3,48,768]{3,2,1,0:T(8,128)(2,1)} %get-tuple-element.146.refs_14_), channel_id=1, source_target_pairs={{0,4},{2,6},{4,0},{6,2},{8,12},{10,14},{12,8},{14,10},{16,20},{18,... | collective-permute-start | bytes 1327112 | tf_op jit(solution)/shard_map/ppermute | solution.py:1108
  192.3 21.3 %collective-permute-start.17 = (bf16[2,3,48,768]{3,2,1,0:T(8,128)(2,1)}, bf16[2,3,48,768]{3,2,1,0:T(8,128)(2,1)}, u32[]{:S(2)}, u32[]{:S(2)}) collective-permute-start(bf16[2,3,48,768]{3,2,1,0:T(8,128)(2,1)} %get-tuple-element.147.refs_15_), channel_id=1, source_target_pairs={{0,5},{1,4},{2,7},{3,6},{4,1},{5,0},{6,3},{7,2},{8,13},{9,12},{10,... | collective-permute-start | bytes 1327112 | tf_op jit(solution)/shard_map/ppermute | solution.py:1094
  207.2 12.5 %collective-permute-start.24 = (bf16[2,304,384]{2,1,0:T(8,128)(2,1)}, bf16[2,304,384]{2,1,0:T(8,128)(2,1)}, u32[]{:S(2)}, u32[]{:S(2)}) collective-permute-start(bf16[2,304,384]{2,1,0:T(8,128)(2,1)} %get-tuple-element.154), channel_id=1, source_target_pairs={{0,2},{2,0},{4,6},{6,4},{8,10},{10,8},{12,14},{14,12},{16,18},{18,... | collective-permute-start | bytes 1400840 | tf_op jit(solution)/shard_map/ppermute | solution.py:1108
  210.2 21.8 %collective-permute-start.26 = (bf16[304,384]{1,0:T(8,128)(2,1)}, bf16[304,384]{1,0:T(8,128)(2,1)}, u32[]{:S(2)}, u32[]{:S(2)}) collective-permute-start(bf16[304,384]{1,0:T(8,128)(2,1)} %get-tuple-element.169), channel_id=1, source_target_pairs={{0,1},{1,0},{2,3},{3,2},{4,5},{5,4},{6,7},{7,6},{8,9},{9,8},{10,11... | collective-permute-start | bytes 700424 | tf_op jit(solution)/shard_map/ppermute | solution.py:1089
  213.6 19.7 %collective-permute-start.28 = (bf16[304,384]{1,0:T(8,128)(2,1)}, bf16[304,384]{1,0:T(8,128)(2,1)}, u32[]{:S(2)}, u32[]{:S(2)}) collective-permute-start(bf16[304,384]{1,0:T(8,128)(2,1)} %get-tuple-element.170), channel_id=1, source_target_pairs={{0,5},{1,4},{2,7},{3,6},{4,1},{5,0},{6,3},{7,2},{8,13},{9,12},{10,... | collective-permute-start | bytes 700424 | tf_op jit(solution)/shard_map/ppermute | solution.py:1094
  216.3 10.2 %collective-permute-start.20 = (bf16[3,48,768]{2,1,0:T(8,128)(2,1)}, bf16[3,48,768]{2,1,0:T(8,128)(2,1)}, u32[]{:S(2)}, u32[]{:S(2)}) collective-permute-start(bf16[3,48,768]{2,1,0:T(8,128)(2,1)} %get-tuple-element.168.refs_2_), channel_id=1, source_target_pairs={{0,8},{2,10},{4,12},{6,14},{8,0},{10,2},{12,4},{14,6},{16,24},{18,... | collective-permute-start | bytes 663560 | tf_op jit(solution)/shard_map/ppermute | solution.py:1108
  216.8 12.1 %collective-permute-start.22 = (bf16[3,48,768]{2,1,0:T(8,128)(2,1)}, bf16[3,48,768]{2,1,0:T(8,128)(2,1)}, u32[]{:S(2)}, u32[]{:S(2)}) collective-permute-start(bf16[3,48,768]{2,1,0:T(8,128)(2,1)} %get-tuple-element.167.refs_3_), channel_id=1, source_target_pairs={{0,16},{2,18},{4,20},{6,22},{8,24},{10,26},{12,28},{14,30},{16,0},... | collective-permute-start | bytes 663560 | tf_op jit(solution)/shard_map/ppermute | solution.py:1108
  219.7 20.0 %collective-permute-start.32 = (bf16[2,3,48,768]{3,2,1,0:T(8,128)(2,1)}, bf16[2,3,48,768]{3,2,1,0:T(8,128)(2,1)S(1)}, u32[]{:S(2)}, u32[]{:S(2)}) collective-permute-start(bf16[2,3,48,768]{3,2,1,0:T(8,128)(2,1)} %add_convert_fusion.refs_0_), channel_id=1, source_target_pairs={{0,4},{2,6},{4,0},{6,2},{8,12},{10,14},{12,8},{14,10},{16,20},{18,... | collective-permute-start | bytes 1327112 | tf_op jit(solution)/shard_map/ppermute | solution.py:1108
  226.5 48.3 %collective-permute-start.18 = (bf16[1024,384]{1,0:T(8,128)(2,1)}, bf16[1024,384]{1,0:T(8,128)(2,1)}, u32[]{:S(2)}, u32[]{:S(2)}) collective-permute-start(bf16[1024,384]{1,0:T(8,128)(2,1)} %get-tuple-element.151), channel_id=1, source_target_pairs={{0,1},{1,0},{2,3},{3,2},{4,5},{5,4},{6,7},{7,6},{8,9},{9,8},{10,11... | collective-permute-start | bytes 2359304 | tf_op jit(solution)/shard_map/ppermute | solution.py:1089
  232.0 42.8 %collective-permute-start.19 = (bf16[1024,384]{1,0:T(8,128)(2,1)}, bf16[1024,384]{1,0:T(8,128)(2,1)}, u32[]{:S(2)}, u32[]{:S(2)}) collective-permute-start(bf16[1024,384]{1,0:T(8,128)(2,1)} %get-tuple-element.152), channel_id=1, source_target_pairs={{0,1},{1,0},{2,3},{3,2},{4,5},{5,4},{6,7},{7,6},{8,9},{9,8},{10,11... | collective-permute-start | bytes 2359304 | tf_op jit(solution)/shard_map/ppermute | solution.py:1089
  237.9 14.1 %collective-permute-start.23 = (bf16[3,48,768]{2,1,0:T(8,128)(2,1)S(1)}, bf16[3,48,768]{2,1,0:T(8,128)(2,1)S(1)}, u32[]{:S(2)}, u32[]{:S(2)}) collective-permute-start(bf16[3,48,768]{2,1,0:T(8,128)(2,1)S(1)} %add_convert_fusion.7), channel_id=1, source_target_pairs={{0,8},{2,10},{4,12},{6,14},{8,0},{10,2},{12,4},{14,6},{16,24},{18,... | collective-permute-start | bytes 663560 | tf_op jit(solution)/shard_map/ppermute | solution.py:1108
  239.7 12.2 %collective-permute-start.29 = (bf16[304,384]{1,0:T(8,128)(2,1)S(1)}, bf16[304,384]{1,0:T(8,128)(2,1)S(1)}, u32[]{:S(2)}, u32[]{:S(2)}) collective-permute-start(bf16[304,384]{1,0:T(8,128)(2,1)S(1)} %fusion.2), channel_id=1, source_target_pairs={{0,8},{2,10},{4,12},{6,14},{8,0},{10,2},{12,4},{14,6},{16,24},{18,... | collective-permute-start | bytes 700424 | tf_op jit(solution)/shard_map/ppermute | solution.py:1108
  242.3 23.1 %collective-permute-start.33 = (bf16[2,2,3,48,768]{4,3,2,1,0:T(8,128)(2,1)S(1)}, bf16[2,2,3,48,768]{4,3,2,1,0:T(8,128)(2,1)}, u32[]{:S(2)}, u32[]{:S(2)}) collective-permute-start(bf16[2,2,3,48,768]{4,3,2,1,0:T(8,128)(2,1)S(1)} %pad_maximum_fusion), channel_id=1, source_target_pairs={{0,2},{2,0},{4,6},{6,4},{8,10},{10,8},{12,14},{14,12},{16,18},{18,... | collective-permute-start | bytes 2654216 | tf_op jit(solution)/shard_map/ppermute | solution.py:1108
  252.0 12.6 %collective-permute-start.30 = (bf16[304,384]{1,0:T(8,128)(2,1)S(1)}, bf16[304,384]{1,0:T(8,128)(2,1)S(1)}, u32[]{:S(2)}, u32[]{:S(2)}) collective-permute-start(bf16[304,384]{1,0:T(8,128)(2,1)S(1)} %add_convert_fusion.2), channel_id=1, source_target_pairs={{0,16},{2,18},{4,20},{6,22},{8,24},{10,26},{12,28},{14,30},{16,0},... | collective-permute-start | bytes 700424 | tf_op jit(solution)/shard_map/ppermute | solution.py:1108
  270.1 18.2 %collective-permute-start.36 = (bf16[2,3,48,768]{3,2,1,0:T(8,128)(2,1)}, bf16[2,3,48,768]{3,2,1,0:T(8,128)(2,1)S(1)}, u32[]{:S(2)}, u32[]{:S(2)}) collective-permute-start(bf16[2,3,48,768]{3,2,1,0:T(8,128)(2,1)} %get-tuple-element.160.refs_0_), channel_id=1, source_target_pairs={{0,4},{2,6},{4,0},{6,2},{8,12},{10,14},{12,8},{14,10},{16,20},{18,... | collective-permute-start | bytes 1327112 | tf_op jit(solution)/shard_map/ppermute | solution.py:1108
  270.7 16.8 %collective-permute-start.34 = (bf16[304,384]{1,0:T(8,128)(2,1)}, bf16[304,384]{1,0:T(8,128)(2,1)S(1)}, u32[]{:S(2)}, u32[]{:S(2)}) collective-permute-start(bf16[304,384]{1,0:T(8,128)(2,1)} %get-tuple-element.158.refs_0_), channel_id=1, source_target_pairs={{0,4},{2,6},{4,0},{6,2},{8,12},{10,14},{12,8},{14,10},{16,20},{18,... | collective-permute-start | bytes 700424 | tf_op jit(solution)/shard_map/ppermute | solution.py:1108
  (14 other events, 121.3 us)
